TPU v7x, 128 devices: a whole 4x4x4 slice. The times are simulated.
128 devices in a mesh: ctx: 64 (over z, x, y_lo, core), ch: 2 (over y_hi).
Axes of the slice: x: 4, y: 4 (y_hi: 2, y_lo: 2; y = y_hi * 2 + y_lo), z: 4, core: 2. Of those that a mesh axis runs over, the one named last changes fastest.
Arguments:
- rollout_rows: bfloat16 [384, 128, 3, 2048], P('ctx', None, None, 'ch'), may hold values from -6 to 6
- pack_targets: int32 [384, 2], replicated, may hold values from -1 to 63, as said below
- doc_lengths: int32 [128], replicated, may hold values from 1 to 2049, 32768 in all
- filter_taps: float32 [4, 2049], replicated, may hold values from -3 to 3
- skip_gain: float32 [2048], P('ch'), may hold values from 0.1 to 1.9
- out_grad: bfloat16 [32768, 2048], P('ctx', 'ch'), may hold values from -6 to 6
Outputs:
- out_y: bfloat16 [32768, 2048], P('ctx', 'ch')
- grad_streams: bfloat16 [32768, 3, 2048], P('ctx', None, 'ch')
- grad_taps: float32 [4, 2049], replicated
- grad_skip: float32 [2048], P('ch')
Inputs may be any that keep to these rules, and one draw needn't show every extreme that they name: `pack_targets`: owner of slot g is g // 6. Every pair (shard, offset) with offset below 4 is named by exactly one slot; a named shard is the owner itself or one of its two neighbours on the closed cycle of context shards (shard 0 and the last are neighbours). One owner gives at most 1 row to one neighbouring shard, and in every draw some owner gives exactly 1 row to the shard below it and some owner, possibly another, gives exactly 1 row to the shard above it. Unused slots hold (-1, -1). `doc_lengths`: the documents fill all 32768 positions; the longest has exactly 2049 tokens.
All inputs are finite; a program needn't handle non-finite values.
Results may differ from a plain program's by a relative error of at most 0.01.
Values may be sent and summed in bfloat16 or wider, within the bound.
No kernel may reach another device: no remote copies, remote signals or barrier semaphores. Data moves between devices by JAX's collectives and lax.ppermute only.
A program may use at most 128 MiB of HBM per device.

v0:
```python
import math

import jax
import jax.numpy as jnp
from jax import lax
from jax.sharding import PartitionSpec as P


def shifted(array, axis, by):
    length = lax.axis_size(axis)
    return lax.ppermute(array, axis, [(i, (i + by) % length) for i in range(length)])


def padded_2(block, sides, width):
    for axis, dim in sides:
        count = lax.axis_size(axis)
        forward = [(i, i + 1) for i in range(count - 1)]
        backward = [(target, source) for source, target in forward]
        low = lax.ppermute(
            lax.slice_in_dim(block, block.shape[dim] - width, None, axis=dim), axis, forward
        )
        high = lax.ppermute(lax.slice_in_dim(block, 0, width, axis=dim), axis, backward)
        block = jnp.concatenate([low, block, high], axis=dim)
    return block


def skew_right(matrix_rows):
    leading = matrix_rows.shape[:-2]
    height, breadth = (matrix_rows.shape[-2], matrix_rows.shape[-1])
    extra = [(0, 0)] * len(leading)
    padded = jnp.pad(matrix_rows, extra + [(0, 0), (0, height)])
    flatten = padded.reshape(leading + (height * (breadth + height),))
    flatten = flatten[..., : height * (breadth + height - 1)]
    return flatten.reshape(leading + (height, breadth + height - 1))


def band_from(tap_rows, height):
    filters = tap_rows.shape[0]
    repeated = jnp.broadcast_to(
        tap_rows.astype(jnp.bfloat16)[:, None, :], (filters, height, tap_rows.shape[1])
    )
    return skew_right(repeated)


def lag_totals(products, span):
    height, breadth = (products.shape[-2], products.shape[-1])
    flatten = products.reshape(height * breadth)
    flatten = jnp.pad(flatten, [(0, height)])
    sheared = flatten.reshape(height, breadth + 1)
    totals = jnp.sum(sheared, axis=0)
    return totals[: span + 1][::-1]


def doc_start_of(positions, starts):
    inside = starts[None, :] <= positions[:, None]
    doc_begin = jnp.max(jnp.where(inside, starts[None, :], 0), axis=1)
    return doc_begin


def place_rows(shards, offsets, target, rows_dev):
    wanted = shards == target
    offset_ids = jnp.arange(rows_dev, dtype=jnp.int32)
    matches = wanted[None, :] & (offsets[None, :] == offset_ids[:, None])
    slot_ids = jnp.arange(shards.shape[0], dtype=jnp.int32)
    slot_index = jnp.sum(jnp.where(matches, slot_ids[None, :], 0), axis=1)
    return (slot_index, jnp.any(matches, axis=1))


def gather_pick(buffer, slot_index, present):
    picked = jnp.take(buffer, slot_index, axis=0)
    return jnp.where(present[:, None, None, None], picked, jnp.zeros((), buffer.dtype))


def on_device(rollout_rows, pack_targets, doc_lengths, filter_taps, skip_gain, out_grad):
    cycle = lax.axis_size("ctx")
    index = lax.axis_index("ctx")
    own_cap, row_len, streams, channels = rollout_rows.shape
    tokens = out_grad.shape[0]
    rows_dev = tokens // row_len
    half = tokens // 2
    filters = filter_taps.shape[0]
    span = filter_taps.shape[1] - 1
    hops = span // half
    group = channels // filters
    shard_of = pack_targets[:, 0].reshape(cycle, own_cap)
    offset_of = pack_targets[:, 1].reshape(cycle, own_cap)
    below = (index + cycle - 1) % cycle
    above = (index + 1) % cycle

    def owner_lists(owner):
        return (
            lax.dynamic_index_in_dim(shard_of, owner, 0, keepdims=False),
            lax.dynamic_index_in_dim(offset_of, owner, 0, keepdims=False),
        )

    own_shards, own_offsets = owner_lists(index)
    low_shards, low_offsets = owner_lists(below)
    high_shards, high_offsets = owner_lists(above)
    slot_index, present = place_rows(own_shards, own_offsets, index, rows_dev)
    packed = gather_pick(rollout_rows, slot_index, present)
    from_below = shifted(rollout_rows, "ctx", 1)
    from_above = shifted(rollout_rows, "ctx", -1)
    low_slot, low_present = place_rows(low_shards, low_offsets, index, rows_dev)
    high_slot, high_present = place_rows(high_shards, high_offsets, index, rows_dev)
    packed = (
        packed
        + gather_pick(from_below, low_slot, low_present)
        + gather_pick(from_above, high_slot, high_present)
    )
    packed = packed.reshape(tokens, streams, channels)
    query = packed[:, 0]
    key_in = packed[:, 1]
    value_in = packed[:, 2]
    product = (key_in.astype(jnp.float32) * value_in.astype(jnp.float32)).astype(jnp.bfloat16)
    halves_x = product.reshape(2, half, channels).astype(jnp.float32)
    halves_q = query.reshape(2, half, channels).astype(jnp.float32)
    grad_out = out_grad.reshape(2, half, channels).astype(jnp.float32)
    grad_mid = (grad_out * halves_q).astype(jnp.bfloat16)
    first_x = product[:half]
    second_x = product[half:]
    top = index == cycle - 1

    def advance(lower_part, rimmed, axis):
        new_lower = lax.slice_in_dim(rimmed, 0, half, axis=axis)
        from_upper = lax.slice_in_dim(rimmed, 3 * half, 4 * half, axis=axis)
        return (jnp.where(top, lower_part, from_upper), new_lower)

    x_upper, x_lower, g_upper, g_lower = ([], [], [], [])
    upper_part, lower_part = (second_x, first_x)
    for step in range(hops):
        rimmed = padded_2(jnp.concatenate([upper_part, lower_part], axis=0), (("ctx", 0),), half)
        upper_part, lower_part = advance(lower_part, rimmed, 0)
        x_upper.append(upper_part)
        x_lower.append(lower_part)
    upper_part, lower_part = (grad_mid[0], grad_mid[1])
    for step in range(hops):
        rimmed = padded_2(jnp.concatenate([upper_part, lower_part], axis=0), (("ctx", 0),), half)
        upper_part, lower_part = advance(lower_part, rimmed, 0)
        g_upper.append(upper_part)
        g_lower.append(lower_part)
    fwd_windows = [
        jnp.concatenate(x_lower[::-1] + [first_x], axis=0),
        jnp.concatenate(x_upper[::-1] + [second_x], axis=0),
    ]
    bwd_windows = [
        jnp.concatenate([grad_mid[0]] + g_upper, axis=0),
        jnp.concatenate([grad_mid[1]] + g_lower, axis=0),
    ]
    starts = jnp.cumsum(doc_lengths, dtype=jnp.int32) - doc_lengths
    block_base = jnp.stack([index * half, (2 * cycle - 1 - index) * half])
    own_pos = block_base[:, None] + jnp.arange(half, dtype=jnp.int32)[None, :]
    fwd_pos = block_base[:, None] - span + jnp.arange(span + half, dtype=jnp.int32)[None, :]
    bwd_pos = block_base[:, None] + jnp.arange(half + span, dtype=jnp.int32)[None, :]
    fwd_band = band_from(filter_taps[:, ::-1], half)
    bwd_band = band_from(filter_taps, half)

    def split_groups(rows):
        return rows.reshape(rows.shape[0], filters, group).transpose(1, 0, 2)

    conv_parts, back_parts, tap_parts = ([], [], [])
    for which in range(2):
        keep_fwd = fwd_pos[which][None, :] >= doc_start_of(own_pos[which], starts)[:, None]
        keep_bwd = own_pos[which][:, None] >= doc_start_of(bwd_pos[which], starts)[None, :]

        def per_filter(items, keep_fwd=keep_fwd, keep_bwd=keep_bwd):
            fwd_rows, bwd_rows, sources, ahead, own_grad = items
            fwd_mat = jnp.where(keep_fwd, fwd_rows, jnp.zeros((), jnp.bfloat16))
            bwd_mat = jnp.where(keep_bwd, bwd_rows, jnp.zeros((), jnp.bfloat16))
            conv_part = jnp.dot(fwd_mat, sources, preferred_element_type=jnp.float32)
            back_part = jnp.dot(bwd_mat, ahead, preferred_element_type=jnp.float32)
            pairs = lax.dot_general(
                own_grad, sources, (((1,), (1,)), ((), ())), preferred_element_type=jnp.float32
            )
            pairs = jnp.where(keep_fwd, pairs, jnp.zeros((), jnp.float32))
            return (conv_part, back_part, lag_totals(pairs, span))

        conv_f, back_f, tap_f = lax.map(
            per_filter,
            (
                fwd_band,
                bwd_band,
                split_groups(fwd_windows[which]),
                split_groups(bwd_windows[which]),
                split_groups(grad_mid[which]),
            ),
        )
        conv_parts.append(conv_f.transpose(1, 0, 2).reshape(half, channels))
        back_parts.append(back_f.transpose(1, 0, 2).reshape(half, channels))
        tap_parts.append(tap_f)
    conv_out = jnp.stack(conv_parts)
    grad_conv = jnp.stack(back_parts)
    mixed = conv_out + skip_gain[None, None, :] * halves_x
    out_y = (halves_q * mixed).astype(jnp.bfloat16).reshape(tokens, channels)
    grad_query = (grad_out * mixed).astype(jnp.bfloat16)
    grad_x = grad_conv + skip_gain[None, None, :] * grad_mid.astype(jnp.float32)
    halves_k = key_in.reshape(2, half, channels).astype(jnp.float32)
    halves_v = value_in.reshape(2, half, channels).astype(jnp.float32)
    grad_key = (grad_x * halves_v).astype(jnp.bfloat16)
    grad_value = (grad_x * halves_k).astype(jnp.bfloat16)
    grad_streams = jnp.stack([grad_query, grad_key, grad_value], axis=2).reshape(
        tokens, 3, channels
    )
    tap_local = tap_parts[0] + tap_parts[1]
    skip_local = jnp.sum(grad_mid.astype(jnp.float32) * halves_x, axis=(0, 1))
    tap_total = lax.psum(tap_local, ("ctx", "ch"))
    skip_total = lax.psum(skip_local, "ctx")
    seq_total = tokens * cycle
    chan_total = channels * lax.axis_size("ch")
    grad_taps = tap_total / math.sqrt(seq_total * chan_total / filters)
    grad_skip = skip_total / math.sqrt(seq_total)
    return (out_y, grad_streams, grad_taps, grad_skip)


def solution(mesh):
    return jax.shard_map(
        on_device,
        mesh=mesh,
        in_specs=(P("ctx", None, None, "ch"), P(), P(), P(), P("ch"), P("ctx", "ch")),
        out_specs=(P("ctx", "ch"), P("ctx", None, "ch"), P(), P("ch")),
        check_vma=False,
    )
```

profile of v0, /device:TPU:1, one launch (start us, length us, event | category | flops | bytes accessed | tf_op | source)
XLA Modules:
  0.0 743.8 jit_solution(11004851079440982973)
XLA Ops:
  10.8 13.1 %reshape.301 = bf16[2360320]{0:T(1024)(128)(2,1)} reshape(bf16[4,256,2305]{2,1,0:T(8,128)(2,1)} %pad.21) | data formatting | bytes 9441280
  23.9 6.3 reshape.244
  35.1 13.1 %reshape.299 = bf16[2360320]{0:T(1024)(128)(2,1)} reshape(bf16[4,256,2305]{2,1,0:T(8,128)(2,1)} %pad.20) | data formatting | bytes 9441280
  48.2 6.2 reshape.241
  54.4 6.9 slice.105
  61.8 49.9 %collective-permute-done.1 = bf16[6,128,3,1024]{3,1,2,0:T(8,128)(2,1)} collective-permute-done((bf16[6,128,3,1024]{3,1,2,0:T(8,128)(2,1)}, bf16[6,128,3,1024]{3,1,2,0:T(8,128)(2,1)}, u32[]{:S(2)}, u32[]{:S(2)}) %collective-permute-start.1) | collective-permute-done | bytes 4718624 | tf_op jit(solution)/shard_map/ppermute | solution.py:11
  111.7 4.7 gather_fusion.2
  116.4 4.7 gather_fusion.1
  130.8 7.2 copy_bitcast_fusion
  142.4 5.7 collective-permute-done.3
  159.2 4.5 collective-permute-start.5
  191.7 142.3 %psum.15 = f32[1024]{0:T(1024)S(1)} all-reduce(f32[1024]{0:T(1024)S(1)} %get-tuple-element.417), channel_id=1, replica_groups=mesh['ctx'=64,'ch'=2] {'ctx'}, use_global_device_ids=true, to_apply=%region_19.21 | all-reduce | flops 1024 | bytes 8192 | tf_op jit(solution)/shard_map/psum | solution.py:206
  339.3 6.3 collective-permute-start.12
  355.1 8.8 %collective-permute-done.12 = bf16[256,1024]{1,0:T(8,128)(2,1)S(1)} collective-permute-done((bf16[256,1024]{1,0:T(8,128)(2,1)S(1)}, bf16[256,1024]{1,0:T(8,128)(2,1)S(1)}, u32[]{:S(2)}, u32[]{:S(2)}) %collective-permute-start.12) | collective-permute-done | bytes 524320 | tf_op jit(solution)/shard_map/ppermute | solution.py:22
  391.7 8.4 %collective-permute-done.16 = bf16[256,1024]{1,0:T(8,128)(2,1)S(1)} collective-permute-done((bf16[256,1024]{1,0:T(8,128)(2,1)S(1)}, bf16[256,1024]{1,0:T(8,128)(2,1)S(1)}, u32[]{:S(2)}, u32[]{:S(2)}) %collective-permute-start.16) | collective-permute-done | bytes 524320 | tf_op jit(solution)/shard_map/ppermute | solution.py:22
  402.1 4.5 collective-permute-done.17
  407.4 4.4 collective-permute-start.19
  418.9 6.6 collective-permute-done.19
  435.6 8.8 %collective-permute-done.21 = bf16[256,1024]{1,0:T(8,128)(2,1)S(1)} collective-permute-done((bf16[256,1024]{1,0:T(8,128)(2,1)S(1)}, bf16[256,1024]{1,0:T(8,128)(2,1)S(1)}, u32[]{:S(2)}, u32[]{:S(2)}) %collective-permute-start.21) | collective-permute-done | bytes 524320 | tf_op jit(solution)/shard_map/ppermute | solution.py:19
  445.2 4.4 collective-permute-start.23
  458.2 7.6 %collective-permute-done.30 = bf16[256,1024]{1,0:T(8,128)(2,1)S(1)} collective-permute-done((bf16[256,1024]{1,0:T(8,128)(2,1)S(1)}, bf16[256,1024]{1,0:T(8,128)(2,1)S(1)}, u32[]{:S(2)}, u32[]{:S(2)}) %collective-permute-start.30) | collective-permute-done | bytes 524320 | tf_op jit(solution)/shard_map/ppermute | solution.py:22
  482.8 74.5 %while.34 = (s32[]{:T(128)}, f32[4,256,256]{1,2,0:T(8,128)}, f32[4,256,256]{1,2,0:T(8,128)}, f32[4,2049]{1,0:T(4,128)}, bf16[4,256,2304]{2,1,0:T(8,128)(2,1)}, /...) while((s32[]{:T(128)}, f32[4,256,256]{1,2,0:T(8,128)}, ...), condition=%wide.region_11.13_spmd.clone, body=%wide.region_9.12_spmd.clone.sunk | while | flops 910096384 | bytes 25552068 | solution.py:177
  567.5 71.2 %while.35 = (s32[]{:T(128)}, f32[4,256,256]{1,2,0:T(8,128)S(1)}, f32[4,256,256]{1,2,0:T(8,128)}, f32[4,2049]{1,0:T(4,128)}, bf16[4,256,2304]{2,1,0:T(8,128)(2,1)...) while((s32[]{:T(128)}, f32[4,256,256]{1,2,0:T(8,128)S(1)}, ...), condition=%wide.region_16.18_spmd.clone, body=%wide.region_14.17_spmd.clone.sunk | while | flops 910096384 | bytes 25552068 | solution.py:177
  652.0 81.8 %psum.14 = f32[4,2049]{1,0:T(4,128)S(1)} all-reduce(f32[4,2049]{1,0:T(4,128)S(1)} %add.143), channel_id=1, replica_groups=mesh['ctx'=64,'ch'=2] {'ctx','ch'}, use_global_device_ids=true, to_apply=%region_17.19 | all-reduce | flops 8196 | bytes 65568 | tf_op jit(solution)/shard_map/psum | solution.py:205
  (327 shorter events, 335.3 us)
Async XLA Ops:
  0.6 111.1 %collective-permute-start.1 = (bf16[6,128,3,1024]{3,1,2,0:T(8,128)(2,1)}, bf16[6,128,3,1024]{3,1,2,0:T(8,128)(2,1)}, u32[]{:S(2)}, u32[]{:S(2)}) collective-permute-start(bf16[6,128,3,1024]{3,1,2,0:T(8,128)(2,1)} %param.12), channel_id=1, source_target_pairs={{0,126},{2,0},{4,2},{6,4},{8,6},{10,8},{12,10},{14,12},{16,14},{18... | collective-permute-start | bytes 14155784 | tf_op jit(solution)/shard_map/ppermute | solution.py:11
  2.1 114.3 %collective-permute-start = (bf16[6,128,3,1024]{3,1,2,0:T(8,128)(2,1)}, bf16[6,128,3,1024]{3,1,2,0:T(8,128)(2,1)}, u32[]{:S(2)}, u32[]{:S(2)}) collective-permute-start(bf16[6,128,3,1024]{3,1,2,0:T(8,128)(2,1)} %param.12), channel_id=1, source_target_pairs={{0,2},{2,4},{4,6},{6,8},{8,10},{10,12},{12,14},{14,16},{16,18},{18... | collective-permute-start | bytes 14155784 | tf_op jit(solution)/shard_map/ppermute | solution.py:11
  166.4 208.7 %collective-permute-start.25 = (bf16[256,1024]{1,0:T(8,128)(2,1)}, bf16[256,1024]{1,0:T(8,128)(2,1)}, u32[]{:S(2)}, u32[]{:S(2)}) collective-permute-start(bf16[256,1024]{1,0:T(8,128)(2,1)} %get-tuple-element.430), channel_id=1, source_target_pairs={{2,0},{4,2},{6,4},{8,6},{10,8},{12,10},{14,12},{16,14},{18,16},{20... | collective-permute-start | bytes 1572872 | tf_op jit(solution)/shard_map/ppermute | solution.py:22
  177.8 168.3 %collective-permute-start.11 = (bf16[256,1024]{1,0:T(8,128)(2,1)}, bf16[256,1024]{1,0:T(8,128)(2,1)}, u32[]{:S(2)}, u32[]{:S(2)}) collective-permute-start(bf16[256,1024]{1,0:T(8,128)(2,1)} %get-tuple-element.425), channel_id=1, source_target_pairs={{0,2},{2,4},{4,6},{6,8},{8,10},{10,12},{12,14},{14,16},{16,18},{18... | collective-permute-start | bytes 1572872 | tf_op jit(solution)/shard_map/ppermute | solution.py:19
  181.5 156.7 %collective-permute-start.10 = (bf16[256,1024]{1,0:T(8,128)(2,1)}, bf16[256,1024]{1,0:T(8,128)(2,1)}, u32[]{:S(2)}, u32[]{:S(2)}) collective-permute-start(bf16[256,1024]{1,0:T(8,128)(2,1)} %get-tuple-element.424), channel_id=1, source_target_pairs={{2,0},{4,2},{6,4},{8,6},{10,8},{12,10},{14,12},{16,14},{18,16},{20... | collective-permute-start | bytes 1572872 | tf_op jit(solution)/shard_map/ppermute | solution.py:22
  185.3 148.7 %collective-permute-start.7 = (bf16[256,1024]{1,0:T(8,128)(2,1)S(1)}, bf16[256,1024]{1,0:T(8,128)(2,1)S(1)}, u32[]{:S(2)}, u32[]{:S(2)}) collective-permute-start(bf16[256,1024]{1,0:T(8,128)(2,1)S(1)} %collective-permute-done.6), channel_id=1, source_target_pairs={{0,2},{2,4},{4,6},{6,8},{8,10},{10,12},{12,14},{14,16},{16,18},{18... | collective-permute-start | bytes 1572872 | tf_op jit(solution)/shard_map/ppermute | solution.py:19
  334.0 16.0 %collective-permute-start.8 = (bf16[256,1024]{1,0:T(8,128)(2,1)S(1)}, bf16[256,1024]{1,0:T(8,128)(2,1)S(1)}, u32[]{:S(2)}, u32[]{:S(2)}) collective-permute-start(bf16[256,1024]{1,0:T(8,128)(2,1)S(1)} %collective-permute-done.7), channel_id=1, source_target_pairs={{0,2},{2,4},{4,6},{6,8},{8,10},{10,12},{12,14},{14,16},{16,18},{18... | collective-permute-start | bytes 1572872 | tf_op jit(solution)/shard_map/ppermute | solution.py:19
  339.3 24.6 %collective-permute-start.12 = (bf16[256,1024]{1,0:T(8,128)(2,1)S(1)}, bf16[256,1024]{1,0:T(8,128)(2,1)S(1)}, u32[]{:S(2)}, u32[]{:S(2)}) collective-permute-start(bf16[256,1024]{1,0:T(8,128)(2,1)S(1)} %broadcast_select_fusion.14), channel_id=1, source_target_pairs={{2,0},{4,2},{6,4},{8,6},{10,8},{12,10},{14,12},{16,14},{18,16},{20... | collective-permute-start | bytes 1572872 | tf_op jit(solution)/shard_map/ppermute | solution.py:22
  346.2 19.7 %collective-permute-start.13 = (bf16[256,1024]{1,0:T(8,128)(2,1)}, bf16[256,1024]{1,0:T(8,128)(2,1)S(1)}, u32[]{:S(2)}, u32[]{:S(2)}) collective-permute-start(bf16[256,1024]{1,0:T(8,128)(2,1)} %collective-permute-done.11), channel_id=1, source_target_pairs={{0,2},{2,4},{4,6},{6,8},{8,10},{10,12},{12,14},{14,16},{16,18},{18... | collective-permute-start | bytes 1572872 | tf_op jit(solution)/shard_map/ppermute | solution.py:19
  350.0 20.5 %collective-permute-start.9 = (bf16[256,1024]{1,0:T(8,128)(2,1)S(1)}, bf16[256,1024]{1,0:T(8,128)(2,1)S(1)}, u32[]{:S(2)}, u32[]{:S(2)}) collective-permute-start(bf16[256,1024]{1,0:T(8,128)(2,1)S(1)} %collective-permute-done.8), channel_id=1, source_target_pairs={{0,2},{2,4},{4,6},{6,8},{8,10},{10,12},{12,14},{14,16},{16,18},{18... | collective-permute-start | bytes 1572872 | tf_op jit(solution)/shard_map/ppermute | solution.py:19
  379.2 20.9 %collective-permute-start.16 = (bf16[256,1024]{1,0:T(8,128)(2,1)S(1)}, bf16[256,1024]{1,0:T(8,128)(2,1)S(1)}, u32[]{:S(2)}, u32[]{:S(2)}) collective-permute-start(bf16[256,1024]{1,0:T(8,128)(2,1)S(1)} %broadcast_select_fusion.12), channel_id=1, source_target_pairs={{2,0},{4,2},{6,4},{8,6},{10,8},{12,10},{14,12},{16,14},{18,16},{20... | collective-permute-start | bytes 1572872 | tf_op jit(solution)/shard_map/ppermute | solution.py:22
  382.0 24.6 %collective-permute-start.17 = (bf16[256,1024]{1,0:T(8,128)(2,1)S(1)}, bf16[256,1024]{1,0:T(8,128)(2,1)S(1)}, u32[]{:S(2)}, u32[]{:S(2)}) collective-permute-start(bf16[256,1024]{1,0:T(8,128)(2,1)S(1)} %collective-permute-done.15), channel_id=1, source_target_pairs={{0,2},{2,4},{4,6},{6,8},{8,10},{10,12},{12,14},{14,16},{16,18},{18... | collective-permute-start | bytes 1572872 | tf_op jit(solution)/shard_map/ppermute | solution.py:19
  388.9 22.9 %collective-permute-start.27 = (bf16[256,1024]{1,0:T(8,128)(2,1)S(1)}, bf16[256,1024]{1,0:T(8,128)(2,1)S(1)}, u32[]{:S(2)}, u32[]{:S(2)}) collective-permute-start(bf16[256,1024]{1,0:T(8,128)(2,1)S(1)} %broadcast_select_fusion.5), channel_id=1, source_target_pairs={{2,0},{4,2},{6,4},{8,6},{10,8},{12,10},{14,12},{16,14},{18,16},{20... | collective-permute-start | bytes 1572872 | tf_op jit(solution)/shard_map/ppermute | solution.py:22
  400.1 16.8 %collective-permute-start.18 = (bf16[256,1024]{1,0:T(8,128)(2,1)S(1)}, bf16[256,1024]{1,0:T(8,128)(2,1)S(1)}, u32[]{:S(2)}, u32[]{:S(2)}) collective-permute-start(bf16[256,1024]{1,0:T(8,128)(2,1)S(1)} %broadcast_select_fusion.11), channel_id=1, source_target_pairs={{2,0},{4,2},{6,4},{8,6},{10,8},{12,10},{14,12},{16,14},{18,16},{20... | collective-permute-start | bytes 1572872 | tf_op jit(solution)/shard_map/ppermute | solution.py:22
  407.4 18.2 %collective-permute-start.19 = (bf16[256,1024]{1,0:T(8,128)(2,1)S(1)}, bf16[256,1024]{1,0:T(8,128)(2,1)S(1)}, u32[]{:S(2)}, u32[]{:S(2)}) collective-permute-start(bf16[256,1024]{1,0:T(8,128)(2,1)S(1)} %collective-permute-done.17), channel_id=1, source_target_pairs={{0,2},{2,4},{4,6},{6,8},{8,10},{10,12},{12,14},{14,16},{16,18},{18... | collective-permute-start | bytes 1572872 | tf_op jit(solution)/shard_map/ppermute | solution.py:19
  411.9 18.9 %collective-permute-start.28 = (bf16[256,1024]{1,0:T(8,128)(2,1)S(1)}, bf16[256,1024]{1,0:T(8,128)(2,1)S(1)}, u32[]{:S(2)}, u32[]{:S(2)}) collective-permute-start(bf16[256,1024]{1,0:T(8,128)(2,1)S(1)} %broadcast_select_fusion.4), channel_id=1, source_target_pairs={{2,0},{4,2},{6,4},{8,6},{10,8},{12,10},{14,12},{16,14},{18,16},{20... | collective-permute-start | bytes 1572872 | tf_op jit(solution)/shard_map/ppermute | solution.py:22
  417.0 16.7 %collective-permute-start.20 = (bf16[256,1024]{1,0:T(8,128)(2,1)S(1)}, bf16[256,1024]{1,0:T(8,128)(2,1)S(1)}, u32[]{:S(2)}, u32[]{:S(2)}) collective-permute-start(bf16[256,1024]{1,0:T(8,128)(2,1)S(1)} %broadcast_select_fusion.10), channel_id=1, source_target_pairs={{2,0},{4,2},{6,4},{8,6},{10,8},{12,10},{14,12},{16,14},{18,16},{20... | collective-permute-start | bytes 1572872 | tf_op jit(solution)/shard_map/ppermute | solution.py:22
  426.4 18.0 %collective-permute-start.21 = (bf16[256,1024]{1,0:T(8,128)(2,1)S(1)}, bf16[256,1024]{1,0:T(8,128)(2,1)S(1)}, u32[]{:S(2)}, u32[]{:S(2)}) collective-permute-start(bf16[256,1024]{1,0:T(8,128)(2,1)S(1)} %collective-permute-done.19), channel_id=1, source_target_pairs={{0,2},{2,4},{4,6},{6,8},{8,10},{10,12},{12,14},{14,16},{16,18},{18... | collective-permute-start | bytes 1572872 | tf_op jit(solution)/shard_map/ppermute | solution.py:19
  430.9 18.7 %collective-permute-start.29 = (bf16[256,1024]{1,0:T(8,128)(2,1)S(1)}, bf16[256,1024]{1,0:T(8,128)(2,1)S(1)}, u32[]{:S(2)}, u32[]{:S(2)}) collective-permute-start(bf16[256,1024]{1,0:T(8,128)(2,1)S(1)} %broadcast_select_fusion.3), channel_id=1, source_target_pairs={{2,0},{4,2},{6,4},{8,6},{10,8},{12,10},{14,12},{16,14},{18,16},{20... | collective-permute-start | bytes 1572872 | tf_op jit(solution)/shard_map/ppermute | solution.py:22
  433.7 18.8 %collective-permute-start.22 = (bf16[256,1024]{1,0:T(8,128)(2,1)S(1)}, bf16[256,1024]{1,0:T(8,128)(2,1)S(1)}, u32[]{:S(2)}, u32[]{:S(2)}) collective-permute-start(bf16[256,1024]{1,0:T(8,128)(2,1)S(1)} %broadcast_select_fusion.9), channel_id=1, source_target_pairs={{2,0},{4,2},{6,4},{8,6},{10,8},{12,10},{14,12},{16,14},{18,16},{20... | collective-permute-start | bytes 1572872 | tf_op jit(solution)/shard_map/ppermute | solution.py:22
  449.7 16.1 %collective-permute-start.30 = (bf16[256,1024]{1,0:T(8,128)(2,1)S(1)}, bf16[256,1024]{1,0:T(8,128)(2,1)S(1)}, u32[]{:S(2)}, u32[]{:S(2)}) collective-permute-start(bf16[256,1024]{1,0:T(8,128)(2,1)S(1)} %broadcast_select_fusion.2), channel_id=1, source_target_pairs={{2,0},{4,2},{6,4},{8,6},{10,8},{12,10},{14,12},{16,14},{18,16},{20... | collective-permute-start | bytes 1572872 | tf_op jit(solution)/shard_map/ppermute | solution.py:22
  452.5 22.3 %collective-permute-start.24 = (bf16[256,1024]{1,0:T(8,128)(2,1)S(1)}, bf16[256,1024]{1,0:T(8,128)(2,1)S(1)}, u32[]{:S(2)}, u32[]{:S(2)}) collective-permute-start(bf16[256,1024]{1,0:T(8,128)(2,1)S(1)} %broadcast_select_fusion.8), channel_id=1, source_target_pairs={{2,0},{4,2},{6,4},{8,6},{10,8},{12,10},{14,12},{16,14},{18,16},{20... | collective-permute-start | bytes 1572872 | tf_op jit(solution)/shard_map/ppermute | solution.py:22
  468.7 88.7 %collective-permute-start.33 = (bf16[256,1024]{1,0:T(8,128)(2,1)}, bf16[256,1024]{1,0:T(8,128)(2,1)}, u32[]{:S(2)}, u32[]{:S(2)}) collective-permute-start(bf16[256,1024]{1,0:T(8,128)(2,1)} %collective-permute-done.23), channel_id=1, source_target_pairs={{0,2},{2,4},{4,6},{6,8},{8,10},{10,12},{12,14},{14,16},{16,18},{18... | collective-permute-start | bytes 1572872 | tf_op jit(solution)/shard_map/ppermute | solution.py:19
  477.9 81.5 %collective-permute-start.32 = (bf16[256,1024]{1,0:T(8,128)(2,1)}, bf16[256,1024]{1,0:T(8,128)(2,1)}, u32[]{:S(2)}, u32[]{:S(2)}) collective-permute-start(bf16[256,1024]{1,0:T(8,128)(2,1)} %broadcast_select_fusion), channel_id=1, source_target_pairs={{2,0},{4,2},{6,4},{8,6},{10,8},{12,10},{14,12},{16,14},{18,16},{20... | collective-permute-start | bytes 1572872 | tf_op jit(solution)/shard_map/ppermute | solution.py:22
  (43 other events, 847.0 us)
where the time goes:
time: 756 us; the launch traced here: 744 us
  blocking collectives  224 us (30%)
  local copies, waits for them, and re-layouts  196 us (26%)
  waiting for transfers between devices  116 us (15%)
  starting transfers between devices  98.3 us (13%)
  matrix products  72.4 us (10%)
  other arithmetic  34.8 us (5%)
    psum x1, blocking collectives, on_device(): skip_total = lax.psum(skip_local, 'ctx')  142 us
    psum x1, blocking collectives, on_device(): tap_total = lax.psum(tap_local, ('ctx', 'ch'))  81.8 us
    ppermute x16, starting transfers between devices, padded_2(): lax.ppermute(lax.slice_in_dim(block, block.shape[dim] - width, None, axis...  60.2 us
    unnamed x97, local copies, waits for them, and re-layouts  51.3 us
    ppermute x2, waiting for transfers between devices, shifted(): lax.ppermute(array, axis, [(i, (i + by) % length) for i in range(length)])  49.9 us
    ppermute x16, starting transfers between devices, padded_2(): lax.ppermute(lax.slice_in_dim(block, 0, width, axis=dim), axis, backward)  35.3 us
    ppermute x16, waiting for transfers between devices, padded_2(): lax.ppermute(lax.slice_in_dim(block, block.shape[dim] - width, None, axis...  34.8 us
    ppermute x16, waiting for transfers between devices, padded_2(): lax.ppermute(lax.slice_in_dim(block, 0, width, axis=dim), axis, backward)  31.7 us
  transfers between devices with their start and end apart: 34, of which 15 were waited for; matrix products, arithmetic and copies ran while one was open for 25% of the time, Pallas kernels for 0%

commit v1 on v0

v1 whole, which is shorter than its diff:
```python
import functools
import math

import jax
import jax.numpy as jnp
from jax import lax
from jax.experimental import pallas as pl
from jax.experimental.pallas import tpu as pltpu
from jax.sharding import PartitionSpec as P

BF16 = jnp.bfloat16
F32 = jnp.float32
SMEM = pltpu.SMEM
VMEM = pltpu.VMEM

BLK = 256
HOPS = 8
SLOTS = 6
ROWS = 4
LANES = 128
VLIM = 56 * 1024 * 1024


def smem():
    return pl.BlockSpec(memory_space=SMEM)


def vmem():
    return pl.BlockSpec(memory_space=VMEM)


def choose_kernel(cycle, me_ref, target_ref, own_ref, up_ref, down_ref, code_ref, slot_ref, sems):
    me = me_ref[0]
    below = lax.rem(me + cycle - 1, cycle)
    above = lax.rem(me + 1, cycle)
    up_slot = jnp.int32(0)
    down_slot = jnp.int32(0)
    for o in range(ROWS):
        code_ref[o] = 0
        slot_ref[o] = 0
    for k in range(SLOTS):
        shard = target_ref[0, me * SLOTS + k]
        offset = target_ref[1, me * SLOTS + k]
        up_slot = jnp.where(shard == above, k, up_slot)
        down_slot = jnp.where(shard == below, k, down_slot)

        @pl.when(shard == me)
        def _():
            slot_ref[offset] = k

        for owner, code in ((below, 1), (above, 2)):
            their_shard = target_ref[0, owner * SLOTS + k]
            their_offset = target_ref[1, owner * SLOTS + k]

            @pl.when(their_shard == me)
            def _():
                code_ref[their_offset] = code

    up = pltpu.make_async_copy(own_ref.at[up_slot], up_ref, sems.at[0])
    down = pltpu.make_async_copy(own_ref.at[down_slot], down_ref, sems.at[1])
    up.start()
    down.start()
    up.wait()
    down.wait()


def tables_kernel(docs, length_ref, taps_ref, table_ref, fwd_ref, bwd_ref):
    def one_doc(d, start):
        end = start + length_ref[d]
        table_ref[3, d] = start
        table_ref[4, d] = end

        def heads(b, carry):
            table_ref[0, b] = b - lax.shift_right_logical(start, 8)
            table_ref[1, b] = jnp.minimum(end - BLK * b, BLK)
            return carry

        def tails(b, carry):
            table_ref[2, b] = jnp.maximum(start - BLK * b, 0)
            return carry

        lax.fori_loop(
            lax.shift_right_logical(start + BLK - 1, 8),
            lax.shift_right_logical(end + BLK - 1, 8),
            heads,
            0,
        )
        lax.fori_loop(
            lax.shift_right_logical(start, 8), lax.shift_right_logical(end, 8), tails, 0
        )
        return end

    lax.fori_loop(0, docs, one_doc, jnp.int32(0))
    width = BLK * (HOPS + 2)
    part = 32
    for r in range(BLK // part):
        rows = jnp.broadcast_to(taps_ref[...], (part, width))
        rows = pltpu.roll(rows, part * r, 1, stride=1, stride_axis=0)
        for delta in range(HOPS + 1):
            at = BLK * (HOPS - delta) + part * r
            fwd_ref[at : at + part, :] = rows[:, BLK * (delta + 1) : BLK * (delta + 2)].astype(BF16)
    for delta in range(HOPS + 1):
        at = BLK * (HOPS - delta)
        bwd_ref[BLK * delta : BLK * (delta + 1), :] = fwd_ref[at : at + BLK, :].T


def pick(code, own_ref, low_ref, high_ref, stream):
    own = own_ref[0, stream]
    low = low_ref[stream]
    high = high_ref[stream]
    return jnp.where(code == 0, own, jnp.where(code == 1, low, high))


def round_mul(a, b):
    return (a.astype(F32) * b.astype(F32)).astype(BF16)


def make_kernel(code_ref, slot_ref, own_ref, low_ref, high_ref, grad_ref, sent_ref):
    code = code_ref[pl.program_id(0)]

    def emit(read):
        product = round_mul(read(1), read(2))
        grad_mid = round_mul(grad_ref[...], read(0))
        peers, _, chans, toks = sent_ref.shape
        sent_ref[:, 0] = product.T.reshape(peers, chans, toks)
        sent_ref[:, 1] = grad_mid.T.reshape(peers, chans, toks)

    pl.when(code == 0)(lambda: emit(lambda s: own_ref[0, s]))
    pl.when(code == 1)(lambda: emit(lambda s: low_ref[s]))
    pl.when(code == 2)(lambda: emit(lambda s: high_ref[s]))


def place_of(b, peers):
    src = jnp.where(b < peers, b, 2 * peers - 1 - b)
    lane = pl.multiple_of(jnp.where(b < peers, 0, BLK), BLK)
    return src, lane


def long_kernel(
    table_ref, got_ref, fwd_ref, bwd_ref, out_ref,
    x_all, z_all, x_tail, z_head, reach, head_end, tail_start,
    xd, zd, ze, flip_all, flip_head, flip_doc, conv, back, pairs, extra,
):
    peers = got_ref.shape[0]
    ch = got_ref.shape[2]
    blocks = 2 * peers
    docs = blocks
    rows = blocks * ch
    pad = HOPS * ch
    lane = lax.broadcasted_iota(jnp.int32, (ch, BLK), 1)
    zero = jnp.zeros((), BF16)

    x_tail[0:pad, :] = jnp.zeros((pad, BLK), BF16)
    z_head[rows : rows + pad, :] = jnp.zeros((pad, BLK), BF16)
    reach[rows : rows + pad, :] = jnp.full((pad, BLK), -1, BF16)

    def spread(b, total):
        src, at_lane = place_of(b, peers)
        at = pl.multiple_of(b * ch, ch)
        x = got_ref[src, 0, :, pl.ds(at_lane, BLK)]
        z = got_ref[src, 1, :, pl.ds(at_lane, BLK)]
        x_all[pl.ds(at, ch), :] = x
        z_all[pl.ds(at, ch), :] = z
        first, end, tail = table_ref[0, b], table_ref[1, b], table_ref[2, b]
        x_f, z_f = x.astype(F32), z.astype(F32)
        x_tail[pl.ds(at + pad, ch), :] = jnp.where(lane >= tail, x_f, 0).astype(BF16)
        z_head[pl.ds(at, ch), :] = jnp.where(lane < end, z_f, 0).astype(BF16)
        reach[pl.ds(at, ch), :] = jnp.full((ch, BLK), first.astype(F32)).astype(BF16)
        head_end[pl.ds(at, ch), :] = jnp.full((ch, BLK), end, jnp.int32)
        tail_start[pl.ds(at, ch), :] = jnp.full((ch, BLK), tail, jnp.int32)
        return total + x_f * z_f

    skip = lax.fori_loop(0, blocks, spread, jnp.zeros((ch, BLK), F32))

    def doc_parts(d):
        start, end = table_ref[3, d], table_ref[4, d]
        end_block = lax.shift_right_logical(end - 1, 8)
        end_at = jnp.bitwise_and(end, BLK - 1)
        end_from = jnp.maximum(start - BLK * end_block, 0)
        start_block = lax.shift_right_logical(start, 8)
        start_at = jnp.bitwise_and(start, BLK - 1)
        start_at = jnp.where(start_at == 0, BLK, start_at)
        start_to = end - BLK * start_block
        return end_block, end_from, end_at, start_block, start_at, start_to

    def spread_docs(d, carry):
        end_block, end_from, end_at, start_block, start_at, start_to = doc_parts(d)
        at = pl.multiple_of(d * ch, ch)
        at_end = pl.multiple_of(end_block * ch, ch)
        at_start = pl.multiple_of(start_block * ch, ch)
        ends = (lane >= end_from) & (lane < end_at)
        begins = (lane >= start_at) & (lane < start_to)
        x = x_all[pl.ds(at_end, ch), :].astype(F32)
        z = z_all[pl.ds(at_end, ch), :].astype(F32)
        z2 = z_all[pl.ds(at_start, ch), :].astype(F32)
        xd[pl.ds(at, ch), :] = jnp.where(ends, x, 0).astype(BF16)
        zd[pl.ds(at, ch), :] = jnp.where(ends, z, 0).astype(BF16)
        ze[pl.ds(at, ch), :] = jnp.where(begins, z2, 0).astype(BF16)
        return carry

    lax.fori_loop(0, docs, spread_docs, 0)

    r_id = lax.broadcasted_iota(jnp.int32, (BLK, BLK), 0)
    c_id = lax.broadcasted_iota(jnp.int32, (BLK, BLK), 1)
    anti = jnp.where(r_id + c_id == BLK - 1, 1.0, 0.0).astype(BF16)
    step = 256
    steps = rows // step

    def flips(c, carry):
        at = pl.multiple_of(c * step, step)
        for src, dst in ((z_all, flip_all), (z_head, flip_head), (zd, flip_doc)):
            dst[:, pl.ds(at, step)] = lax.dot_general(
                anti, src[pl.ds(at, step), :], (((1,), (1,)), ((), ())),
                preferred_element_type=F32,
            ).astype(BF16)
        return carry

    lax.fori_loop(0, steps, flips, 0)
    pairs[...] = jnp.zeros_like(pairs)
    wide = lax.broadcasted_iota(jnp.int32, (step, BLK), 1)
    far = HOPS * BLK

    def dot(a, b):
        return jnp.dot(a, b, preferred_element_type=F32)

    def chunk(c, carry):
        at = pl.multiple_of(c * step, step)
        here = reach[pl.ds(at, step), :]
        xs = []
        for delta in range(HOPS, -1, -1):
            x = x_tail[pl.ds(at + ch * (HOPS - delta), step), :]
            xs.append(jnp.where(here >= delta, x, zero) if delta else x)
        x_far = jnp.concatenate(xs[:-1], axis=1)
        far_part = dot(x_far, fwd_ref[0:far, :])
        far_part = jnp.where(wide < head_end[pl.ds(at, step), :], far_part, 0.0)
        conv[pl.ds(at, step), :] = far_part + dot(xs[-1], fwd_ref[far:, :])
        pairs[:, 0:far] += dot(flip_head[:, pl.ds(at, step)], x_far)
        pairs[:, far:] += dot(flip_all[:, pl.ds(at, step)], xs[-1]) + dot(
            flip_doc[:, pl.ds(at, step)], xd[pl.ds(at, step), :]
        )
        zs = []
        for delta in range(HOPS + 1):
            z = z_head[pl.ds(at + ch * delta, step), :]
            there = reach[pl.ds(at + ch * delta, step), :]
            zs.append(jnp.where(there >= delta, z, zero) if delta else z)
        z_far = jnp.concatenate(zs[1:], axis=1)
        far_part = dot(z_far, bwd_ref[BLK:, :])
        far_part = jnp.where(wide >= tail_start[pl.ds(at, step), :], far_part, 0.0)
        back[pl.ds(at, step), :] = far_part + dot(zs[0], bwd_ref[0:BLK, :])
        return carry

    lax.fori_loop(0, steps, chunk, 0)

    def doc_chunk(c, carry):
        at = pl.multiple_of(c * step, step)
        y_end = dot(xd[pl.ds(at, step), :], fwd_ref[far:, :])
        y_start = dot(ze[pl.ds(at, step), :], bwd_ref[0:BLK, :])
        for i in range(step // ch):
            d = c * (step // ch) + i
            end_block, end_from, end_at, start_block, start_at, start_to = doc_parts(d)
            at_end = pl.multiple_of(end_block * ch, ch)
            at_start = pl.multiple_of(start_block * ch, ch)
            conv[pl.ds(at_end, ch), :] += jnp.where(
                lane < end_at, y_end[i * ch : (i + 1) * ch], 0.0
            )
            back[pl.ds(at_start, ch), :] += jnp.where(
                lane >= start_at, y_start[i * ch : (i + 1) * ch], 0.0
            )
        return carry

    lax.fori_loop(0, steps, doc_chunk, 0)

    def gather_out(b, carry):
        src, at_lane = place_of(b, peers)
        at = pl.multiple_of(b * ch, ch)
        out_ref[src, 0, :, pl.ds(at_lane, BLK)] = conv[pl.ds(at, ch), :].astype(BF16)
        out_ref[src, 1, :, pl.ds(at_lane, BLK)] = back[pl.ds(at, ch), :].astype(BF16)
        return carry

    lax.fori_loop(0, blocks, gather_out, 0)

    total = jnp.zeros((8, far + 2 * BLK), F32)
    for r in range(BLK // 8):
        band = jnp.concatenate([pairs[8 * r : 8 * (r + 1), :], jnp.zeros((8, BLK), F32)], axis=1)
        total = total + pltpu.roll(band, 8 * r, 1, stride=1, stride_axis=0)
    lags = jnp.sum(total, axis=0, keepdims=True)
    extra[...] = jnp.zeros_like(extra)
    count = (far + BLK) // LANES
    for r in range(count):
        extra[r : r + 1, :] = lags[:, LANES * r : LANES * (r + 1)]
    by_channel = jnp.sum(skip, axis=1, keepdims=True)
    e_row = lax.broadcasted_iota(jnp.int32, (ch, LANES), 0)
    e_col = lax.broadcasted_iota(jnp.int32, (ch, LANES), 1)
    skip_row = jnp.sum(jnp.where(e_row == e_col, by_channel, 0.0), axis=0, keepdims=True)
    high = skip_row.astype(BF16).astype(F32)
    extra[count : count + 1, :] = high
    extra[count + 1 : count + 2, :] = skip_row - high
    packed = extra[...].astype(BF16)
    for side in range(2):
        out_ref[:, side, :, 2 * BLK : 2 * BLK + LANES] = jnp.broadcast_to(
            packed[side * ch : (side + 1) * ch][None], (peers, ch, LANES)
        )


def finish_kernel(
    code_ref, slot_ref, own_ref, low_ref, high_ref, grad_ref, gain_ref, got_ref, y_ref, grads_ref
):
    code = code_ref[pl.program_id(0)]

    def emit(read):
        peers, _, chans, toks = got_ref.shape
        width = peers * chans
        conv = got_ref[:, 0].reshape(width, toks).T.astype(F32)
        back = got_ref[:, 1].reshape(width, toks).T.astype(F32)
        query, key_in, value = (read(s).astype(F32) for s in range(3))
        grad = grad_ref[...].astype(F32)
        gain = gain_ref[...]
        product = (key_in * value).astype(BF16).astype(F32)
        grad_mid = (grad * query).astype(BF16).astype(F32)
        mixed = conv + gain * product
        grad_x = back + gain * grad_mid
        y_ref[...] = (query * mixed).astype(BF16)
        grads_ref[0] = (grad * mixed).astype(BF16)
        grads_ref[1] = (grad_x * value).astype(BF16)
        grads_ref[2] = (grad_x * key_in).astype(BF16)

    pl.when(code == 0)(lambda: emit(lambda s: own_ref[0, s]))
    pl.when(code == 1)(lambda: emit(lambda s: low_ref[s]))
    pl.when(code == 2)(lambda: emit(lambda s: high_ref[s]))


def shifted(array, axis, by):
    length = lax.axis_size(axis)
    return lax.ppermute(array, axis, [(i, (i + by) % length) for i in range(length)])


def on_device(rollout_rows, pack_targets, doc_lengths, filter_taps, skip_gain, out_grad):
    peers = lax.axis_size("ctx")
    index = lax.axis_index("ctx").astype(jnp.int32)
    slots, row_len, streams, channels = rollout_rows.shape
    tokens = out_grad.shape[0]
    filters, tap_count = filter_taps.shape
    docs = doc_lengths.shape[0]
    ch = channels // peers
    blocks = 2 * peers
    own = rollout_rows.transpose(0, 2, 1, 3)
    row_shape = jax.ShapeDtypeStruct((streams, row_len, channels), BF16)

    any_spec = pl.BlockSpec(memory_space=pl.ANY)
    up, down, code, slot = pl.pallas_call(
        functools.partial(choose_kernel, peers),
        out_shape=(
            row_shape,
            row_shape,
            jax.ShapeDtypeStruct((ROWS,), jnp.int32),
            jax.ShapeDtypeStruct((ROWS,), jnp.int32),
        ),
        in_specs=[smem(), smem(), any_spec],
        out_specs=(any_spec, any_spec, smem(), smem()),
        scratch_shapes=[pltpu.SemaphoreType.DMA((2,))],
        name="choose",
    )(index[None], pack_targets.T, own)
    low = shifted(up, "ctx", 1)
    high = shifted(down, "ctx", -1)

    mine = lax.dynamic_index_in_dim(filter_taps, index // (peers // filters), 0, keepdims=True)
    mine = mine.astype(BF16).astype(F32)
    mine = jnp.pad(mine, [(0, 0), (BLK, BLK * (HOPS + 1) - tap_count)])
    band = jax.ShapeDtypeStruct((BLK * (HOPS + 1), BLK), BF16)
    table, fwd_band, bwd_band = pl.pallas_call(
        functools.partial(tables_kernel, docs),
        out_shape=(jax.ShapeDtypeStruct((8, docs), jnp.int32), band, band),
        in_specs=[smem(), vmem()],
        out_specs=(smem(), vmem(), vmem()),
        compiler_params=pltpu.CompilerParams(vmem_limit_bytes=VLIM),
        cost_estimate=pl.CostEstimate(flops=0, bytes_accessed=20_000_000, transcendentals=0),
        name="tables",
    )(doc_lengths, mine)

    def row_specs():
        return [
            pl.BlockSpec(
                (1, streams, row_len, channels), lambda o, code, slot: (slot[o], 0, 0, 0)
            ),
            pl.BlockSpec((streams, row_len, channels), lambda o, code, slot: (0, 0, 0)),
            pl.BlockSpec((streams, row_len, channels), lambda o, code, slot: (0, 0, 0)),
            pl.BlockSpec((row_len, channels), lambda o, code, slot: (o, 0)),
        ]

    sent = pl.pallas_call(
        make_kernel,
        out_shape=jax.ShapeDtypeStruct((peers, 2, ch, tokens), BF16),
        grid_spec=pltpu.PrefetchScalarGridSpec(
            num_scalar_prefetch=2,
            grid=(ROWS,),
            in_specs=row_specs(),
            out_specs=pl.BlockSpec((peers, 2, ch, row_len), lambda o, code, slot: (0, 0, 0, o)),
        ),
        compiler_params=pltpu.CompilerParams(vmem_limit_bytes=VLIM),
        name="products",
    )(code, slot, own, low, high, out_grad)
    got = lax.all_to_all(sent, "ctx", 0, 0, tiled=True)

    rows = blocks * ch
    pad = HOPS * ch
    reply = pl.pallas_call(
        long_kernel,
        out_shape=jax.ShapeDtypeStruct((peers, 2, ch, tokens + LANES), BF16),
        in_specs=[smem(), vmem(), vmem(), vmem()],
        out_specs=vmem(),
        scratch_shapes=[
            VMEM((rows, BLK), BF16),
            VMEM((rows, BLK), BF16),
            VMEM((rows + pad, BLK), BF16),
            VMEM((rows + pad, BLK), BF16),
            VMEM((rows + pad, BLK), BF16),
            VMEM((rows, BLK), jnp.int32),
            VMEM((rows, BLK), jnp.int32),
            VMEM((rows, BLK), BF16),
            VMEM((rows, BLK), BF16),
            VMEM((rows, BLK), BF16),
            VMEM((BLK, rows), BF16),
            VMEM((BLK, rows), BF16),
            VMEM((BLK, rows), BF16),
            VMEM((rows, BLK), F32),
            VMEM((rows, BLK), F32),
            VMEM((BLK, BLK * (HOPS + 1)), F32),
            VMEM((2 * ch, LANES), F32),
        ],
        compiler_params=pltpu.CompilerParams(vmem_limit_bytes=VLIM),
        name="long_filter",
    )(table, got, fwd_band, bwd_band)
    back = lax.all_to_all(reply, "ctx", 0, 0, tiled=True)

    sums = back[:, :, :, tokens:].astype(F32).reshape(peers, 2 * ch, LANES)
    count = BLK * (HOPS + 1) // LANES
    tap_sum = sums[:, :count].reshape(filters, peers // filters, count * LANES).sum(axis=1)
    skip_total = (sums[:, count, :ch] + sums[:, count + 1, :ch]).reshape(channels)
    other = lax.ppermute(tap_sum, "ch", [(0, 1), (1, 0)])

    out_y, grads = pl.pallas_call(
        finish_kernel,
        out_shape=(
            jax.ShapeDtypeStruct((tokens, channels), BF16),
            jax.ShapeDtypeStruct((streams, tokens, channels), BF16),
        ),
        grid_spec=pltpu.PrefetchScalarGridSpec(
            num_scalar_prefetch=2,
            grid=(ROWS,),
            in_specs=row_specs()
            + [
                pl.BlockSpec((1, channels), lambda o, code, slot: (0, 0)),
                pl.BlockSpec((peers, 2, ch, row_len), lambda o, code, slot: (0, 0, 0, o)),
            ],
            out_specs=(
                pl.BlockSpec((row_len, channels), lambda o, code, slot: (o, 0)),
                pl.BlockSpec((streams, row_len, channels), lambda o, code, slot: (0, o, 0)),
            ),
        ),
        compiler_params=pltpu.CompilerParams(vmem_limit_bytes=VLIM),
        name="finish",
    )(code, slot, own, low, high, out_grad, skip_gain[None], back)

    seq_total = tokens * peers
    chan_total = channels * lax.axis_size("ch")
    tap_total = (tap_sum + other)[:, ::-1][:, :tap_count]
    grad_taps = tap_total / math.sqrt(seq_total * chan_total / filters)
    grad_skip = skip_total / math.sqrt(seq_total)
    return (out_y, grads.transpose(1, 0, 2), grad_taps, grad_skip)


def solution(mesh):
    return jax.shard_map(
        on_device,
        mesh=mesh,
        in_specs=(P("ctx", None, None, "ch"), P(), P(), P(), P("ch"), P("ctx", "ch")),
        out_specs=(P("ctx", "ch"), P("ctx", None, "ch"), P(), P("ch")),
        check_vma=False,
    )
```

time: 756 us -> 200 us (0.26); the launches traced: 744 us -> 199 us
  local copies, waits for them, and re-layouts: 196 us -> 5.96 us
  blocking collectives: 224 us -> 39.9 us
  Pallas kernels: 0 us -> 94.1 us
  starting transfers between devices: 98.3 us -> 13.9 us
  waiting for transfers between devices: 116 us -> 41.9 us
  matrix products: 72.4 us -> 0 us
  other arithmetic: 34.8 us -> 2.73 us
    psum x2 -> x0, blocking collectives: 224 us -> none  [the longest x1 142 us: on_device(): skip_total = lax.psum(skip_local, 'ctx')]
    pallas_call x0 -> x5, Pallas kernels: none -> 94.1 us  [the longest x1 50.1 us: on_device(): pl.pallas_call(functools.partial(choose_kernel, peers), out_shape=(row_sh...]
    ppermute x32 -> x1, starting transfers between devices: 95.5 us -> 2.69 us  [on_device(): other = lax.ppermute(tap_sum, 'ch', [(0, 1), (1, 0)])]
    dot_general x24 -> x0, matrix products: 72.4 us -> none  [the longest x8 25.6 us: per_filter(): lax.dot_general(own_grad, sources, (((1,), (1,)), ((), ())), preferred_el...]
    reshape x21 -> x1, local copies, waits for them, and re-layouts: 71.4 us -> 1.29 us  [on_device(): sums[:, :count].reshape(filters, peers // filters, count * LANES)]
    ppermute x32 -> x1, waiting for transfers between devices: 66.5 us -> 0.01 us  [on_device(): other = lax.ppermute(tap_sum, 'ch', [(0, 1), (1, 0)])]
    unnamed x97 -> x11, local copies, waits for them, and re-layouts: 51.3 us -> 3.77 us
    all_to_all x0 -> x1, blocking collectives: none -> 39.9 us  [on_device(): back = lax.all_to_all(reply, 'ctx', 0, 0, tiled=True)]
  transfers between devices with their start and end apart: 34 -> 4, of which waited for: 15 -> 3; matrix products, arithmetic and copies ran while one was open for 25% -> 1% of each run, Pallas kernels for 0% -> 7%
where the time goes in v1:
time: 200 us; the launch traced here: 199 us
  Pallas kernels  94.1 us (47%)
  waiting for transfers between devices  41.9 us (21%)
  blocking collectives  39.9 us (20%)
  starting transfers between devices  13.9 us (7%)
  local copies, waits for them, and re-layouts  5.96 us (3%)
  other arithmetic  2.73 us (1%)
    pallas_call x1, Pallas kernels, on_device(): pl.pallas_call(functools.partial(choose_kernel, peers), out_shape=(row_sh...  50.1 us
    all_to_all x1, blocking collectives, on_device(): back = lax.all_to_all(reply, 'ctx', 0, 0, tiled=True)  39.9 us
    pallas_call x1, Pallas kernels, on_device(): pl.pallas_call(long_kernel, out_shape=jax.ShapeDtypeStruct((peers, 2, ch,...  24.7 us
    all_to_all x1, waiting for transfers between devices, on_device(): got = lax.all_to_all(sent, 'ctx', 0, 0, tiled=True)  21.8 us
    ppermute x2, waiting for transfers between devices, shifted(): lax.ppermute(array, axis, [(i, (i + by) % length) for i in range(length)])  20 us
    all_to_all x1, starting transfers between devices, on_device(): got = lax.all_to_all(sent, 'ctx', 0, 0, tiled=True)  8.42 us
    pallas_call x1, Pallas kernels, on_device(): pl.pallas_call(finish_kernel, out_shape=(jax.ShapeDtypeStruct((tokens, ch...  7.25 us
    pallas_call x1, Pallas kernels, on_device(): pl.pallas_call(functools.partial(tables_kernel, docs), out_shape=(jax.Sha...  6.51 us
  transfers between devices with their start and end apart: 4, of which 3 were waited for; matrix products, arithmetic and copies ran while one was open for 1% of the time, Pallas kernels for 7%

profile of v1, /device:TPU:1, one launch (start us, length us, event | category | flops | bytes accessed | tf_op | source)
XLA Modules:
  0.0 199.2 jit_solution(12483487026428499116)
XLA Ops:
  0.7 50.1 %choose.1 = (bf16[3,128,1024]{2,1,0:T(8,128)(2,1)}, bf16[3,128,1024]{2,1,0:T(8,128)(2,1)}, s32[4]{0:T(128)}, s32[4]{0:T(128)}) custom-call(s32[1]{0:T(128)} %bitcast.me_ref, s32[2,384]{1,0:T(2,128)} %bitcast.20, bf16[6,3,128,1024]{3,2,1,0:T(8,128)(2,1)} %bitcast.13), custom_call_target="tpu_custom_call" | custom-call | tf_op jit(solution)/shard_map/choose/pallas_call | solution.py:350
  50.7 2.8 %collective-permute-start = (bf16[3,128,1024]{2,1,0:T(8,128)(2,1)}, bf16[3,128,1024]{2,1,0:T(8,128)(2,1)S(1)}, u32[]{:S(2)}, u32[]{:S(2)}) collective-permute-start(bf16[3,128,1024]{2,1,0:T(8,128)(2,1)} %get-tuple-element.15), channel_id=1, source_target_pairs={{0,2},{2,4},{4,6},{6,8},{8,10},{10,12},{12,14},{14,16},{16,18},{18... | collective-permute-start | bytes 2359304 | tf_op jit(solution)/shard_map/ppermute | solution.py:334
  53.5 17.7 %collective-permute-done.low_ref = bf16[3,128,1024]{2,1,0:T(8,128)(2,1)S(1)} collective-permute-done((bf16[3,128,1024]{2,1,0:T(8,128)(2,1)}, bf16[3,128,1024]{2,1,0:T(8,128)(2,1)S(1)}, u32[]{:S(2)}, u32[]{:S(2)}) %collective-permute-start) | collective-permute-done | bytes 786464 | tf_op jit(solution)/shard_map/ppermute | solution.py:334
  71.2 2.4 %collective-permute-done.1.high_ref = bf16[3,128,1024]{2,1,0:T(8,128)(2,1)S(1)} collective-permute-done((bf16[3,128,1024]{2,1,0:T(8,128)(2,1)}, bf16[3,128,1024]{2,1,0:T(8,128)(2,1)S(1)}, u32[]{:S(2)}, u32[]{:S(2)}) %collective-permute-start.1) | collective-permute-done | bytes 786464 | tf_op jit(solution)/shard_map/ppermute | solution.py:334
  73.5 0.9 copy-done.4
  74.5 5.6 %products.1 = bf16[64,2,16,512]{3,2,1,0:T(8,128)(2,1)} custom-call(s32[4]{0:T(128)} %get-tuple-element.13.code_ref, s32[4]{0:T(128)} %get-tuple-element.14.slot_ref, bf16[6,3,128,1024]{3,2,1,0:T(8,128)(2,1)} %bitcast.14, bf16[3,128,1024]{2,1,0:T(8,128)(2,1)} %copy-done.3, bf16[3,128,1024]{2,1,0:T(8,128)(2,1)} %copy-done.4, bf16[512,1024]{1,0:T(8,128)(2,1)} %grad_ref.3), custom_call_target="tpu_custom_call" | custom-call | tf_op jit(solution)/shard_map/products/pallas_call | solution.py:390
  80.1 8.4 %all-to-all-start = ((bf16[64,2,16,512]{3,2,1,0:T(8,128)(2,1)}), bf16[64,2,16,512]{3,2,1,0:T(8,128)(2,1)S(1)}, u32[]{:S(2)}, u32[]{:S(2)}) async-start(bf16[64,2,16,512]{3,2,1,0:T(8,128)(2,1)} %products.1), calls=%async_computation | async-start | bytes 4194304 | tf_op jit(solution)/shard_map/all_to_all | solution.py:402
  88.6 0.6 pad_convert_fusion.taps_ref
  89.2 6.5 %tables.1 = (s32[8,128]{1,0:T(8,128)}, bf16[2304,256]{1,0:T(8,128)(2,1)}, bf16[2304,256]{1,0:T(8,128)(2,1)}) custom-call(s32[128]{0:T(128)} %length_ref.1, f32[1,2560]{1,0:T(1,128)} %pad_convert_fusion.taps_ref), custom_call_target="tpu_custom_call" | custom-call | bytes 20000000 | tf_op jit(solution)/shard_map/tables/pallas_call | solution.py:370
  95.7 21.8 %all-to-all-done.got_ref = bf16[64,2,16,512]{3,2,1,0:T(8,128)(2,1)S(1)} async-done(((bf16[64,2,16,512]{3,2,1,0:T(8,128)(2,1)}), bf16[64,2,16,512]{3,2,1,0:T(8,128)(2,1)S(1)}, u32[]{:S(2)}, u32[]{:S(2)}) %all-to-all-start) | async-done | bytes 2097184 | tf_op jit(solution)/shard_map/all_to_all | solution.py:402
  117.5 1.3 copy-done.2
  118.9 24.7 %long_filter.1 = bf16[64,2,16,640]{3,2,1,0:T(8,128)(2,1)} custom-call(s32[8,128]{1,0:T(8,128)} %get-tuple-element.17.table_ref, bf16[64,2,16,512]{3,2,1,0:T(8,128)(2,1)} %copy-done.2, bf16[2304,256]{1,0:T(8,128)(2,1)} %get-tuple-element.18.fwd_ref, bf16[2304,256]{1,0:T(8,128)(2,1)} %get-tuple-element.19.bwd_ref), custom_call_target="tpu_custom_call" | custom-call | tf_op jit(solution)/shard_map/long_filter/pallas_call | solution.py:406
  143.5 39.9 %all_to_all.10.got_ref = bf16[64,2,16,640]{3,2,1,0:T(8,128)(2,1)S(1)} all-to-all(bf16[64,2,16,640]{3,2,1,0:T(8,128)(2,1)} %long_filter.1), channel_id=1, replica_groups=mesh['ctx'=64,'ch'=2] {'ctx'}, dimensions={0} | all-to-all | bytes 5242880 | tf_op jit(solution)/shard_map/all_to_all | solution.py:433
  183.5 0.1 slice.24
  183.6 0.2 bitcast_convert_fusion
  183.8 0.1 slice.25
  183.9 1.3 reshape.25
  185.1 1.2 reduce_sum.9
  186.3 2.7 %collective-permute-start.2 = (f32[4,2304]{1,0:T(4,128)S(1)}, f32[4,2304]{1,0:T(4,128)S(1)}, u32[]{:S(2)}, u32[]{:S(2)}) collective-permute-start(f32[4,2304]{1,0:T(4,128)S(1)} %reduce_sum.9), channel_id=1, source_target_pairs={{0,1},{1,0},{2,3},{3,2},{4,5},{5,4},{6,7},{7,6},{8,9},{9,8},{10,11... | collective-permute-start | bytes 110600 | tf_op jit(solution)/shard_map/ppermute | solution.py:439
  189.0 0.7 div.29
  189.7 7.3 %finish.1 = (bf16[512,1024]{1,0:T(8,128)(2,1)}, bf16[3,512,1024]{2,1,0:T(8,128)(2,1)}) custom-call(s32[4]{0:T(128)} %get-tuple-element.13.code_ref, s32[4]{0:T(128)} %get-tuple-element.14.slot_ref, bf16[6,3,128,1024]{3,2,1,0:T(8,128)(2,1)} %bitcast.15, bf16[3,128,1024]{2,1,0:T(8,128)(2,1)} %copy-done.3, bf16[3,128,1024]{2,1,0:T(8,128)(2,1)} %copy-done.4, ...), custom_call_target="tpu_custom_call" | custom-call | tf_op jit(solution)/shard_map/finish/pallas_call | solution.py:441
  196.9 0.1 slice_add_fusion
  197.0 1.5 reverse.1
  198.5 0.7 broadcast_multiply_fusion
  (13 shorter events, 0.1 us)
Async XLA Ops:
  0.6 87.9 %copy-start = (f32[4,2049]{1,0:T(4,128)S(1)}, f32[4,2049]{1,0:T(4,128)}, u32[]{:S(2)}) copy-start(f32[4,2049]{1,0:T(4,128)} %param.9) | copy-start | bytes 98356
  50.7 20.4 %collective-permute-start = (bf16[3,128,1024]{2,1,0:T(8,128)(2,1)}, bf16[3,128,1024]{2,1,0:T(8,128)(2,1)S(1)}, u32[]{:S(2)}, u32[]{:S(2)}) collective-permute-start(bf16[3,128,1024]{2,1,0:T(8,128)(2,1)} %get-tuple-element.15), channel_id=1, source_target_pairs={{0,2},{2,4},{4,6},{6,8},{8,10},{10,12},{12,14},{14,16},{16,18},{18... | collective-permute-start | bytes 2359304 | tf_op jit(solution)/shard_map/ppermute | solution.py:334
  53.5 20.1 %collective-permute-start.1 = (bf16[3,128,1024]{2,1,0:T(8,128)(2,1)}, bf16[3,128,1024]{2,1,0:T(8,128)(2,1)S(1)}, u32[]{:S(2)}, u32[]{:S(2)}) collective-permute-start(bf16[3,128,1024]{2,1,0:T(8,128)(2,1)} %get-tuple-element.16), channel_id=1, source_target_pairs={{0,126},{2,0},{4,2},{6,4},{8,6},{10,8},{12,10},{14,12},{16,14},{18... | collective-permute-start | bytes 2359304 | tf_op jit(solution)/shard_map/ppermute | solution.py:334
  71.2 2.4 %copy-start.3 = (bf16[3,128,1024]{2,1,0:T(8,128)(2,1)}, bf16[3,128,1024]{2,1,0:T(8,128)(2,1)S(1)}, u32[]{:S(2)}) copy-start(bf16[3,128,1024]{2,1,0:T(8,128)(2,1)S(1)} %collective-permute-done.low_ref) | copy-start | bytes 2359300
  73.5 0.9 copy-start.4
  80.1 37.4 %all-to-all-start = ((bf16[64,2,16,512]{3,2,1,0:T(8,128)(2,1)}), bf16[64,2,16,512]{3,2,1,0:T(8,128)(2,1)S(1)}, u32[]{:S(2)}, u32[]{:S(2)}) async-start(bf16[64,2,16,512]{3,2,1,0:T(8,128)(2,1)} %products.1), calls=%async_computation | async-start | bytes 4194304 | tf_op jit(solution)/shard_map/all_to_all | solution.py:402
  117.5 1.3 copy-start.2
  183.5 1.7 copy-start.1
  186.3 10.6 %collective-permute-start.2 = (f32[4,2304]{1,0:T(4,128)S(1)}, f32[4,2304]{1,0:T(4,128)S(1)}, u32[]{:S(2)}, u32[]{:S(2)}) collective-permute-start(f32[4,2304]{1,0:T(4,128)S(1)} %reduce_sum.9), channel_id=1, source_target_pairs={{0,1},{1,0},{2,3},{3,2},{4,5},{5,4},{6,7},{7,6},{8,9},{9,8},{10,11... | collective-permute-start | bytes 110600 | tf_op jit(solution)/shard_map/ppermute | solution.py:439

commit v2 on v1

--- a/solution.py
+++ b/solution.py
@@ -18,6 +18,7 @@
 SLOTS = 6
 ROWS = 4
 LANES = 128
+TAP_ROWS = 17
 VLIM = 56 * 1024 * 1024
 
 
@@ -29,20 +30,38 @@
     return pl.BlockSpec(memory_space=VMEM)
 
 
-def choose_kernel(cycle, me_ref, target_ref, own_ref, up_ref, down_ref, code_ref, slot_ref, sems):
+def choose_kernel(
+    cycle, me_ref, target_ref, own_ref, up_ref, down_ref, up_kv_ref, down_kv_ref,
+    code_ref, slot_ref, sems,
+):
     me = me_ref[0]
     below = lax.rem(me + cycle - 1, cycle)
     above = lax.rem(me + 1, cycle)
     up_slot = jnp.int32(0)
     down_slot = jnp.int32(0)
+    for k in range(SLOTS):
+        shard = target_ref[0, me * SLOTS + k]
+        up_slot = jnp.where(shard == above, k, up_slot)
+        down_slot = jnp.where(shard == below, k, down_slot)
+    copies = []
+    for n, (slot, first, later) in enumerate(
+        ((up_slot, up_ref, up_kv_ref), (down_slot, down_ref, down_kv_ref))
+    ):
+        copies.append(
+            (
+                pltpu.make_async_copy(own_ref.at[slot, 0], first.at[0], sems.at[2 * n]),
+                pltpu.make_async_copy(own_ref.at[slot, pl.ds(1, 2)], later, sems.at[2 * n + 1]),
+            )
+        )
+    for one, two in copies:
+        two.start()
+        one.start()
     for o in range(ROWS):
         code_ref[o] = 0
         slot_ref[o] = 0
     for k in range(SLOTS):
         shard = target_ref[0, me * SLOTS + k]
         offset = target_ref[1, me * SLOTS + k]
-        up_slot = jnp.where(shard == above, k, up_slot)
-        down_slot = jnp.where(shard == below, k, down_slot)
 
         @pl.when(shard == me)
         def _():
@@ -56,12 +75,10 @@
             def _():
                 code_ref[their_offset] = code
 
-    up = pltpu.make_async_copy(own_ref.at[up_slot], up_ref, sems.at[0])
-    down = pltpu.make_async_copy(own_ref.at[down_slot], down_ref, sems.at[1])
-    up.start()
-    down.start()
-    up.wait()
-    down.wait()
+    for (one, two), first, later in zip(copies, (up_ref, down_ref), (up_kv_ref, down_kv_ref)):
+        two.wait()
+        first[1] = round_mul(later[0], later[1])
+        one.wait()
 
 
 def tables_kernel(docs, length_ref, taps_ref, table_ref, fwd_ref, bwd_ref):
@@ -104,13 +121,6 @@
         bwd_ref[BLK * delta : BLK * (delta + 1), :] = fwd_ref[at : at + BLK, :].T
 
 
-def pick(code, own_ref, low_ref, high_ref, stream):
-    own = own_ref[0, stream]
-    low = low_ref[stream]
-    high = high_ref[stream]
-    return jnp.where(code == 0, own, jnp.where(code == 1, low, high))
-
-
 def round_mul(a, b):
     return (a.astype(F32) * b.astype(F32)).astype(BF16)
 
@@ -118,16 +128,15 @@
 def make_kernel(code_ref, slot_ref, own_ref, low_ref, high_ref, grad_ref, sent_ref):
     code = code_ref[pl.program_id(0)]
 
-    def emit(read):
-        product = round_mul(read(1), read(2))
-        grad_mid = round_mul(grad_ref[...], read(0))
+    def emit(query, product):
+        grad_mid = round_mul(grad_ref[...], query)
         peers, _, chans, toks = sent_ref.shape
         sent_ref[:, 0] = product.T.reshape(peers, chans, toks)
         sent_ref[:, 1] = grad_mid.T.reshape(peers, chans, toks)
 
-    pl.when(code == 0)(lambda: emit(lambda s: own_ref[0, s]))
-    pl.when(code == 1)(lambda: emit(lambda s: low_ref[s]))
-    pl.when(code == 2)(lambda: emit(lambda s: high_ref[s]))
+    pl.when(code == 0)(lambda: emit(own_ref[0, 0], round_mul(own_ref[0, 1], own_ref[0, 2])))
+    pl.when(code == 1)(lambda: emit(low_ref[0], low_ref[1]))
+    pl.when(code == 2)(lambda: emit(high_ref[0], high_ref[1]))
 
 
 def place_of(b, peers):
@@ -139,7 +148,7 @@
 def long_kernel(
     table_ref, got_ref, fwd_ref, bwd_ref, out_ref,
     x_all, z_all, x_tail, z_head, reach, head_end, tail_start,
-    xd, zd, ze, flip_all, flip_head, flip_doc, conv, back, pairs, extra,
+    xd, ze, xe, flip_all, flip_tail, flip_doc, conv, back, pairs, extra,
 ):
     peers = got_ref.shape[0]
     ch = got_ref.shape[2]
@@ -191,11 +200,11 @@
         ends = (lane >= end_from) & (lane < end_at)
         begins = (lane >= start_at) & (lane < start_to)
         x = x_all[pl.ds(at_end, ch), :].astype(F32)
-        z = z_all[pl.ds(at_end, ch), :].astype(F32)
+        x2 = x_all[pl.ds(at_start, ch), :].astype(F32)
         z2 = z_all[pl.ds(at_start, ch), :].astype(F32)
         xd[pl.ds(at, ch), :] = jnp.where(ends, x, 0).astype(BF16)
-        zd[pl.ds(at, ch), :] = jnp.where(ends, z, 0).astype(BF16)
         ze[pl.ds(at, ch), :] = jnp.where(begins, z2, 0).astype(BF16)
+        xe[pl.ds(at, ch), :] = jnp.where(begins, x2, 0).astype(BF16)
         return carry
 
     lax.fori_loop(0, docs, spread_docs, 0)
@@ -208,9 +217,9 @@
 
     def flips(c, carry):
         at = pl.multiple_of(c * step, step)
-        for src, dst in ((z_all, flip_all), (z_head, flip_head), (zd, flip_doc)):
+        for src, skew, dst in ((x_all, 0, flip_all), (x_tail, pad, flip_tail), (xe, 0, flip_doc)):
             dst[:, pl.ds(at, step)] = lax.dot_general(
-                anti, src[pl.ds(at, step), :], (((1,), (1,)), ((), ())),
+                anti, src[pl.ds(at + skew, step), :], (((1,), (1,)), ((), ())),
                 preferred_element_type=F32,
             ).astype(BF16)
         return carry
@@ -234,10 +243,6 @@
         far_part = dot(x_far, fwd_ref[0:far, :])
         far_part = jnp.where(wide < head_end[pl.ds(at, step), :], far_part, 0.0)
         conv[pl.ds(at, step), :] = far_part + dot(xs[-1], fwd_ref[far:, :])
-        pairs[:, 0:far] += dot(flip_head[:, pl.ds(at, step)], x_far)
-        pairs[:, far:] += dot(flip_all[:, pl.ds(at, step)], xs[-1]) + dot(
-            flip_doc[:, pl.ds(at, step)], xd[pl.ds(at, step), :]
-        )
         zs = []
         for delta in range(HOPS + 1):
             z = z_head[pl.ds(at + ch * delta, step), :]
@@ -247,6 +252,10 @@
         far_part = dot(z_far, bwd_ref[BLK:, :])
         far_part = jnp.where(wide >= tail_start[pl.ds(at, step), :], far_part, 0.0)
         back[pl.ds(at, step), :] = far_part + dot(zs[0], bwd_ref[0:BLK, :])
+        pairs[:, BLK:] += dot(flip_tail[:, pl.ds(at, step)], z_far)
+        pairs[:, 0:BLK] += dot(flip_all[:, pl.ds(at, step)], zs[0]) + dot(
+            flip_doc[:, pl.ds(at, step)], ze[pl.ds(at, step), :]
+        )
         return carry
 
     lax.fori_loop(0, steps, chunk, 0)
@@ -282,12 +291,12 @@
     total = jnp.zeros((8, far + 2 * BLK), F32)
     for r in range(BLK // 8):
         band = jnp.concatenate([pairs[8 * r : 8 * (r + 1), :], jnp.zeros((8, BLK), F32)], axis=1)
-        total = total + pltpu.roll(band, 8 * r, 1, stride=1, stride_axis=0)
+        total = total + pltpu.roll(band, 8 * r + 1, 1, stride=1, stride_axis=0)
     lags = jnp.sum(total, axis=0, keepdims=True)
     extra[...] = jnp.zeros_like(extra)
-    count = (far + BLK) // LANES
+    count = TAP_ROWS
     for r in range(count):
-        extra[r : r + 1, :] = lags[:, LANES * r : LANES * (r + 1)]
+        extra[r : r + 1, :] = lags[:, BLK + LANES * r : BLK + LANES * (r + 1)]
     by_channel = jnp.sum(skip, axis=1, keepdims=True)
     e_row = lax.broadcasted_iota(jnp.int32, (ch, LANES), 0)
     e_col = lax.broadcasted_iota(jnp.int32, (ch, LANES), 1)
@@ -303,16 +312,17 @@
 
 
 def finish_kernel(
-    code_ref, slot_ref, own_ref, low_ref, high_ref, grad_ref, gain_ref, got_ref, y_ref, grads_ref
+    code_ref, slot_ref, own_ref, low_ref, high_ref, grad_ref,
+    low_kv_ref, high_kv_ref, gain_ref, got_ref, y_ref, grads_ref,
 ):
     code = code_ref[pl.program_id(0)]
 
-    def emit(read):
+    def emit(query, key_in, value):
         peers, _, chans, toks = got_ref.shape
         width = peers * chans
         conv = got_ref[:, 0].reshape(width, toks).T.astype(F32)
         back = got_ref[:, 1].reshape(width, toks).T.astype(F32)
-        query, key_in, value = (read(s).astype(F32) for s in range(3))
+        query, key_in, value = (a.astype(F32) for a in (query, key_in, value))
         grad = grad_ref[...].astype(F32)
         gain = gain_ref[...]
         product = (key_in * value).astype(BF16).astype(F32)
@@ -324,9 +334,23 @@
         grads_ref[1] = (grad_x * value).astype(BF16)
         grads_ref[2] = (grad_x * key_in).astype(BF16)
 
-    pl.when(code == 0)(lambda: emit(lambda s: own_ref[0, s]))
-    pl.when(code == 1)(lambda: emit(lambda s: low_ref[s]))
-    pl.when(code == 2)(lambda: emit(lambda s: high_ref[s]))
+    pl.when(code == 0)(lambda: emit(own_ref[0, 0], own_ref[0, 1], own_ref[0, 2]))
+    pl.when(code == 1)(lambda: emit(low_ref[0], low_kv_ref[0], low_kv_ref[1]))
+    pl.when(code == 2)(lambda: emit(high_ref[0], high_kv_ref[0], high_kv_ref[1]))
+
+
+def totals_kernel(tap_scale, skip_scale, part_ref, taps_ref, skip_ref):
+    filters, count, lanes = taps_ref.shape
+    peers, _, ch, _ = part_ref.shape
+    group = peers // filters
+    for f in range(filters):
+        part = part_ref[f * group : (f + 1) * group].astype(F32)
+        total = jnp.sum(part, axis=0) * tap_scale
+        taps_ref[f, 0:ch] = total[0]
+        taps_ref[f, ch:] = total[1, 0 : count - ch]
+    side = part_ref[:, 1].astype(F32)
+    at = count - ch
+    skip_ref[...] = (side[:, at, :] + side[:, at + 1, :]) * skip_scale
 
 
 def shifted(array, axis, by):
@@ -344,20 +368,15 @@
     ch = channels // peers
     blocks = 2 * peers
     own = rollout_rows.transpose(0, 2, 1, 3)
-    row_shape = jax.ShapeDtypeStruct((streams, row_len, channels), BF16)
-
-    any_spec = pl.BlockSpec(memory_space=pl.ANY)
-    up, down, code, slot = pl.pallas_call(
+    half_shape = jax.ShapeDtypeStruct((2, row_len, channels), BF16)
+    list_shape = jax.ShapeDtypeStruct((ROWS,), jnp.int32)
+    up, down, up_kv, down_kv, code, slot = pl.pallas_call(
         functools.partial(choose_kernel, peers),
-        out_shape=(
-            row_shape,
-            row_shape,
-            jax.ShapeDtypeStruct((ROWS,), jnp.int32),
-            jax.ShapeDtypeStruct((ROWS,), jnp.int32),
-        ),
-        in_specs=[smem(), smem(), any_spec],
-        out_specs=(any_spec, any_spec, smem(), smem()),
-        scratch_shapes=[pltpu.SemaphoreType.DMA((2,))],
+        out_shape=(half_shape,) * 4 + (list_shape,) * 2,
+        in_specs=[smem(), smem(), pl.BlockSpec(memory_space=pl.ANY)],
+        out_specs=(vmem(),) * 4 + (smem(),) * 2,
+        scratch_shapes=[pltpu.SemaphoreType.DMA((4,))],
+        compiler_params=pltpu.CompilerParams(vmem_limit_bytes=VLIM),
         name="choose",
     )(index[None], pack_targets.T, own)
     low = shifted(up, "ctx", 1)
@@ -382,8 +401,8 @@
             pl.BlockSpec(
                 (1, streams, row_len, channels), lambda o, code, slot: (slot[o], 0, 0, 0)
             ),
-            pl.BlockSpec((streams, row_len, channels), lambda o, code, slot: (0, 0, 0)),
-            pl.BlockSpec((streams, row_len, channels), lambda o, code, slot: (0, 0, 0)),
+            pl.BlockSpec((2, row_len, channels), lambda o, code, slot: (0, 0, 0)),
+            pl.BlockSpec((2, row_len, channels), lambda o, code, slot: (0, 0, 0)),
             pl.BlockSpec((row_len, channels), lambda o, code, slot: (o, 0)),
         ]
 
@@ -400,6 +419,9 @@
         name="products",
     )(code, slot, own, low, high, out_grad)
     got = lax.all_to_all(sent, "ctx", 0, 0, tiled=True)
+    up_kv, down_kv, got = lax.optimization_barrier((up_kv, down_kv, got))
+    low_kv = shifted(up_kv, "ctx", 1)
+    high_kv = shifted(down_kv, "ctx", -1)
 
     rows = blocks * ch
     pad = HOPS * ch
@@ -427,15 +449,37 @@
             VMEM((BLK, BLK * (HOPS + 1)), F32),
             VMEM((2 * ch, LANES), F32),
         ],
-        compiler_params=pltpu.CompilerParams(vmem_limit_bytes=VLIM),
+        compiler_params=pltpu.CompilerParams(vmem_limit_bytes=34 * 1024 * 1024),
+        cost_estimate=pl.CostEstimate(
+            flops=2 * 30 * rows * BLK * BLK, bytes_accessed=7_000_000, transcendentals=0
+        ),
         name="long_filter",
     )(table, got, fwd_band, bwd_band)
+    low_kv, high_kv, reply = lax.optimization_barrier((low_kv, high_kv, reply))
     back = lax.all_to_all(reply, "ctx", 0, 0, tiled=True)
 
-    sums = back[:, :, :, tokens:].astype(F32).reshape(peers, 2 * ch, LANES)
-    count = BLK * (HOPS + 1) // LANES
-    tap_sum = sums[:, :count].reshape(filters, peers // filters, count * LANES).sum(axis=1)
-    skip_total = (sums[:, count, :ch] + sums[:, count + 1, :ch]).reshape(channels)
+    seq_total = tokens * peers
+    chan_total = channels * lax.axis_size("ch")
+    tap_sum, skip_sum = pl.pallas_call(
+        functools.partial(
+            totals_kernel,
+            1.0 / math.sqrt(seq_total * chan_total / filters),
+            1.0 / math.sqrt(seq_total),
+        ),
+        out_shape=(
+            jax.ShapeDtypeStruct((filters, TAP_ROWS, LANES), F32),
+            jax.ShapeDtypeStruct((peers, LANES), F32),
+        ),
+        grid=(1,),
+        in_specs=[
+            pl.BlockSpec((peers, 2, ch, LANES), lambda o: (0, 0, 0, tokens // LANES)),
+        ],
+        out_specs=(
+            pl.BlockSpec((filters, TAP_ROWS, LANES), lambda o: (0, 0, 0)),
+            pl.BlockSpec((peers, LANES), lambda o: (0, 0)),
+        ),
+        name="totals",
+    )(back)
     other = lax.ppermute(tap_sum, "ch", [(0, 1), (1, 0)])
 
     out_y, grads = pl.pallas_call(
@@ -449,6 +493,8 @@
             grid=(ROWS,),
             in_specs=row_specs()
             + [
+                pl.BlockSpec((2, row_len, channels), lambda o, code, slot: (0, 0, 0)),
+                pl.BlockSpec((2, row_len, channels), lambda o, code, slot: (0, 0, 0)),
                 pl.BlockSpec((1, channels), lambda o, code, slot: (0, 0)),
                 pl.BlockSpec((peers, 2, ch, row_len), lambda o, code, slot: (0, 0, 0, o)),
             ],
@@ -459,13 +505,10 @@
         ),
         compiler_params=pltpu.CompilerParams(vmem_limit_bytes=VLIM),
         name="finish",
-    )(code, slot, own, low, high, out_grad, skip_gain[None], back)
-
-    seq_total = tokens * peers
-    chan_total = channels * lax.axis_size("ch")
-    tap_total = (tap_sum + other)[:, ::-1][:, :tap_count]
-    grad_taps = tap_total / math.sqrt(seq_total * chan_total / filters)
-    grad_skip = skip_total / math.sqrt(seq_total)
+    )(code, slot, own, low, high, out_grad, low_kv, high_kv, skip_gain[None], back)
+
+    grad_taps = (tap_sum + other).reshape(filters, TAP_ROWS * LANES)[:, :tap_count]
+    grad_skip = skip_sum[:, :ch].reshape(channels)
     return (out_y, grads.transpose(1, 0, 2), grad_taps, grad_skip)
 
 

time: 200 us -> 149 us (0.74)
  Pallas kernels: 94.1 us -> 46.1 us
  waiting for transfers between devices: 41.9 us -> 36.2 us
  blocking collectives: 39.9 us -> 44.4 us
  other arithmetic: 2.73 us -> 0.62 us
    pallas_call x1 -> x2, Pallas kernels: 50.1 us -> 5.2 us  [the longest x1 3.45 us: on_device(): pl.pallas_call(functools.partial(choose_kernel, peers), out_shape=(half_s...]
    ppermute x2 -> x4, waiting for transfers between devices: 20 us -> 14.4 us  [shifted(): lax.ppermute(array, axis, [(i, (i + by) % length) for i in range(length)])]
    all_to_all x1, blocking collectives: 39.9 us -> 44.4 us  [on_device(): back = lax.all_to_all(reply, 'ctx', 0, 0, tiled=True)]
    pallas_call x1, Pallas kernels: 24.7 us -> 21.4 us  [on_device(): pl.pallas_call(long_kernel, out_shape=jax.ShapeDtypeStruct((peers, 2, ch,...]
    unnamed x11 -> x19, local copies, waits for them, and re-layouts: 3.77 us -> 4.67 us
  transfers between devices with their start and end apart: 4 -> 6, of which waited for: 3 -> 3; matrix products, arithmetic and copies ran while one was open for 1% -> 1% of each run, Pallas kernels for 7% -> 24%
where the time goes in v2:
time: 149 us
  Pallas kernels  46.1 us (31%)
  blocking collectives  44.4 us (30%)
  waiting for transfers between devices  36.2 us (24%)
  starting transfers between devices  14.3 us (10%)
  local copies, waits for them, and re-layouts  6.11 us (4%)
    all_to_all x1, blocking collectives, on_device(): back = lax.all_to_all(reply, 'ctx', 0, 0, tiled=True)  44.4 us
    all_to_all x1, waiting for transfers between devices, on_device(): got = lax.all_to_all(sent, 'ctx', 0, 0, tiled=True)  21.8 us
    pallas_call x1, Pallas kernels, on_device(): pl.pallas_call(long_kernel, out_shape=jax.ShapeDtypeStruct((peers, 2, ch,...  21.4 us
    ppermute x4, waiting for transfers between devices, shifted(): lax.ppermute(array, axis, [(i, (i + by) % length) for i in range(length)])  14.4 us
    all_to_all x1, starting transfers between devices, on_device(): got = lax.all_to_all(sent, 'ctx', 0, 0, tiled=True)  8.26 us
    pallas_call x1, Pallas kernels, on_device(): pl.pallas_call(finish_kernel, out_shape=(jax.ShapeDtypeStruct((tokens, ch...  7.54 us
    pallas_call x1, Pallas kernels, on_device(): pl.pallas_call(functools.partial(tables_kernel, docs), out_shape=(jax.Sha...  6.55 us
    pallas_call x1, Pallas kernels, on_device(): pl.pallas_call(make_kernel, out_shape=jax.ShapeDtypeStruct((peers, 2, ch,...  5.46 us
  transfers between devices with their start and end apart: 6, of which 3 were waited for; matrix products, arithmetic and copies ran while one was open for 1% of the time, Pallas kernels for 24%

profile of v2, /device:TPU:1, one launch (start us, length us, event | category | flops | bytes accessed | tf_op | source)
XLA Modules:
  0.0 148.5 jit_solution(11496114422950705752)
XLA Ops:
  0.6 0.0 copy-start
  0.7 3.5 %choose.1 = (bf16[2,128,1024]{2,1,0:T(8,128)(2,1)}, bf16[2,128,1024]{2,1,0:T(8,128)(2,1)}, bf16[2,128,1024]{2,1,0:T(8,128)(2,1)}, bf16[2,128,1024]{2,1,0:T(8,128)(2,1)}, s32[4]{0:T(128)}, /*index=5*/s32[4]{0:T(128)}) custom-call(s32[1]{0:T(128)} %bitcast.me_ref, s32[2,384]{1,0:T(2,128)} %bitcast.18, bf16[6,3,128,1024]{3,2,1,0:T(8,128)(2,1)} %bitcast.12), custom_call_target="tpu_custom_call" | custom-call | tf_op jit(solution)/shard_map/choose/pallas_call | solution.py:373
  4.1 2.8 %collective-permute-start = (bf16[2,128,1024]{2,1,0:T(8,128)(2,1)}, bf16[2,128,1024]{2,1,0:T(8,128)(2,1)S(1)}, u32[]{:S(2)}, u32[]{:S(2)}) collective-permute-start(bf16[2,128,1024]{2,1,0:T(8,128)(2,1)} %get-tuple-element.25), channel_id=1, source_target_pairs={{0,2},{2,4},{4,6},{6,8},{8,10},{10,12},{12,14},{14,16},{16,18},{18... | collective-permute-start | bytes 1572872 | tf_op jit(solution)/shard_map/ppermute | solution.py:358
  6.9 0.0 collective-permute-start.1
  6.9 12.1 %collective-permute-done.low_ref = bf16[2,128,1024]{2,1,0:T(8,128)(2,1)S(1)} collective-permute-done((bf16[2,128,1024]{2,1,0:T(8,128)(2,1)}, bf16[2,128,1024]{2,1,0:T(8,128)(2,1)S(1)}, u32[]{:S(2)}, u32[]{:S(2)}) %collective-permute-start) | collective-permute-done | bytes 524320 | tf_op jit(solution)/shard_map/ppermute | solution.py:358
  19.0 2.4 %collective-permute-done.1.high_ref = bf16[2,128,1024]{2,1,0:T(8,128)(2,1)S(1)} collective-permute-done((bf16[2,128,1024]{2,1,0:T(8,128)(2,1)}, bf16[2,128,1024]{2,1,0:T(8,128)(2,1)S(1)}, u32[]{:S(2)}, u32[]{:S(2)}) %collective-permute-start.1) | collective-permute-done | bytes 524320 | tf_op jit(solution)/shard_map/ppermute | solution.py:358
  21.4 0.8 copy-done.5
  22.2 5.5 %products.1 = bf16[64,2,16,512]{3,2,1,0:T(8,128)(2,1)} custom-call(s32[4]{0:T(128)} %get-tuple-element.23.code_ref, s32[4]{0:T(128)} %get-tuple-element.24.slot_ref, bf16[6,3,128,1024]{3,2,1,0:T(8,128)(2,1)} %bitcast.13, bf16[2,128,1024]{2,1,0:T(8,128)(2,1)} %copy-done.4, bf16[2,128,1024]{2,1,0:T(8,128)(2,1)} %copy-done.5, bf16[512,1024]{1,0:T(8,128)(2,1)} %grad_ref.3), custom_call_target="tpu_custom_call" | custom-call | tf_op jit(solution)/shard_map/products/pallas_call | solution.py:409
  27.6 8.3 %all-to-all-start = ((bf16[64,2,16,512]{3,2,1,0:T(8,128)(2,1)}), bf16[64,2,16,512]{3,2,1,0:T(8,128)(2,1)S(1)}, u32[]{:S(2)}, u32[]{:S(2)}) async-start(bf16[64,2,16,512]{3,2,1,0:T(8,128)(2,1)} %products.1), calls=%async_computation | async-start | bytes 4194304 | tf_op jit(solution)/shard_map/all_to_all | solution.py:421
  35.9 0.6 pad_convert_fusion.taps_ref
  36.6 6.6 %tables.1 = (s32[8,128]{1,0:T(8,128)}, bf16[2304,256]{1,0:T(8,128)(2,1)}, bf16[2304,256]{1,0:T(8,128)(2,1)}) custom-call(s32[128]{0:T(128)} %length_ref.1, f32[1,2560]{1,0:T(1,128)} %pad_convert_fusion.taps_ref), custom_call_target="tpu_custom_call" | custom-call | bytes 20000000 | tf_op jit(solution)/shard_map/tables/pallas_call | solution.py:389
  43.1 21.8 %all-to-all-done.got_ref = bf16[64,2,16,512]{3,2,1,0:T(8,128)(2,1)S(1)} async-done(((bf16[64,2,16,512]{3,2,1,0:T(8,128)(2,1)}), bf16[64,2,16,512]{3,2,1,0:T(8,128)(2,1)S(1)}, u32[]{:S(2)}, u32[]{:S(2)}) %all-to-all-start) | async-done | bytes 2097184 | tf_op jit(solution)/shard_map/all_to_all | solution.py:421
  64.9 0.6 collective-permute-start.2
  65.5 0.0 collective-permute-start.3
  65.5 1.3 copy-done.1
  66.7 1.3 copy-done.2
  68.0 0.7 copy-done.3
  68.7 21.4 %long_filter.1 = bf16[64,2,16,640]{3,2,1,0:T(8,128)(2,1)S(1)} custom-call(s32[8,128]{1,0:T(8,128)S(1)} %copy-done.3, bf16[64,2,16,512]{3,2,1,0:T(8,128)(2,1)S(1)} %all-to-all-done.got_ref, bf16[2304,256]{1,0:T(8,128)(2,1)S(1)} %copy-done.1, bf16[2304,256]{1,0:T(8,128)(2,1)S(1)} %copy-done.2), custom_call_target="tpu_custom_call" | custom-call | flops 8053063680 | bytes 7000000 | tf_op jit(solution)/shard_map/long_filter/pallas_call | solution.py:428
  90.1 44.4 %all_to_all.10.got_ref.part_ref = bf16[64,2,16,640]{3,2,1,0:T(8,128)(2,1)} all-to-all(bf16[64,2,16,640]{3,2,1,0:T(8,128)(2,1)S(1)} %long_filter.1), channel_id=1, replica_groups=mesh['ctx'=64,'ch'=2] {'ctx'}, dimensions={0} | all-to-all | bytes 5242880 | tf_op jit(solution)/shard_map/all_to_all | solution.py:459
  134.5 1.8 %totals.1 = (f32[4,17,128]{2,1,0:T(8,128)}, f32[64,128]{1,0:T(8,128)}) custom-call(bf16[64,2,16,640]{3,2,1,0:T(8,128)(2,1)} %all_to_all.10.got_ref.part_ref), custom_call_target="tpu_custom_call" | custom-call | tf_op jit(solution)/shard_map/totals/pallas_call | solution.py:463
  136.3 2.6 %collective-permute-start.4 = (f32[4,17,128]{2,1,0:T(8,128)}, f32[4,17,128]{2,1,0:T(8,128)S(1)}, u32[]{:S(2)}, u32[]{:S(2)}) collective-permute-start(f32[4,17,128]{2,1,0:T(8,128)} %get-tuple-element.40), channel_id=1, source_target_pairs={{0,1},{1,0},{2,3},{3,2},{4,5},{5,4},{6,7},{7,6},{8,9},{9,8},{10,11... | collective-permute-start | bytes 104456 | tf_op jit(solution)/shard_map/ppermute | solution.py:483
  138.9 1.4 reshape.15
  140.3 7.5 %finish.1 = (bf16[512,1024]{1,0:T(8,128)(2,1)}, bf16[3,512,1024]{2,1,0:T(8,128)(2,1)}) custom-call(s32[4]{0:T(128)} %get-tuple-element.23.code_ref, s32[4]{0:T(128)} %get-tuple-element.24.slot_ref, bf16[6,3,128,1024]{3,2,1,0:T(8,128)(2,1)} %bitcast.14, bf16[2,128,1024]{2,1,0:T(8,128)(2,1)} %copy-done.4, bf16[2,128,1024]{2,1,0:T(8,128)(2,1)} %copy-done.5, ...), custom_call_target="tpu_custom_call" | custom-call | tf_op jit(solution)/shard_map/finish/pallas_call | solution.py:485
  147.9 0.6 copy.12
  (18 shorter events, 0.1 us)
Async XLA Ops:
  0.6 35.3 %copy-start = (f32[4,2049]{1,0:T(4,128)S(1)}, f32[4,2049]{1,0:T(4,128)}, u32[]{:S(2)}) copy-start(f32[4,2049]{1,0:T(4,128)} %param.9) | copy-start | bytes 98356
  4.1 14.9 %collective-permute-start = (bf16[2,128,1024]{2,1,0:T(8,128)(2,1)}, bf16[2,128,1024]{2,1,0:T(8,128)(2,1)S(1)}, u32[]{:S(2)}, u32[]{:S(2)}) collective-permute-start(bf16[2,128,1024]{2,1,0:T(8,128)(2,1)} %get-tuple-element.25), channel_id=1, source_target_pairs={{0,2},{2,4},{4,6},{6,8},{8,10},{10,12},{12,14},{14,16},{16,18},{18... | collective-permute-start | bytes 1572872 | tf_op jit(solution)/shard_map/ppermute | solution.py:358
  6.9 14.4 %collective-permute-start.1 = (bf16[2,128,1024]{2,1,0:T(8,128)(2,1)}, bf16[2,128,1024]{2,1,0:T(8,128)(2,1)S(1)}, u32[]{:S(2)}, u32[]{:S(2)}) collective-permute-start(bf16[2,128,1024]{2,1,0:T(8,128)(2,1)} %get-tuple-element.26), channel_id=1, source_target_pairs={{0,126},{2,0},{4,2},{6,4},{8,6},{10,8},{12,10},{14,12},{16,14},{18... | collective-permute-start | bytes 1572872 | tf_op jit(solution)/shard_map/ppermute | solution.py:358
  19.0 2.4 %copy-start.4 = (bf16[2,128,1024]{2,1,0:T(8,128)(2,1)}, bf16[2,128,1024]{2,1,0:T(8,128)(2,1)S(1)}, u32[]{:S(2)}) copy-start(bf16[2,128,1024]{2,1,0:T(8,128)(2,1)S(1)} %collective-permute-done.low_ref) | copy-start | bytes 1572868
  21.4 0.8 copy-start.5
  27.6 37.3 %all-to-all-start = ((bf16[64,2,16,512]{3,2,1,0:T(8,128)(2,1)}), bf16[64,2,16,512]{3,2,1,0:T(8,128)(2,1)S(1)}, u32[]{:S(2)}, u32[]{:S(2)}) async-start(bf16[64,2,16,512]{3,2,1,0:T(8,128)(2,1)} %products.1), calls=%async_computation | async-start | bytes 4194304 | tf_op jit(solution)/shard_map/all_to_all | solution.py:421
  64.9 25.2 %collective-permute-start.2 = (bf16[2,128,1024]{2,1,0:T(8,128)(2,1)}, bf16[2,128,1024]{2,1,0:T(8,128)(2,1)S(1)}, u32[]{:S(2)}, u32[]{:S(2)}) collective-permute-start(bf16[2,128,1024]{2,1,0:T(8,128)(2,1)} %get-tuple-element.29), channel_id=1, source_target_pairs={{0,2},{2,4},{4,6},{6,8},{8,10},{10,12},{12,14},{14,16},{16,18},{18... | collective-permute-start | bytes 1572872 | tf_op jit(solution)/shard_map/ppermute | solution.py:358
  65.5 24.6 %collective-permute-start.3 = (bf16[2,128,1024]{2,1,0:T(8,128)(2,1)}, bf16[2,128,1024]{2,1,0:T(8,128)(2,1)S(1)}, u32[]{:S(2)}, u32[]{:S(2)}) collective-permute-start(bf16[2,128,1024]{2,1,0:T(8,128)(2,1)} %get-tuple-element.30), channel_id=1, source_target_pairs={{0,126},{2,0},{4,2},{6,4},{8,6},{10,8},{12,10},{14,12},{16,14},{18... | collective-permute-start | bytes 1572872 | tf_op jit(solution)/shard_map/ppermute | solution.py:358
  65.5 1.3 copy-start.1
  66.7 1.3 copy-start.2
  68.0 0.7 copy-start.3
  90.1 44.5 %copy-start.6 = (bf16[2,128,1024]{2,1,0:T(8,128)(2,1)}, bf16[2,128,1024]{2,1,0:T(8,128)(2,1)S(1)}, u32[]{:S(2)}) copy-start(bf16[2,128,1024]{2,1,0:T(8,128)(2,1)S(1)} %collective-permute-done.2.low_kv_ref) | copy-start | bytes 1572868
  90.1 44.4 %copy-start.7 = (bf16[2,128,1024]{2,1,0:T(8,128)(2,1)}, bf16[2,128,1024]{2,1,0:T(8,128)(2,1)S(1)}, u32[]{:S(2)}) copy-start(bf16[2,128,1024]{2,1,0:T(8,128)(2,1)S(1)} %collective-permute-done.3.high_kv_ref) | copy-start | bytes 1572868
  136.3 11.6 %collective-permute-start.4 = (f32[4,17,128]{2,1,0:T(8,128)}, f32[4,17,128]{2,1,0:T(8,128)S(1)}, u32[]{:S(2)}, u32[]{:S(2)}) collective-permute-start(f32[4,17,128]{2,1,0:T(8,128)} %get-tuple-element.40), channel_id=1, source_target_pairs={{0,1},{1,0},{2,3},{3,2},{4,5},{5,4},{6,7},{7,6},{8,9},{9,8},{10,11... | collective-permute-start | bytes 104456 | tf_op jit(solution)/shard_map/ppermute | solution.py:483
  140.3 7.5 %copy-start.8 = (f32[4,17,128]{2,1,0:T(8,128)S(1)}, f32[4,17,128]{2,1,0:T(8,128)}, u32[]{:S(2)}) copy-start(f32[4,17,128]{2,1,0:T(8,128)} %get-tuple-element.40) | copy-start | bytes 104452

commit v3 on v2

v3 whole, which is shorter than its diff:
```python
import functools
import math

import jax
import jax.numpy as jnp
from jax import lax
from jax.experimental import pallas as pl
from jax.experimental.pallas import tpu as pltpu
from jax.sharding import PartitionSpec as P

BF16 = jnp.bfloat16
F32 = jnp.float32
SMEM = pltpu.SMEM
VMEM = pltpu.VMEM

BLK = 256
HOPS = 8
SLOTS = 6
ROWS = 4
LANES = 128
WIDE = 256
GROUP = 32
TAP_ROWS = 17
VLIM = 56 * 1024 * 1024


def hbm():
    return pl.BlockSpec(memory_space=pltpu.HBM)


def smem():
    return pl.BlockSpec(memory_space=SMEM)


def vmem():
    return pl.BlockSpec(memory_space=VMEM)


def choose_kernel(
    cycle, me_ref, target_ref, own_ref, up_ref, down_ref, up_kv_ref, down_kv_ref,
    code_ref, slot_ref, sems,
):
    me = me_ref[0]
    below = lax.rem(me + cycle - 1, cycle)
    above = lax.rem(me + 1, cycle)
    up_slot = jnp.int32(0)
    down_slot = jnp.int32(0)
    for k in range(SLOTS):
        shard = target_ref[0, me * SLOTS + k]
        up_slot = jnp.where(shard == above, k, up_slot)
        down_slot = jnp.where(shard == below, k, down_slot)
    copies = []
    for n, (slot, first, later) in enumerate(
        ((up_slot, up_ref, up_kv_ref), (down_slot, down_ref, down_kv_ref))
    ):
        copies.append(
            (
                pltpu.make_async_copy(own_ref.at[slot, 0], first.at[0], sems.at[2 * n]),
                pltpu.make_async_copy(own_ref.at[slot, pl.ds(1, 2)], later, sems.at[2 * n + 1]),
            )
        )
    for one, two in copies:
        two.start()
        one.start()
    for o in range(ROWS):
        code_ref[o] = 0
        slot_ref[o] = 0
    for k in range(SLOTS):
        shard = target_ref[0, me * SLOTS + k]
        offset = target_ref[1, me * SLOTS + k]

        @pl.when(shard == me)
        def _():
            slot_ref[offset] = k

        for owner, code in ((below, 1), (above, 2)):
            their_shard = target_ref[0, owner * SLOTS + k]
            their_offset = target_ref[1, owner * SLOTS + k]

            @pl.when(their_shard == me)
            def _():
                code_ref[their_offset] = code

    for (one, two), first, later in zip(copies, (up_ref, down_ref), (up_kv_ref, down_kv_ref)):
        two.wait()
        first[1] = round_mul(later[0], later[1])
        one.wait()


def tables_kernel(docs, length_ref, table_ref, count_ref):
    def one_doc(d, start):
        end = start + length_ref[d]
        table_ref[3, d] = start
        table_ref[4, d] = end

        def heads(b, carry):
            table_ref[0, b] = b - lax.shift_right_logical(start, 8)
            table_ref[1, b] = jnp.minimum(end - BLK * b, BLK)
            return carry

        def tails(b, carry):
            table_ref[2, b] = jnp.maximum(start - BLK * b, 0)
            return carry

        lax.fori_loop(
            lax.shift_right_logical(start + BLK - 1, 8),
            lax.shift_right_logical(end + BLK - 1, 8),
            heads,
            0,
        )
        lax.fori_loop(
            lax.shift_right_logical(start, 8), lax.shift_right_logical(end, 8), tails, 0
        )
        return end

    lax.fori_loop(0, docs, one_doc, jnp.int32(0))

    for n in range(HOPS + 1):
        count_ref[n] = 0

    def count(b, carry):
        reach = table_ref[0, b]
        count_ref[reach] = count_ref[reach] + 1
        return carry

    lax.fori_loop(0, docs, count, 0)
    before = jnp.int32(0)
    for n in range(HOPS, -1, -1):
        these = count_ref[n]
        count_ref[n] = before
        before = before + these

    def place(b, carry):
        reach = table_ref[0, b]
        at = count_ref[reach]
        count_ref[reach] = at + 1
        table_ref[5, at] = b
        table_ref[6, b] = at
        table_ref[7, at] = reach
        return carry

    lax.fori_loop(0, docs, place, 0)


def make_bands(taps_ref, fwd_ref, bwd_ref):
    width = BLK * (HOPS + 2)
    part = 32
    for r in range(BLK // part):
        rows = jnp.broadcast_to(taps_ref[...], (part, width))
        rows = pltpu.roll(rows, part * r, 1, stride=1, stride_axis=0)
        for delta in range(HOPS + 1):
            at = BLK * (HOPS - delta) + part * r
            fwd_ref[at : at + part, :] = rows[:, BLK * (delta + 1) : BLK * (delta + 2)].astype(BF16)
    for delta in range(HOPS + 1):
        at = BLK * (HOPS - delta)
        bwd_ref[BLK * delta : BLK * (delta + 1), :] = fwd_ref[at : at + BLK, :].T


def round_mul(a, b):
    return (a.astype(F32) * b.astype(F32)).astype(BF16)


def write_row(sent_ref, lane, toks, read_product, read_grad_mid):
    peers, _, chans, _ = sent_ref.shape
    together = WIDE // chans
    for n in range(peers // together):
        lanes = slice(n * WIDE, (n + 1) * WIDE)
        to = slice(n * together, (n + 1) * together)
        for side, read in enumerate((read_product, read_grad_mid)):
            sent_ref[to, side, :, lane : lane + toks] = read(lanes).T.reshape(together, chans, toks)


def own_kernel(code_ref, slot_ref, own_ref, grad_ref, sent_ref, row, grad, sems):
    toks = row.shape[2]

    def copies(o):
        return (
            pltpu.make_async_copy(own_ref.at[slot_ref[o]], row.at[o], sems.at[o]),
            pltpu.make_async_copy(
                grad_ref.at[pl.ds(o * toks, toks)], grad.at[o], sems.at[ROWS + o]
            ),
        )

    for o in range(ROWS):
        for copy in copies(o):
            copy.start()
    for o in range(ROWS):
        for copy in copies(o):
            copy.wait()

        @pl.when(code_ref[o] == 0)
        def _():
            write_row(
                sent_ref,
                o * toks,
                toks,
                lambda c: round_mul(row[o, 1, :, c], row[o, 2, :, c]),
                lambda c: round_mul(grad[o, :, c], row[o, 0, :, c]),
            )


def guest_kernel(code_ref, low_ref, high_ref, grad_ref, part_ref, sent_ref, grad, ready, sems):
    del part_ref
    toks = low_ref.shape[1]
    guests = []
    for n, ref in enumerate((low_ref, high_ref)):
        at = jnp.int32(0)
        for o in range(ROWS):
            at = jnp.where(code_ref[o] == n + 1, o + 1, at)
        here = pl.ds(pl.multiple_of(jnp.maximum(at - 1, 0) * toks, toks), toks)
        copy_in = pltpu.make_async_copy(grad_ref.at[here], grad.at[n], sems.at[n])
        copy_out = pltpu.make_async_copy(
            ready.at[n], sent_ref.at[:, :, :, here], sems.at[2 + n]
        )
        guests.append((n, ref, at > 0, copy_in, copy_out))
    for n, ref, live, copy_in, copy_out in guests:
        pl.when(live)(copy_in.start)
    for n, ref, live, copy_in, copy_out in guests:

        @pl.when(live)
        def _():
            copy_in.wait()
            write_row(
                ready.at[n],
                0,
                toks,
                lambda c: ref[1, :, c],
                lambda c: round_mul(grad[n, :, c], ref[0, :, c]),
            )
            copy_out.start()

    for n, ref, live, copy_in, copy_out in guests:
        pl.when(live)(copy_out.wait)


def place_of(b, peers):
    src = jnp.where(b < peers, b, 2 * peers - 1 - b)
    lane = pl.multiple_of(jnp.where(b < peers, 0, BLK), BLK)
    return src, lane


def dot(a, b):
    return jnp.dot(a, b, preferred_element_type=F32)


def long_kernel(
    me_ref, table_ref, got_ref, taps_ref, out_ref,
    fwd_ref, bwd_ref, x_all, z_all, x_tail, z_head, xd, zd, ze, turned, doc_near, doc_back,
    near, far_sum, back_near, back_far, pairs, extra,
):
    peers = got_ref.shape[0]
    ch = got_ref.shape[2]
    blocks = 2 * peers
    docs = blocks
    rows = blocks * ch
    pad = HOPS * ch
    far = HOPS * BLK
    lane = lax.broadcasted_iota(jnp.int32, (ch, BLK), 1)

    make_bands(taps_ref, fwd_ref, bwd_ref)
    x_tail[0:pad, :] = jnp.zeros((pad, BLK), BF16)
    back_far[...] = jnp.zeros_like(back_far)
    far_sum[...] = jnp.zeros_like(far_sum)
    pairs[...] = jnp.zeros_like(pairs)

    def spread(k, total):
        b = table_ref[5, k]
        src, at_lane = place_of(b, peers)
        at = pl.multiple_of(b * ch, ch)
        x = got_ref[src, 0, :, pl.ds(at_lane, BLK)]
        z = got_ref[src, 1, :, pl.ds(at_lane, BLK)]
        x_all[pl.ds(at, ch), :] = x
        z_all[pl.ds(at, ch), :] = z
        end, tail = table_ref[1, b], table_ref[2, b]
        x_f, z_f = x.astype(F32), z.astype(F32)
        x_tail[pl.ds(at + pad, ch), :] = jnp.where(lane >= tail, x_f, 0).astype(BF16)
        z_head[pl.ds(pl.multiple_of(k * ch, ch), ch), :] = jnp.where(lane < end, z_f, 0).astype(BF16)
        return total + x_f * z_f

    skip = lax.fori_loop(0, blocks, spread, jnp.zeros((ch, BLK), F32), unroll=4)

    def doc_parts(d):
        start, end = table_ref[3, d], table_ref[4, d]
        end_block = lax.shift_right_logical(end - 1, 8)
        end_at = jnp.bitwise_and(end, BLK - 1)
        end_from = jnp.maximum(start - BLK * end_block, 0)
        start_block = lax.shift_right_logical(start, 8)
        start_at = jnp.bitwise_and(start, BLK - 1)
        start_at = jnp.where(start_at == 0, BLK, start_at)
        start_to = end - BLK * start_block
        return end_block, end_from, end_at, start_block, start_at, start_to

    def spread_docs(d, carry):
        end_block, end_from, end_at, start_block, start_at, start_to = doc_parts(d)
        at = pl.multiple_of(d * ch, ch)
        at_end = pl.multiple_of(end_block * ch, ch)
        at_start = pl.multiple_of(start_block * ch, ch)
        ends = (lane >= end_from) & (lane < end_at)
        begins = (lane >= start_at) & (lane < start_to)
        x = x_all[pl.ds(at_end, ch), :].astype(F32)
        z = z_all[pl.ds(at_end, ch), :].astype(F32)
        z2 = z_all[pl.ds(at_start, ch), :].astype(F32)
        xd[pl.ds(at, ch), :] = jnp.where(ends, x, 0).astype(BF16)
        zd[pl.ds(at, ch), :] = jnp.where(ends, z, 0).astype(BF16)
        ze[pl.ds(at, ch), :] = jnp.where(begins, z2, 0).astype(BF16)
        return carry

    lax.fori_loop(0, docs, spread_docs, 0, unroll=4)

    step = 256
    first_fwd = fwd_ref.at[far : far + BLK, :]
    first_bwd = bwd_ref.at[0:BLK, :]

    def inner(c, carry):
        at = pl.multiple_of(c * step, step)
        here = pl.ds(at, step)
        z = z_head[here, :]
        x = jnp.concatenate([x_tail[pl.ds(at + pad, step), :], xd[here, :]], axis=0)
        ahead = dot(x, first_fwd[...])
        near[here, :] = ahead[:step]
        doc_near[here, :] = ahead[step:]
        behind = dot(jnp.concatenate([z, ze[here, :]], axis=0), first_bwd[...])
        back_near[here, :] = behind[:step]
        doc_back[here, :] = behind[step:]
        turned[:, here] = z.T
        pairs[:, far:] += dot(jnp.concatenate([z_all[here, :].T, zd[here, :].T], axis=1), x)
        return carry

    lax.fori_loop(0, rows // step, inner, 0)

    def add_docs(d, carry):
        end_block, end_from, end_at, start_block, start_at, start_to = doc_parts(d)
        here = pl.ds(pl.multiple_of(d * ch, ch), ch)
        at_end = pl.multiple_of(end_block * ch, ch)
        at_start = pl.multiple_of(table_ref[6, start_block] * ch, ch)
        near[pl.ds(at_end, ch), :] += jnp.where(lane < end_at, doc_near[here, :], 0.0)
        back_near[pl.ds(at_start, ch), :] += jnp.where(lane >= start_at, doc_back[here, :], 0.0)
        return carry

    lax.fori_loop(0, docs, add_docs, 0, unroll=4)

    wide = GROUP * ch
    zero = jnp.zeros((), BF16)

    def outer(c, carry):
        at = pl.multiple_of(c * wide, wide)
        here = pl.ds(at, wide)

        def one_lag(delta, carry):
            tiles, targets, live = [], [], []
            for i in range(GROUP):
                k = c * GROUP + i
                target = pl.multiple_of((table_ref[5, k] + HOPS - delta) * ch, ch)
                inside = table_ref[7, k] >= delta
                tiles.append(jnp.where(inside, x_tail[pl.ds(target, ch), :], zero))
                targets.append(target)
                live.append(inside)
            x = jnp.concatenate(tiles, axis=0)
            fwd_at = pl.multiple_of((HOPS - delta) * BLK, BLK)
            bwd_at = pl.multiple_of(delta * BLK, BLK)
            far_sum[here, :] += dot(x, fwd_ref[pl.ds(fwd_at, BLK), :])
            pairs[:, pl.ds(fwd_at, BLK)] += dot(turned[:, here], x)
            y = dot(z_head[here, :], bwd_ref[pl.ds(bwd_at, BLK), :])
            for i in range(GROUP):
                back_far[pl.ds(targets[i], ch), :] += jnp.where(
                    live[i], y[i * ch : (i + 1) * ch], 0.0
                )
            return carry

        lax.fori_loop(1, table_ref[7, c * GROUP] + 1, one_lag, 0)
        return carry

    lax.fori_loop(0, blocks // GROUP, outer, 0)

    def gather_out(k, carry):
        b = table_ref[5, k]
        src, at_lane = place_of(b, peers)
        here = pl.ds(pl.multiple_of(k * ch, ch), ch)
        at = pl.multiple_of(b * ch, ch)
        ahead = jnp.where(lane < table_ref[1, b], far_sum[here, :], 0.0)
        behind = jnp.where(lane >= table_ref[2, b], back_far[pl.ds(at + pad, ch), :], 0.0)
        out_ref[src, 0, :, pl.ds(at_lane, BLK)] = (near[pl.ds(at, ch), :] + ahead).astype(BF16)
        out_ref[src, 1, :, pl.ds(at_lane, BLK)] = (back_near[here, :] + behind).astype(BF16)
        return carry

    lax.fori_loop(0, blocks, gather_out, 0, unroll=4)

    total = jnp.zeros((8, far + 2 * BLK), F32)
    for r in range(BLK // 8):
        band = jnp.concatenate([pairs[8 * r : 8 * (r + 1), :], jnp.zeros((8, BLK), F32)], axis=1)
        total = total + pltpu.roll(band, BLK - 8 - 8 * r, 1)
    lags = total[7:8]
    for r in range(7):
        lags = lags + pltpu.roll(total[r : r + 1], 7 - r, 1)
    extra[...] = jnp.zeros_like(extra)
    count = TAP_ROWS
    for r in range(count):
        at = far + BLK - LANES * (r + 1)
        extra[r : r + 1, :] = lags[:, at : at + LANES]
    r_id = lax.broadcasted_iota(jnp.int32, (LANES, LANES), 0)
    c_id = lax.broadcasted_iota(jnp.int32, (LANES, LANES), 1)
    anti = jnp.where(r_id + c_id == LANES - 1, 1.0, 0.0).astype(BF16)
    extra[...] = dot(extra[...].astype(BF16), anti)

    by_channel = jnp.sum(skip, axis=1, keepdims=True)
    e_row = lax.broadcasted_iota(jnp.int32, (ch, LANES), 0)
    e_col = lax.broadcasted_iota(jnp.int32, (ch, LANES), 1)
    mine = e_row + ch * lax.rem(me_ref[0], LANES // ch) == e_col
    skip_row = jnp.sum(jnp.where(mine, by_channel, 0.0), axis=0, keepdims=True)
    high = skip_row.astype(BF16).astype(F32)
    extra[count : count + 1, :] = high
    extra[count + 1 : count + 2, :] = skip_row - high
    packed = extra[...].astype(BF16)
    for side in range(2):
        out_ref[:, side, :, 2 * BLK : 2 * BLK + LANES] = jnp.broadcast_to(
            packed[side * ch : (side + 1) * ch][None], (peers, ch, LANES)
        )


def finish_kernel(
    code_ref, slot_ref, gain_ref, own_ref, low_ref, high_ref, grad_ref,
    low_kv_ref, high_kv_ref, got_ref, y_ref, grads_ref,
    row, grad, got, y_row, grads_row, in_sems, out_sems,
):
    _, peers, _, chans, toks = got.shape

    def here(o):
        return pl.ds(o * toks, toks)

    def fetch(o, act):
        code = code_ref[o]

        @pl.when(code == 0)
        def _():
            act(pltpu.make_async_copy(own_ref.at[slot_ref[o]], row.at[o], in_sems.at[o, 0]))

        for n, first, later in ((1, low_ref, low_kv_ref), (2, high_ref, high_kv_ref)):

            @pl.when(code == n)
            def _():
                act(pltpu.make_async_copy(first.at[0], row.at[o, 0], in_sems.at[o, 0]))
                act(pltpu.make_async_copy(later, row.at[o, pl.ds(1, 2)], in_sems.at[o, 1]))

        act(pltpu.make_async_copy(grad_ref.at[here(o)], grad.at[o], in_sems.at[o, 2]))
        act(pltpu.make_async_copy(got_ref.at[:, :, :, here(o)], got.at[o], in_sems.at[o, 3]))

    def results(o, act):
        act(pltpu.make_async_copy(y_row.at[o], y_ref.at[here(o)], out_sems.at[o, 0]))
        for n in range(3):
            act(
                pltpu.make_async_copy(
                    grads_row.at[o, n], grads_ref.at[n, here(o)], out_sems.at[o, 1 + n]
                )
            )

    together = WIDE // chans
    for o in range(ROWS):
        fetch(o, lambda copy: copy.start())
    for o in range(ROWS):
        fetch(o, lambda copy: copy.wait())
        for n in range(peers // together):
            lanes = slice(n * WIDE, (n + 1) * WIDE)
            of = slice(n * together, (n + 1) * together)
            conv = got[o, of, 0].reshape(WIDE, toks).T.astype(F32)
            back = got[o, of, 1].reshape(WIDE, toks).T.astype(F32)
            query, key_in, value = (row[o, s, :, lanes].astype(F32) for s in range(3))
            out_grad = grad[o, :, lanes].astype(F32)
            gain = gain_ref[:, lanes]
            product = (key_in * value).astype(BF16).astype(F32)
            grad_mid = (out_grad * query).astype(BF16).astype(F32)
            mixed = conv + gain * product
            grad_x = back + gain * grad_mid
            y_row[o, :, lanes] = (query * mixed).astype(BF16)
            grads_row[o, 0, :, lanes] = (out_grad * mixed).astype(BF16)
            grads_row[o, 1, :, lanes] = (grad_x * value).astype(BF16)
            grads_row[o, 2, :, lanes] = (grad_x * key_in).astype(BF16)
        results(o, lambda copy: copy.start())
    for o in range(ROWS):
        results(o, lambda copy: copy.wait())


def totals_kernel(tap_scale, skip_scale, part_ref, taps_ref, skip_ref):
    filters = taps_ref.shape[0]
    peers, _, ch, lanes = part_ref.shape
    group = peers // filters
    for f in range(filters):
        part = part_ref[f * group : (f + 1) * group].astype(F32)
        total = jnp.sum(part, axis=0) * tap_scale
        for r in range(TAP_ROWS):
            row = total[r // ch, r % ch : r % ch + 1]
            taps_ref[f : f + 1, r * lanes : (r + 1) * lanes] = row
    at = TAP_ROWS - ch
    together = lanes // ch
    for r in range(peers // together):
        part = part_ref[r * together : (r + 1) * together, 1, :, :].astype(F32)
        total = jnp.sum(part, axis=0) * skip_scale
        skip_ref[r : r + 1, :] = total[at : at + 1] + total[at + 1 : at + 2]


def shifted(array, axis, by):
    length = lax.axis_size(axis)
    return lax.ppermute(array, axis, [(i, (i + by) % length) for i in range(length)])


def on_device(rollout_rows, pack_targets, doc_lengths, filter_taps, skip_gain, out_grad):
    peers = lax.axis_size("ctx")
    index = lax.axis_index("ctx").astype(jnp.int32)
    slots, row_len, streams, channels = rollout_rows.shape
    tokens = out_grad.shape[0]
    filters, tap_count = filter_taps.shape
    docs = doc_lengths.shape[0]
    ch = channels // peers
    blocks = 2 * peers
    own = rollout_rows.transpose(0, 2, 1, 3)
    half_shape = jax.ShapeDtypeStruct((2, row_len, channels), BF16)
    list_shape = jax.ShapeDtypeStruct((ROWS,), jnp.int32)
    up, down, up_kv, down_kv, code, slot = pl.pallas_call(
        functools.partial(choose_kernel, peers),
        out_shape=(half_shape,) * 4 + (list_shape,) * 2,
        in_specs=[smem(), smem(), hbm()],
        out_specs=(vmem(),) * 4 + (smem(),) * 2,
        scratch_shapes=[pltpu.SemaphoreType.DMA((4,))],
        compiler_params=pltpu.CompilerParams(vmem_limit_bytes=VLIM),
        name="choose",
    )(index[None], pack_targets.T, own)
    low = shifted(up, "ctx", 1)
    high = shifted(down, "ctx", -1)

    mine = lax.dynamic_index_in_dim(filter_taps, index // (peers // filters), 0, keepdims=True)
    mine = mine.astype(BF16).astype(F32)
    mine = jnp.pad(mine, [(0, 0), (BLK, BLK * (HOPS + 1) - tap_count)])
    table = pl.pallas_call(
        functools.partial(tables_kernel, docs),
        out_shape=jax.ShapeDtypeStruct((8, docs), jnp.int32),
        in_specs=[smem()],
        out_specs=smem(),
        scratch_shapes=[SMEM((HOPS + 1,), jnp.int32)],
        compiler_params=pltpu.CompilerParams(vmem_limit_bytes=4 * 1024 * 1024),
        cost_estimate=pl.CostEstimate(flops=0, bytes_accessed=20_000_000, transcendentals=0),
        name="tables",
    )(doc_lengths)

    sent_shape = jax.ShapeDtypeStruct((peers, 2, ch, tokens), BF16)
    row_buffers = [
        VMEM((ROWS, streams, row_len, channels), BF16),
        VMEM((ROWS, row_len, channels), BF16),
    ]
    part = pl.pallas_call(
        own_kernel,
        out_shape=sent_shape,
        in_specs=[smem(), smem(), hbm(), hbm()],
        out_specs=vmem(),
        scratch_shapes=row_buffers + [pltpu.SemaphoreType.DMA((2 * ROWS,))],
        compiler_params=pltpu.CompilerParams(vmem_limit_bytes=VLIM),
        cost_estimate=pl.CostEstimate(flops=0, bytes_accessed=20_000_000, transcendentals=0),
        name="own_products",
    )(code, slot, own, out_grad)
    sent = pl.pallas_call(
        guest_kernel,
        out_shape=sent_shape,
        in_specs=[smem(), vmem(), vmem(), hbm(), hbm()],
        out_specs=hbm(),
        scratch_shapes=[
            VMEM((2, row_len, channels), BF16),
            VMEM((2, peers, 2, ch, row_len), BF16),
            pltpu.SemaphoreType.DMA((4,)),
        ],
        input_output_aliases={4: 0},
        compiler_params=pltpu.CompilerParams(vmem_limit_bytes=VLIM),
        name="guest_products",
    )(code, low, high, out_grad, part)
    got = lax.all_to_all(sent, "ctx", 0, 0, tiled=True)
    up_kv, down_kv, got = lax.optimization_barrier((up_kv, down_kv, got))
    low_kv = shifted(up_kv, "ctx", 1)
    high_kv = shifted(down_kv, "ctx", -1)

    rows = blocks * ch
    pad = HOPS * ch
    reply = pl.pallas_call(
        long_kernel,
        out_shape=jax.ShapeDtypeStruct((peers, 2, ch, tokens + LANES), BF16),
        in_specs=[smem(), smem(), vmem(), vmem()],
        out_specs=vmem(),
        scratch_shapes=[
            VMEM((BLK * (HOPS + 1), BLK), BF16),
            VMEM((BLK * (HOPS + 1), BLK), BF16),
            VMEM((rows, BLK), BF16),
            VMEM((rows, BLK), BF16),
            VMEM((rows + pad, BLK), BF16),
            VMEM((rows, BLK), BF16),
            VMEM((rows, BLK), BF16),
            VMEM((rows, BLK), BF16),
            VMEM((rows, BLK), BF16),
            VMEM((BLK, rows), BF16),
            VMEM((rows, BLK), F32),
            VMEM((rows, BLK), F32),
            VMEM((rows, BLK), F32),
            VMEM((rows, BLK), F32),
            VMEM((rows, BLK), F32),
            VMEM((rows + pad, BLK), F32),
            VMEM((BLK, BLK * (HOPS + 1)), F32),
            VMEM((2 * ch, LANES), F32),
        ],
        compiler_params=pltpu.CompilerParams(vmem_limit_bytes=32 * 1024 * 1024),
        cost_estimate=pl.CostEstimate(
            flops=2 * 30 * rows * BLK * BLK, bytes_accessed=7_000_000, transcendentals=0
        ),
        name="long_filter",
    )(index[None], table, got, mine)
    low_kv, high_kv, reply = lax.optimization_barrier((low_kv, high_kv, reply))
    back = lax.all_to_all(reply, "ctx", 0, 0, tiled=True)

    seq_total = tokens * peers
    chan_total = channels * lax.axis_size("ch")
    tap_sum, skip_sum = pl.pallas_call(
        functools.partial(
            totals_kernel,
            1.0 / math.sqrt(seq_total * chan_total / filters),
            1.0 / math.sqrt(seq_total),
        ),
        out_shape=(
            jax.ShapeDtypeStruct((filters, TAP_ROWS * LANES), F32),
            jax.ShapeDtypeStruct((channels // LANES, LANES), F32),
        ),
        grid=(1,),
        in_specs=[
            pl.BlockSpec((peers, 2, ch, LANES), lambda o: (0, 0, 0, tokens // LANES)),
        ],
        out_specs=(
            pl.BlockSpec((filters, TAP_ROWS * LANES), lambda o: (0, 0)),
            pl.BlockSpec((channels // LANES, LANES), lambda o: (0, 0)),
        ),
        name="totals",
    )(back)
    other = lax.ppermute(tap_sum, "ch", [(0, 1), (1, 0)])

    out_y, grads = pl.pallas_call(
        finish_kernel,
        out_shape=(
            jax.ShapeDtypeStruct((tokens, channels), BF16),
            jax.ShapeDtypeStruct((streams, tokens, channels), BF16),
        ),
        in_specs=[smem(), smem(), vmem()] + [hbm()] * 7,
        out_specs=(hbm(), hbm()),
        scratch_shapes=row_buffers
        + [
            VMEM((ROWS, peers, 2, ch, row_len), BF16),
            VMEM((ROWS, row_len, channels), BF16),
            VMEM((ROWS, streams, row_len, channels), BF16),
            pltpu.SemaphoreType.DMA((ROWS, 4)),
            pltpu.SemaphoreType.DMA((ROWS, 4)),
        ],
        compiler_params=pltpu.CompilerParams(vmem_limit_bytes=VLIM),
        name="finish",
    )(code, slot, skip_gain[None], own, low, high, out_grad, low_kv, high_kv, back)

    grad_taps = (tap_sum + other)[:, :tap_count]
    grad_skip = skip_sum.reshape(channels)
    return (out_y, grads.transpose(1, 0, 2), grad_taps, grad_skip)


def solution(mesh):
    return jax.shard_map(
        on_device,
        mesh=mesh,
        in_specs=(P("ctx", None, None, "ch"), P(), P(), P(), P("ch"), P("ctx", "ch")),
        out_specs=(P("ctx", "ch"), P("ctx", None, "ch"), P(), P("ch")),
        check_vma=False,
    )
```

time: 149 us -> 138 us (0.926)
  waiting for transfers between devices: 36.2 us -> 30.8 us
  local copies, waits for them, and re-layouts: 6.11 us -> 0.84 us
  Pallas kernels: 46.1 us -> 43.5 us
  starting transfers between devices: 14.3 us -> 16.8 us
    ppermute x4, waiting for transfers between devices: 14.4 us -> 10 us  [shifted(): lax.ppermute(array, axis, [(i, (i + by) % length) for i in range(length)])]
    unnamed x19 -> x14, local copies, waits for them, and re-layouts: 4.67 us -> 0.83 us
    pallas_call x1, Pallas kernels: 21.4 us -> 18.6 us  [on_device(): pl.pallas_call(long_kernel, out_shape=jax.ShapeDtypeStruct((peers, 2, ch,...]
    all_to_all x1, starting transfers between devices: 8.26 us -> 10.9 us  [on_device(): got = lax.all_to_all(sent, 'ctx', 0, 0, tiled=True)]
    pallas_call x2 -> x3, Pallas kernels: 12 us -> 13.8 us  [the longest x1 8.18 us: on_device(): pl.pallas_call(functools.partial(tables_kernel, docs), out_shape=jax.Shap...]
    pallas_call x1, Pallas kernels: 7.54 us -> 5.78 us  [on_device(): pl.pallas_call(finish_kernel, out_shape=(jax.ShapeDtypeStruct((tokens, ch...]
  transfers between devices with their start and end apart: 6 -> 6, of which waited for: 3 -> 3; matrix products, arithmetic and copies ran while one was open for 1% -> 0% of each run, Pallas kernels for 24% -> 27%
where the time goes in v3:
time: 138 us
  blocking collectives  44.4 us (32%)
  Pallas kernels  43.5 us (32%)
  waiting for transfers between devices  30.8 us (22%)
  starting transfers between devices  16.8 us (12%)
    all_to_all x1, blocking collectives, on_device(): back = lax.all_to_all(reply, 'ctx', 0, 0, tiled=True)  44.4 us
    all_to_all x1, waiting for transfers between devices, on_device(): got = lax.all_to_all(sent, 'ctx', 0, 0, tiled=True)  20.7 us
    pallas_call x1, Pallas kernels, on_device(): pl.pallas_call(long_kernel, out_shape=jax.ShapeDtypeStruct((peers, 2, ch,...  18.6 us
    all_to_all x1, starting transfers between devices, on_device(): got = lax.all_to_all(sent, 'ctx', 0, 0, tiled=True)  10.9 us
    ppermute x4, waiting for transfers between devices, shifted(): lax.ppermute(array, axis, [(i, (i + by) % length) for i in range(length)])  10 us
    pallas_call x1, Pallas kernels, on_device(): pl.pallas_call(functools.partial(tables_kernel, docs), out_shape=jax.Shap...  8.18 us
    pallas_call x1, Pallas kernels, on_device(): pl.pallas_call(finish_kernel, out_shape=(jax.ShapeDtypeStruct((tokens, ch...  5.78 us
    pallas_call x1, Pallas kernels, on_device(): pl.pallas_call(own_kernel, out_shape=sent_shape, in_specs=[smem(), smem()...  4.39 us
  transfers between devices with their start and end apart: 6, of which 3 were waited for; matrix products, arithmetic and copies ran while one was open for 0% of the time, Pallas kernels for 27%

profile of v3, /device:TPU:1, one launch (start us, length us, event | category | flops | bytes accessed | tf_op | source)
XLA Modules:
  0.0 137.7 jit_solution(15165125559332303633)
XLA Ops:
  0.6 0.0 copy-start
  0.7 3.5 %choose.1 = (bf16[2,128,1024]{2,1,0:T(8,128)(2,1)}, bf16[2,128,1024]{2,1,0:T(8,128)(2,1)}, bf16[2,128,1024]{2,1,0:T(8,128)(2,1)}, bf16[2,128,1024]{2,1,0:T(8,128)(2,1)}, s32[4]{0:T(128)}, /*index=5*/s32[4]{0:T(128)}) custom-call(s32[1]{0:T(128)} %bitcast.me_ref, s32[2,384]{1,0:T(2,128)} %bitcast.10, bf16[6,3,128,1024]{3,2,1,0:T(8,128)(2,1)} %bitcast.6), custom_call_target="tpu_custom_call" | custom-call | tf_op jit(solution)/shard_map/choose/pallas_call | solution.py:517
  4.2 2.7 %collective-permute-start = (bf16[2,128,1024]{2,1,0:T(8,128)(2,1)}, bf16[2,128,1024]{2,1,0:T(8,128)(2,1)S(1)}, u32[]{:S(2)}, u32[]{:S(2)}) collective-permute-start(bf16[2,128,1024]{2,1,0:T(8,128)(2,1)} %get-tuple-element.22), channel_id=1, source_target_pairs={{0,2},{2,4},{4,6},{6,8},{8,10},{10,12},{12,14},{14,16},{16,18},{18... | collective-permute-start | bytes 1572872 | tf_op jit(solution)/shard_map/ppermute | solution.py:502
  6.9 0.0 collective-permute-start.1
  6.9 4.4 %own_products.1.part_ref = bf16[64,2,16,512]{3,2,1,0:T(8,128)(2,1)} custom-call(s32[4]{0:T(128)} %get-tuple-element.20.code_ref, s32[4]{0:T(128)} %get-tuple-element.21.slot_ref, bf16[6,3,128,1024]{3,2,1,0:T(8,128)(2,1)} %bitcast.7, bf16[512,1024]{1,0:T(8,128)(2,1)} %grad_ref.5), custom_call_target="tpu_custom_call" | custom-call | bytes 20000000 | tf_op jit(solution)/shard_map/own_products/pallas_call | solution.py:548
  11.3 7.7 %collective-permute-done.low_ref = bf16[2,128,1024]{2,1,0:T(8,128)(2,1)S(1)} collective-permute-done((bf16[2,128,1024]{2,1,0:T(8,128)(2,1)}, bf16[2,128,1024]{2,1,0:T(8,128)(2,1)S(1)}, u32[]{:S(2)}, u32[]{:S(2)}) %collective-permute-start) | collective-permute-done | bytes 524320 | tf_op jit(solution)/shard_map/ppermute | solution.py:502
  18.9 2.4 %collective-permute-done.1.high_ref = bf16[2,128,1024]{2,1,0:T(8,128)(2,1)S(1)} collective-permute-done((bf16[2,128,1024]{2,1,0:T(8,128)(2,1)}, bf16[2,128,1024]{2,1,0:T(8,128)(2,1)S(1)}, u32[]{:S(2)}, u32[]{:S(2)}) %collective-permute-start.1) | collective-permute-done | bytes 524320 | tf_op jit(solution)/shard_map/ppermute | solution.py:502
  21.3 0.8 copy-done.3
  22.1 1.3 guest_products.1
  23.4 0.0 copy-start.1
  23.4 10.9 %all-to-all-start = ((bf16[64,2,16,512]{3,2,1,0:T(8,128)(2,1)}), bf16[64,2,16,512]{3,2,1,0:T(8,128)(2,1)S(1)}, u32[]{:S(2)}, u32[]{:S(2)}) async-start(bf16[64,2,16,512]{3,2,1,0:T(8,128)(2,1)} %guest_products.1), calls=%async_computation | async-start | bytes 4194304 | tf_op jit(solution)/shard_map/all_to_all | solution.py:572
  34.3 8.2 %tables.1.table_ref = s32[8,128]{1,0:T(8,128)S(1)} custom-call(s32[128]{0:T(128)S(1)} %copy-done.1), custom_call_target="tpu_custom_call" | custom-call | bytes 20000000 | tf_op jit(solution)/shard_map/tables/pallas_call | solution.py:532
  42.6 20.7 %all-to-all-done.got_ref = bf16[64,2,16,512]{3,2,1,0:T(8,128)(2,1)S(1)} async-done(((bf16[64,2,16,512]{3,2,1,0:T(8,128)(2,1)}), bf16[64,2,16,512]{3,2,1,0:T(8,128)(2,1)S(1)}, u32[]{:S(2)}, u32[]{:S(2)}) %all-to-all-start) | async-done | bytes 2097184 | tf_op jit(solution)/shard_map/all_to_all | solution.py:572
  63.3 0.6 collective-permute-start.2
  63.9 0.0 collective-permute-start.3
  63.9 18.6 %long_filter.1 = bf16[64,2,16,640]{3,2,1,0:T(8,128)(2,1)S(1)} custom-call(s32[1]{0:T(128)} %bitcast.me_ref, s32[8,128]{1,0:T(8,128)S(1)} %tables.1.table_ref, bf16[64,2,16,512]{3,2,1,0:T(8,128)(2,1)S(1)} %all-to-all-done.got_ref, f32[1,2560]{1,0:T(1,128)S(1)} %pad_convert_fusion.taps_ref), custom_call_target="tpu_custom_call" | custom-call | flops 8053063680 | bytes 7000000 | tf_op jit(solution)/shard_map/long_filter/pallas_call | solution.py:579
  82.5 0.0 collective-permute-done.2.low_kv_ref
  82.5 0.0 collective-permute-done.3.high_kv_ref
  82.5 44.4 %all_to_all.10.got_ref.part_ref = bf16[64,2,16,640]{3,2,1,0:T(8,128)(2,1)} all-to-all(bf16[64,2,16,640]{3,2,1,0:T(8,128)(2,1)S(1)} %long_filter.1), channel_id=1, replica_groups=mesh['ctx'=64,'ch'=2] {'ctx'}, dimensions={0} | all-to-all | bytes 5242880 | tf_op jit(solution)/shard_map/all_to_all | solution.py:611
  127.0 1.7 %totals.1 = (f32[4,2176]{1,0:T(4,128)}, f32[8,128]{1,0:T(8,128)}) custom-call(bf16[64,2,16,640]{3,2,1,0:T(8,128)(2,1)} %all_to_all.10.got_ref.part_ref), custom_call_target="tpu_custom_call" | custom-call | tf_op jit(solution)/shard_map/totals/pallas_call | solution.py:615
  128.7 2.6 %collective-permute-start.4 = (f32[4,2176]{1,0:T(4,128)}, f32[4,2176]{1,0:T(4,128)S(1)}, u32[]{:S(2)}, u32[]{:S(2)}) collective-permute-start(f32[4,2176]{1,0:T(4,128)} %get-tuple-element.34), channel_id=1, source_target_pairs={{0,1},{1,0},{2,3},{3,2},{4,5},{5,4},{6,7},{7,6},{8,9},{9,8},{10,11... | collective-permute-start | bytes 104456 | tf_op jit(solution)/shard_map/ppermute | solution.py:635
  131.3 5.8 %finish.1 = (bf16[512,1024]{1,0:T(8,128)(2,1)}, bf16[3,512,1024]{2,1,0:T(8,128)(2,1)}) custom-call(s32[4]{0:T(128)} %get-tuple-element.20.code_ref, s32[4]{0:T(128)} %get-tuple-element.21.slot_ref, f32[1,1024]{1,0:T(1,128)} %bitcast.9, bf16[6,3,128,1024]{3,2,1,0:T(8,128)(2,1)} %bitcast.8, bf16[2,128,1024]{2,1,0:T(8,128)(2,1)} %copy-done.2, ...), custom_call_target="tpu_custom_call" | custom-call | tf_op jit(solution)/shard_map/finish/pallas_call | solution.py:637
  137.1 0.0 collective-permute-done.4
  137.1 0.6 slice_add_fusion
  (13 shorter events, 0.0 us)
Async XLA Ops:
  0.6 41.9 %copy-start = (f32[4,2049]{1,0:T(4,128)S(1)}, f32[4,2049]{1,0:T(4,128)}, u32[]{:S(2)}) copy-start(f32[4,2049]{1,0:T(4,128)} %param.9) | copy-start | bytes 98356
  4.2 14.7 %collective-permute-start = (bf16[2,128,1024]{2,1,0:T(8,128)(2,1)}, bf16[2,128,1024]{2,1,0:T(8,128)(2,1)S(1)}, u32[]{:S(2)}, u32[]{:S(2)}) collective-permute-start(bf16[2,128,1024]{2,1,0:T(8,128)(2,1)} %get-tuple-element.22), channel_id=1, source_target_pairs={{0,2},{2,4},{4,6},{6,8},{8,10},{10,12},{12,14},{14,16},{16,18},{18... | collective-permute-start | bytes 1572872 | tf_op jit(solution)/shard_map/ppermute | solution.py:502
  6.9 14.4 %collective-permute-start.1 = (bf16[2,128,1024]{2,1,0:T(8,128)(2,1)}, bf16[2,128,1024]{2,1,0:T(8,128)(2,1)S(1)}, u32[]{:S(2)}, u32[]{:S(2)}) collective-permute-start(bf16[2,128,1024]{2,1,0:T(8,128)(2,1)} %get-tuple-element.23), channel_id=1, source_target_pairs={{0,126},{2,0},{4,2},{6,4},{8,6},{10,8},{12,10},{14,12},{16,14},{18... | collective-permute-start | bytes 1572872 | tf_op jit(solution)/shard_map/ppermute | solution.py:502
  18.9 2.4 %copy-start.2 = (bf16[2,128,1024]{2,1,0:T(8,128)(2,1)}, bf16[2,128,1024]{2,1,0:T(8,128)(2,1)S(1)}, u32[]{:S(2)}) copy-start(bf16[2,128,1024]{2,1,0:T(8,128)(2,1)S(1)} %collective-permute-done.low_ref) | copy-start | bytes 1572868
  21.3 0.8 copy-start.3
  23.4 11.0 %copy-start.1 = (s32[128]{0:T(128)S(1)}, s32[128]{0:T(128)}, u32[]{:S(2)}) copy-start(s32[128]{0:T(128)} %length_ref.1) | copy-start | bytes 1540
  23.4 39.9 %all-to-all-start = ((bf16[64,2,16,512]{3,2,1,0:T(8,128)(2,1)}), bf16[64,2,16,512]{3,2,1,0:T(8,128)(2,1)S(1)}, u32[]{:S(2)}, u32[]{:S(2)}) async-start(bf16[64,2,16,512]{3,2,1,0:T(8,128)(2,1)} %guest_products.1), calls=%async_computation | async-start | bytes 4194304 | tf_op jit(solution)/shard_map/all_to_all | solution.py:572
  63.3 19.2 %collective-permute-start.2 = (bf16[2,128,1024]{2,1,0:T(8,128)(2,1)}, bf16[2,128,1024]{2,1,0:T(8,128)(2,1)S(1)}, u32[]{:S(2)}, u32[]{:S(2)}) collective-permute-start(bf16[2,128,1024]{2,1,0:T(8,128)(2,1)} %get-tuple-element.26), channel_id=1, source_target_pairs={{0,2},{2,4},{4,6},{6,8},{8,10},{10,12},{12,14},{14,16},{16,18},{18... | collective-permute-start | bytes 1572872 | tf_op jit(solution)/shard_map/ppermute | solution.py:502
  63.9 18.6 %collective-permute-start.3 = (bf16[2,128,1024]{2,1,0:T(8,128)(2,1)}, bf16[2,128,1024]{2,1,0:T(8,128)(2,1)S(1)}, u32[]{:S(2)}, u32[]{:S(2)}) collective-permute-start(bf16[2,128,1024]{2,1,0:T(8,128)(2,1)} %get-tuple-element.27), channel_id=1, source_target_pairs={{0,126},{2,0},{4,2},{6,4},{8,6},{10,8},{12,10},{14,12},{16,14},{18... | collective-permute-start | bytes 1572872 | tf_op jit(solution)/shard_map/ppermute | solution.py:502
  82.5 44.5 %copy-start.4 = (bf16[2,128,1024]{2,1,0:T(8,128)(2,1)}, bf16[2,128,1024]{2,1,0:T(8,128)(2,1)S(1)}, u32[]{:S(2)}) copy-start(bf16[2,128,1024]{2,1,0:T(8,128)(2,1)S(1)} %collective-permute-done.2.low_kv_ref) | copy-start | bytes 1572868
  82.5 44.4 %copy-start.5 = (bf16[2,128,1024]{2,1,0:T(8,128)(2,1)}, bf16[2,128,1024]{2,1,0:T(8,128)(2,1)S(1)}, u32[]{:S(2)}) copy-start(bf16[2,128,1024]{2,1,0:T(8,128)(2,1)S(1)} %collective-permute-done.3.high_kv_ref) | copy-start | bytes 1572868
  128.7 8.4 %collective-permute-start.4 = (f32[4,2176]{1,0:T(4,128)}, f32[4,2176]{1,0:T(4,128)S(1)}, u32[]{:S(2)}, u32[]{:S(2)}) collective-permute-start(f32[4,2176]{1,0:T(4,128)} %get-tuple-element.34), channel_id=1, source_target_pairs={{0,1},{1,0},{2,3},{3,2},{4,5},{5,4},{6,7},{7,6},{8,9},{9,8},{10,11... | collective-permute-start | bytes 104456 | tf_op jit(solution)/shard_map/ppermute | solution.py:635
  131.3 5.8 %copy-start.6 = (f32[4,2176]{1,0:T(4,128)S(1)}, f32[4,2176]{1,0:T(4,128)}, u32[]{:S(2)}) copy-start(f32[4,2176]{1,0:T(4,128)} %get-tuple-element.34) | copy-start | bytes 104452

commit v4 on v3

--- a/solution.py
+++ b/solution.py
@@ -37,8 +37,7 @@
 
 
 def choose_kernel(
-    cycle, me_ref, target_ref, own_ref, up_ref, down_ref, up_kv_ref, down_kv_ref,
-    code_ref, slot_ref, sems,
+    cycle, me_ref, target_ref, own_ref, up_ref, down_ref, code_ref, slot_ref, rows, sems
 ):
     me = me_ref[0]
     below = lax.rem(me + cycle - 1, cycle)
@@ -49,22 +48,18 @@
         shard = target_ref[0, me * SLOTS + k]
         up_slot = jnp.where(shard == above, k, up_slot)
         down_slot = jnp.where(shard == below, k, down_slot)
-    copies = []
-    for n, (slot, first, later) in enumerate(
-        ((up_slot, up_ref, up_kv_ref), (down_slot, down_ref, down_kv_ref))
-    ):
-        copies.append(
-            (
-                pltpu.make_async_copy(own_ref.at[slot, 0], first.at[0], sems.at[2 * n]),
-                pltpu.make_async_copy(own_ref.at[slot, pl.ds(1, 2)], later, sems.at[2 * n + 1]),
-            )
-        )
-    for one, two in copies:
-        two.start()
-        one.start()
+    copies = [
+        pltpu.make_async_copy(own_ref.at[slot, n], rows.at[side, n], sems.at[side, n])
+        for side, slot in enumerate((up_slot, down_slot))
+        for n in range(3)
+    ]
+    for copy in copies:
+        copy.start()
     for o in range(ROWS):
         code_ref[o] = 0
         slot_ref[o] = 0
+    slot_ref[ROWS] = up_slot
+    slot_ref[ROWS + 1] = down_slot
     for k in range(SLOTS):
         shard = target_ref[0, me * SLOTS + k]
         offset = target_ref[1, me * SLOTS + k]
@@ -81,10 +76,24 @@
             def _():
                 code_ref[their_offset] = code
 
-    for (one, two), first, later in zip(copies, (up_ref, down_ref), (up_kv_ref, down_kv_ref)):
-        two.wait()
-        first[1] = round_mul(later[0], later[1])
-        one.wait()
+    for copy in copies:
+        copy.wait()
+    for side, to_ref in enumerate((up_ref, down_ref)):
+        to_ref[0] = rows[side, 0]
+        for n in range(rows.shape[-1] // WIDE):
+            lanes = slice(n * WIDE, (n + 1) * WIDE)
+            to_ref[1, :, lanes] = round_mul(rows[side, 1, :, lanes], rows[side, 2, :, lanes])
+
+
+def later_kernel(slot_ref, own_ref, up_ref, down_ref, sems):
+    copies = [
+        pltpu.make_async_copy(own_ref.at[slot_ref[ROWS + n], pl.ds(1, 2)], to_ref, sems.at[n])
+        for n, to_ref in enumerate((up_ref, down_ref))
+    ]
+    for copy in copies:
+        copy.start()
+    for copy in copies:
+        copy.wait()
 
 
 def tables_kernel(docs, length_ref, table_ref, count_ref):
@@ -100,6 +109,7 @@
 
         def tails(b, carry):
             table_ref[2, b] = jnp.maximum(start - BLK * b, 0)
+            table_ref[8, b] = lax.shift_right_logical(end - 1, 8) - b
             return carry
 
         lax.fori_loop(
@@ -115,31 +125,32 @@
 
     lax.fori_loop(0, docs, one_doc, jnp.int32(0))
 
-    for n in range(HOPS + 1):
-        count_ref[n] = 0
-
-    def count(b, carry):
-        reach = table_ref[0, b]
-        count_ref[reach] = count_ref[reach] + 1
-        return carry
-
-    lax.fori_loop(0, docs, count, 0)
-    before = jnp.int32(0)
-    for n in range(HOPS, -1, -1):
-        these = count_ref[n]
-        count_ref[n] = before
-        before = before + these
-
-    def place(b, carry):
-        reach = table_ref[0, b]
-        at = count_ref[reach]
-        count_ref[reach] = at + 1
-        table_ref[5, at] = b
-        table_ref[6, b] = at
-        table_ref[7, at] = reach
-        return carry
-
-    lax.fori_loop(0, docs, place, 0)
+    for kind, (reach_row, order_row) in enumerate(((0, 5), (8, 9))):
+        for n in range(HOPS + 1):
+            count_ref[kind, n] = 0
+
+        def count(b, carry):
+            reach = table_ref[reach_row, b]
+            count_ref[kind, reach] = count_ref[kind, reach] + 1
+            return carry
+
+        lax.fori_loop(0, docs, count, 0)
+        before = jnp.int32(0)
+        for n in range(HOPS, -1, -1):
+            these = count_ref[kind, n]
+            count_ref[kind, n] = before
+            before = before + these
+
+        def place(b, carry):
+            reach = table_ref[reach_row, b]
+            at = count_ref[kind, reach]
+            count_ref[kind, reach] = at + 1
+            table_ref[order_row, at] = b
+            table_ref[order_row + 1, b] = at
+            table_ref[order_row + 2, at] = reach
+            return carry
+
+        lax.fori_loop(0, docs, place, 0)
 
 
 def make_bands(taps_ref, fwd_ref, bwd_ref):
@@ -199,38 +210,59 @@
             )
 
 
-def guest_kernel(code_ref, low_ref, high_ref, grad_ref, part_ref, sent_ref, grad, ready, sems):
+def guest_kernel(
+    code_ref, low_ref, high_ref, grad_ref, part_ref, sent_ref, guest, grad, ready, in_sems, out_sems
+):
     del part_ref
-    toks = low_ref.shape[1]
+    _, peers, _, chans, toks = ready.shape
+    together = WIDE // chans
+    parts = peers // together
     guests = []
     for n, ref in enumerate((low_ref, high_ref)):
         at = jnp.int32(0)
         for o in range(ROWS):
             at = jnp.where(code_ref[o] == n + 1, o + 1, at)
         here = pl.ds(pl.multiple_of(jnp.maximum(at - 1, 0) * toks, toks), toks)
-        copy_in = pltpu.make_async_copy(grad_ref.at[here], grad.at[n], sems.at[n])
-        copy_out = pltpu.make_async_copy(
-            ready.at[n], sent_ref.at[:, :, :, here], sems.at[2 + n]
-        )
-        guests.append((n, ref, at > 0, copy_in, copy_out))
-    for n, ref, live, copy_in, copy_out in guests:
-        pl.when(live)(copy_in.start)
-    for n, ref, live, copy_in, copy_out in guests:
+        into = [
+            pltpu.make_async_copy(ref, guest.at[n], in_sems.at[n, 0]),
+            pltpu.make_async_copy(grad_ref.at[here], grad.at[n], in_sems.at[n, 1]),
+        ]
+        out = []
+        for m in range(parts):
+            to = pl.ds(m * together, together)
+            out.append(
+                pltpu.make_async_copy(
+                    ready.at[n, to], sent_ref.at[to, :, :, here], out_sems.at[n, m]
+                )
+            )
+        guests.append((n, at > 0, into, out))
+    for n, live, into, out in guests:
 
         @pl.when(live)
         def _():
-            copy_in.wait()
-            write_row(
-                ready.at[n],
-                0,
-                toks,
-                lambda c: ref[1, :, c],
-                lambda c: round_mul(grad[n, :, c], ref[0, :, c]),
-            )
-            copy_out.start()
-
-    for n, ref, live, copy_in, copy_out in guests:
-        pl.when(live)(copy_out.wait)
+            for copy in into:
+                copy.start()
+
+    for n, live, into, out in guests:
+
+        @pl.when(live)
+        def _():
+            for copy in into:
+                copy.wait()
+            for m in range(parts):
+                lanes = slice(m * WIDE, (m + 1) * WIDE)
+                to = slice(m * together, (m + 1) * together)
+                grad_mid = round_mul(grad[n, :, lanes], guest[n, 0, :, lanes])
+                ready[n, to, 0] = guest[n, 1, :, lanes].T.reshape(together, chans, toks)
+                ready[n, to, 1] = grad_mid.T.reshape(together, chans, toks)
+                out[m].start()
+
+    for n, live, into, out in guests:
+
+        @pl.when(live)
+        def _():
+            for copy in out:
+                copy.wait()
 
 
 def place_of(b, peers):
@@ -245,7 +277,7 @@
 
 def long_kernel(
     me_ref, table_ref, got_ref, taps_ref, out_ref,
-    fwd_ref, bwd_ref, x_all, z_all, x_tail, z_head, xd, zd, ze, turned, doc_near, doc_back,
+    fwd_ref, bwd_ref, x_all, z_all, x_tail, z_head, z_back, xd, zd, ze, turned, doc_near, doc_back,
     near, far_sum, back_near, back_far, pairs, extra,
 ):
     peers = got_ref.shape[0]
@@ -259,6 +291,7 @@
 
     make_bands(taps_ref, fwd_ref, bwd_ref)
     x_tail[0:pad, :] = jnp.zeros((pad, BLK), BF16)
+    z_head[rows : rows + pad, :] = jnp.zeros((pad, BLK), BF16)
     back_far[...] = jnp.zeros_like(back_far)
     far_sum[...] = jnp.zeros_like(far_sum)
     pairs[...] = jnp.zeros_like(pairs)
@@ -274,7 +307,9 @@
         end, tail = table_ref[1, b], table_ref[2, b]
         x_f, z_f = x.astype(F32), z.astype(F32)
         x_tail[pl.ds(at + pad, ch), :] = jnp.where(lane >= tail, x_f, 0).astype(BF16)
-        z_head[pl.ds(pl.multiple_of(k * ch, ch), ch), :] = jnp.where(lane < end, z_f, 0).astype(BF16)
+        z_cut = jnp.where(lane < end, z_f, 0).astype(BF16)
+        z_head[pl.ds(at, ch), :] = z_cut
+        z_back[pl.ds(pl.multiple_of(k * ch, ch), ch), :] = z_cut
         return total + x_f * z_f
 
     skip = lax.fori_loop(0, blocks, spread, jnp.zeros((ch, BLK), F32), unroll=4)
@@ -322,7 +357,7 @@
         behind = dot(jnp.concatenate([z, ze[here, :]], axis=0), first_bwd[...])
         back_near[here, :] = behind[:step]
         doc_back[here, :] = behind[step:]
-        turned[:, here] = z.T
+        turned[:, here] = z_back[here, :].T
         pairs[:, far:] += dot(jnp.concatenate([z_all[here, :].T, zd[here, :].T], axis=1), x)
         return carry
 
@@ -332,7 +367,7 @@
         end_block, end_from, end_at, start_block, start_at, start_to = doc_parts(d)
         here = pl.ds(pl.multiple_of(d * ch, ch), ch)
         at_end = pl.multiple_of(end_block * ch, ch)
-        at_start = pl.multiple_of(table_ref[6, start_block] * ch, ch)
+        at_start = pl.multiple_of(start_block * ch, ch)
         near[pl.ds(at_end, ch), :] += jnp.where(lane < end_at, doc_near[here, :], 0.0)
         back_near[pl.ds(at_start, ch), :] += jnp.where(lane >= start_at, doc_back[here, :], 0.0)
         return carry
@@ -340,34 +375,37 @@
     lax.fori_loop(0, docs, add_docs, 0, unroll=4)
 
     wide = GROUP * ch
-    zero = jnp.zeros((), BF16)
+
+    def collect(c, order_row, source, by, delta, empty):
+        tiles = []
+        for i in range(GROUP):
+            k = c * GROUP + i
+            inside = table_ref[order_row + 2, k] >= delta
+            at = jnp.where(inside, table_ref[order_row, k] + by, empty)
+            tiles.append(source[pl.ds(pl.multiple_of(at * ch, ch), ch), :])
+        return jnp.concatenate(tiles, axis=0)
 
     def outer(c, carry):
-        at = pl.multiple_of(c * wide, wide)
-        here = pl.ds(at, wide)
-
-        def one_lag(delta, carry):
-            tiles, targets, live = [], [], []
-            for i in range(GROUP):
-                k = c * GROUP + i
-                target = pl.multiple_of((table_ref[5, k] + HOPS - delta) * ch, ch)
-                inside = table_ref[7, k] >= delta
-                tiles.append(jnp.where(inside, x_tail[pl.ds(target, ch), :], zero))
-                targets.append(target)
-                live.append(inside)
-            x = jnp.concatenate(tiles, axis=0)
-            fwd_at = pl.multiple_of((HOPS - delta) * BLK, BLK)
-            bwd_at = pl.multiple_of(delta * BLK, BLK)
-            far_sum[here, :] += dot(x, fwd_ref[pl.ds(fwd_at, BLK), :])
-            pairs[:, pl.ds(fwd_at, BLK)] += dot(turned[:, here], x)
-            y = dot(z_head[here, :], bwd_ref[pl.ds(bwd_at, BLK), :])
-            for i in range(GROUP):
-                back_far[pl.ds(targets[i], ch), :] += jnp.where(
-                    live[i], y[i * ch : (i + 1) * ch], 0.0
+        here = pl.ds(pl.multiple_of(c * wide, wide), wide)
+        reach_back, reach_ahead = table_ref[7, c * GROUP], table_ref[11, c * GROUP]
+        for reach in range(1, HOPS + 1):
+
+            @pl.when(reach_back == reach)
+            def _():
+                x = jnp.concatenate(
+                    [collect(c, 5, x_tail, HOPS - n, n, 0) for n in range(reach, 0, -1)], axis=1
                 )
-            return carry
-
-        lax.fori_loop(1, table_ref[7, c * GROUP] + 1, one_lag, 0)
+                lags = slice((HOPS - reach) * BLK, far)
+                far_sum[here, :] = dot(x, fwd_ref[lags, :])
+                pairs[:, lags] += dot(turned[:, here], x)
+
+            @pl.when(reach_ahead == reach)
+            def _():
+                z = jnp.concatenate(
+                    [collect(c, 9, z_head, n, n, blocks) for n in range(1, reach + 1)], axis=1
+                )
+                back_far[here, :] = dot(z, bwd_ref[BLK : (reach + 1) * BLK, :])
+
         return carry
 
     lax.fori_loop(0, blocks // GROUP, outer, 0)
@@ -378,9 +416,10 @@
         here = pl.ds(pl.multiple_of(k * ch, ch), ch)
         at = pl.multiple_of(b * ch, ch)
         ahead = jnp.where(lane < table_ref[1, b], far_sum[here, :], 0.0)
-        behind = jnp.where(lane >= table_ref[2, b], back_far[pl.ds(at + pad, ch), :], 0.0)
+        ahead_at = pl.multiple_of(table_ref[10, b] * ch, ch)
+        behind = jnp.where(lane >= table_ref[2, b], back_far[pl.ds(ahead_at, ch), :], 0.0)
         out_ref[src, 0, :, pl.ds(at_lane, BLK)] = (near[pl.ds(at, ch), :] + ahead).astype(BF16)
-        out_ref[src, 1, :, pl.ds(at_lane, BLK)] = (back_near[here, :] + behind).astype(BF16)
+        out_ref[src, 1, :, pl.ds(at_lane, BLK)] = (back_near[pl.ds(at, ch), :] + behind).astype(BF16)
         return carry
 
     lax.fori_loop(0, blocks, gather_out, 0, unroll=4)
@@ -513,16 +552,33 @@
     blocks = 2 * peers
     own = rollout_rows.transpose(0, 2, 1, 3)
     half_shape = jax.ShapeDtypeStruct((2, row_len, channels), BF16)
-    list_shape = jax.ShapeDtypeStruct((ROWS,), jnp.int32)
-    up, down, up_kv, down_kv, code, slot = pl.pallas_call(
+    up, down, code, slot = pl.pallas_call(
         functools.partial(choose_kernel, peers),
-        out_shape=(half_shape,) * 4 + (list_shape,) * 2,
+        out_shape=(
+            half_shape,
+            half_shape,
+            jax.ShapeDtypeStruct((ROWS,), jnp.int32),
+            jax.ShapeDtypeStruct((ROWS + 2,), jnp.int32),
+        ),
         in_specs=[smem(), smem(), hbm()],
-        out_specs=(vmem(),) * 4 + (smem(),) * 2,
-        scratch_shapes=[pltpu.SemaphoreType.DMA((4,))],
+        out_specs=(vmem(), vmem(), smem(), smem()),
+        scratch_shapes=[
+            VMEM((2, streams, row_len, channels), BF16),
+            pltpu.SemaphoreType.DMA((2, 3)),
+        ],
         compiler_params=pltpu.CompilerParams(vmem_limit_bytes=VLIM),
         name="choose",
     )(index[None], pack_targets.T, own)
+    up_kv, down_kv = pl.pallas_call(
+        later_kernel,
+        out_shape=(half_shape, half_shape),
+        in_specs=[smem(), hbm()],
+        out_specs=(vmem(), vmem()),
+        scratch_shapes=[pltpu.SemaphoreType.DMA((2,))],
+        compiler_params=pltpu.CompilerParams(vmem_limit_bytes=VLIM),
+        cost_estimate=pl.CostEstimate(flops=0, bytes_accessed=6_000_000, transcendentals=0),
+        name="later",
+    )(slot, own)
     low = shifted(up, "ctx", 1)
     high = shifted(down, "ctx", -1)
 
@@ -531,10 +587,10 @@
     mine = jnp.pad(mine, [(0, 0), (BLK, BLK * (HOPS + 1) - tap_count)])
     table = pl.pallas_call(
         functools.partial(tables_kernel, docs),
-        out_shape=jax.ShapeDtypeStruct((8, docs), jnp.int32),
+        out_shape=jax.ShapeDtypeStruct((16, docs), jnp.int32),
         in_specs=[smem()],
         out_specs=smem(),
-        scratch_shapes=[SMEM((HOPS + 1,), jnp.int32)],
+        scratch_shapes=[SMEM((2, HOPS + 1), jnp.int32)],
         compiler_params=pltpu.CompilerParams(vmem_limit_bytes=4 * 1024 * 1024),
         cost_estimate=pl.CostEstimate(flops=0, bytes_accessed=20_000_000, transcendentals=0),
         name="tables",
@@ -558,12 +614,14 @@
     sent = pl.pallas_call(
         guest_kernel,
         out_shape=sent_shape,
-        in_specs=[smem(), vmem(), vmem(), hbm(), hbm()],
+        in_specs=[smem(), hbm(), hbm(), hbm(), hbm()],
         out_specs=hbm(),
         scratch_shapes=[
+            VMEM((2, 2, row_len, channels), BF16),
             VMEM((2, row_len, channels), BF16),
             VMEM((2, peers, 2, ch, row_len), BF16),
-            pltpu.SemaphoreType.DMA((4,)),
+            pltpu.SemaphoreType.DMA((2, 2)),
+            pltpu.SemaphoreType.DMA((2, channels // WIDE)),
         ],
         input_output_aliases={4: 0},
         compiler_params=pltpu.CompilerParams(vmem_limit_bytes=VLIM),
@@ -587,6 +645,7 @@
             VMEM((rows, BLK), BF16),
             VMEM((rows, BLK), BF16),
             VMEM((rows + pad, BLK), BF16),
+            VMEM((rows + pad, BLK), BF16),
             VMEM((rows, BLK), BF16),
             VMEM((rows, BLK), BF16),
             VMEM((rows, BLK), BF16),
@@ -597,11 +656,11 @@
             VMEM((rows, BLK), F32),
             VMEM((rows, BLK), F32),
             VMEM((rows, BLK), F32),
-            VMEM((rows + pad, BLK), F32),
+            VMEM((rows, BLK), F32),
             VMEM((BLK, BLK * (HOPS + 1)), F32),
             VMEM((2 * ch, LANES), F32),
         ],
-        compiler_params=pltpu.CompilerParams(vmem_limit_bytes=32 * 1024 * 1024),
+        compiler_params=pltpu.CompilerParams(vmem_limit_bytes=34 * 1024 * 1024),
         cost_estimate=pl.CostEstimate(
             flops=2 * 30 * rows * BLK * BLK, bytes_accessed=7_000_000, transcendentals=0
         ),

time: 138 us -> 136 us (0.986)
  waiting for transfers between devices: 30.8 us -> 23.6 us
  Pallas kernels: 43.5 us -> 49.7 us
  starting transfers between devices: 16.8 us -> 14.9 us
    all_to_all x1, waiting for transfers between devices: 20.7 us -> 13.4 us  [on_device(): got = lax.all_to_all(sent, 'ctx', 0, 0, tiled=True)]
    pallas_call x1 -> x2, Pallas kernels: 1.27 us -> 5.97 us  [the longest x1 2.99 us: on_device(): pl.pallas_call(guest_kernel, out_shape=sent_shape, in_specs=[smem(), hbm(...]
    pallas_call x1, Pallas kernels: 8.18 us -> 12.5 us  [on_device(): pl.pallas_call(functools.partial(tables_kernel, docs), out_shape=jax.Shap...]
    pallas_call x1, Pallas kernels: 18.6 us -> 16.3 us  [on_device(): pl.pallas_call(long_kernel, out_shape=jax.ShapeDtypeStruct((peers, 2, ch,...]
    all_to_all x1, starting transfers between devices: 10.9 us -> 8.97 us  [on_device(): got = lax.all_to_all(sent, 'ctx', 0, 0, tiled=True)]
  transfers between devices with their start and end apart: 6 -> 6, of which waited for: 3 -> 3; matrix products, arithmetic and copies ran while one was open for 0% -> 0% of each run, Pallas kernels for 27% -> 31%
where the time goes in v4:
time: 136 us; the launch traced here: 135 us
  Pallas kernels  49.7 us (37%)
  blocking collectives  44.4 us (33%)
  waiting for transfers between devices  23.6 us (17%)
  starting transfers between devices  14.9 us (11%)
    all_to_all x1, blocking collectives, on_device(): back = lax.all_to_all(reply, 'ctx', 0, 0, tiled=True)  44.4 us
    pallas_call x1, Pallas kernels, on_device(): pl.pallas_call(long_kernel, out_shape=jax.ShapeDtypeStruct((peers, 2, ch,...  16.3 us
    all_to_all x1, waiting for transfers between devices, on_device(): got = lax.all_to_all(sent, 'ctx', 0, 0, tiled=True)  13.4 us
    pallas_call x1, Pallas kernels, on_device(): pl.pallas_call(functools.partial(tables_kernel, docs), out_shape=jax.Shap...  12.5 us
    ppermute x4, waiting for transfers between devices, shifted(): lax.ppermute(array, axis, [(i, (i + by) % length) for i in range(length)])  10.2 us
    all_to_all x1, starting transfers between devices, on_device(): got = lax.all_to_all(sent, 'ctx', 0, 0, tiled=True)  8.97 us
    pallas_call x1, Pallas kernels, on_device(): pl.pallas_call(finish_kernel, out_shape=(jax.ShapeDtypeStruct((tokens, ch...  5.78 us
    pallas_call x1, Pallas kernels, on_device(): pl.pallas_call(own_kernel, out_shape=sent_shape, in_specs=[smem(), smem()...  4.19 us
  transfers between devices with their start and end apart: 6, of which 3 were waited for; matrix products, arithmetic and copies ran while one was open for 0% of the time, Pallas kernels for 31%

profile of v4, /device:TPU:1, one launch (start us, length us, event | category | flops | bytes accessed | tf_op | source)
XLA Modules:
  0.0 135.0 jit_solution(12019041253290335752)
XLA Ops:
  0.6 0.0 copy-start
  0.7 3.2 %choose.1 = (bf16[2,128,1024]{2,1,0:T(8,128)(2,1)}, bf16[2,128,1024]{2,1,0:T(8,128)(2,1)}, s32[4]{0:T(128)}, s32[6]{0:T(128)}) custom-call(s32[1]{0:T(128)} %bitcast.me_ref, s32[2,384]{1,0:T(2,128)} %bitcast.11, bf16[6,3,128,1024]{3,2,1,0:T(8,128)(2,1)} %bitcast.6), custom_call_target="tpu_custom_call" | custom-call | tf_op jit(solution)/shard_map/choose/pallas_call | solution.py:555
  3.9 2.8 %collective-permute-start = (bf16[2,128,1024]{2,1,0:T(8,128)(2,1)}, bf16[2,128,1024]{2,1,0:T(8,128)(2,1)S(1)}, u32[]{:S(2)}, u32[]{:S(2)}) collective-permute-start(bf16[2,128,1024]{2,1,0:T(8,128)(2,1)} %get-tuple-element.22), channel_id=1, source_target_pairs={{0,2},{2,4},{4,6},{6,8},{8,10},{10,12},{12,14},{14,16},{16,18},{18... | collective-permute-start | bytes 1572872 | tf_op jit(solution)/shard_map/ppermute | solution.py:541
  6.6 0.0 collective-permute-start.1
  6.6 4.2 %own_products.1.part_ref = bf16[64,2,16,512]{3,2,1,0:T(8,128)(2,1)} custom-call(s32[4]{0:T(128)} %get-tuple-element.20.code_ref, s32[6]{0:T(128)} %get-tuple-element.21.slot_ref, bf16[6,3,128,1024]{3,2,1,0:T(8,128)(2,1)} %bitcast.7, bf16[512,1024]{1,0:T(8,128)(2,1)} %grad_ref.5), custom_call_target="tpu_custom_call" | custom-call | bytes 20000000 | tf_op jit(solution)/shard_map/own_products/pallas_call | solution.py:604
  10.8 7.9 %collective-permute-done.low_ref = bf16[2,128,1024]{2,1,0:T(8,128)(2,1)S(1)} collective-permute-done((bf16[2,128,1024]{2,1,0:T(8,128)(2,1)}, bf16[2,128,1024]{2,1,0:T(8,128)(2,1)S(1)}, u32[]{:S(2)}, u32[]{:S(2)}) %collective-permute-start) | collective-permute-done | bytes 524320 | tf_op jit(solution)/shard_map/ppermute | solution.py:541
  18.7 2.4 %collective-permute-done.1.high_ref = bf16[2,128,1024]{2,1,0:T(8,128)(2,1)S(1)} collective-permute-done((bf16[2,128,1024]{2,1,0:T(8,128)(2,1)}, bf16[2,128,1024]{2,1,0:T(8,128)(2,1)S(1)}, u32[]{:S(2)}, u32[]{:S(2)}) %collective-permute-start.1) | collective-permute-done | bytes 524320 | tf_op jit(solution)/shard_map/ppermute | solution.py:541
  21.1 0.8 copy-done.3
  21.9 3.0 %guest_products.1 = bf16[64,2,16,512]{3,2,1,0:T(8,128)(2,1)} custom-call(s32[4]{0:T(128)} %get-tuple-element.20.code_ref, bf16[2,128,1024]{2,1,0:T(8,128)(2,1)} %copy-done.2, bf16[2,128,1024]{2,1,0:T(8,128)(2,1)} %copy-done.3, bf16[512,1024]{1,0:T(8,128)(2,1)} %grad_ref.5, bf16[64,2,16,512]{3,2,1,0:T(8,128)(2,1)} %own_products.1.part_ref), custom_call_target="tpu_custom_call", output_to_operand_aliasing={{}: (4, {})} | custom-call | tf_op jit(solution)/shard_map/guest_products/pallas_call | solution.py:614
  24.8 9.0 %all-to-all-start = ((bf16[64,2,16,512]{3,2,1,0:T(8,128)(2,1)}), bf16[64,2,16,512]{3,2,1,0:T(8,128)(2,1)S(1)}, u32[]{:S(2)}, u32[]{:S(2)}) async-start(bf16[64,2,16,512]{3,2,1,0:T(8,128)(2,1)} %guest_products.1), calls=%async_computation | async-start | bytes 4194304 | tf_op jit(solution)/shard_map/all_to_all | solution.py:630
  33.8 0.0 copy-start.1
  33.8 3.0 %later.1 = (bf16[2,128,1024]{2,1,0:T(8,128)(2,1)}, bf16[2,128,1024]{2,1,0:T(8,128)(2,1)}) custom-call(s32[6]{0:T(128)} %get-tuple-element.21.slot_ref, bf16[6,3,128,1024]{3,2,1,0:T(8,128)(2,1)} %bitcast.8), custom_call_target="tpu_custom_call" | custom-call | bytes 6000000 | tf_op jit(solution)/shard_map/later/pallas_call | solution.py:572
  36.9 12.5 %tables.1.table_ref = s32[16,128]{1,0:T(8,128)S(1)} custom-call(s32[128]{0:T(128)S(1)} %copy-done.1), custom_call_target="tpu_custom_call" | custom-call | bytes 20000000 | tf_op jit(solution)/shard_map/tables/pallas_call | solution.py:588
  49.4 13.4 %all-to-all-done.got_ref = bf16[64,2,16,512]{3,2,1,0:T(8,128)(2,1)S(1)} async-done(((bf16[64,2,16,512]{3,2,1,0:T(8,128)(2,1)}), bf16[64,2,16,512]{3,2,1,0:T(8,128)(2,1)S(1)}, u32[]{:S(2)}, u32[]{:S(2)}) %all-to-all-start) | async-done | bytes 2097184 | tf_op jit(solution)/shard_map/all_to_all | solution.py:630
  62.8 0.6 collective-permute-start.2
  63.4 0.0 collective-permute-start.3
  63.4 16.3 %long_filter.1 = bf16[64,2,16,640]{3,2,1,0:T(8,128)(2,1)S(1)} custom-call(s32[1]{0:T(128)} %bitcast.me_ref, s32[16,128]{1,0:T(8,128)S(1)} %tables.1.table_ref, bf16[64,2,16,512]{3,2,1,0:T(8,128)(2,1)S(1)} %all-to-all-done.got_ref, f32[1,2560]{1,0:T(1,128)S(1)} %pad_convert_fusion.taps_ref), custom_call_target="tpu_custom_call" | custom-call | flops 8053063680 | bytes 7000000 | tf_op jit(solution)/shard_map/long_filter/pallas_call | solution.py:637
  79.7 0.0 collective-permute-done.3.high_kv_ref
  79.8 44.4 %all_to_all.10.got_ref.part_ref = bf16[64,2,16,640]{3,2,1,0:T(8,128)(2,1)} all-to-all(bf16[64,2,16,640]{3,2,1,0:T(8,128)(2,1)S(1)} %long_filter.1), channel_id=1, replica_groups=mesh['ctx'=64,'ch'=2] {'ctx'}, dimensions={0} | all-to-all | bytes 5242880 | tf_op jit(solution)/shard_map/all_to_all | solution.py:670
  124.2 1.7 %totals.1 = (f32[4,2176]{1,0:T(4,128)}, f32[8,128]{1,0:T(8,128)}) custom-call(bf16[64,2,16,640]{3,2,1,0:T(8,128)(2,1)} %all_to_all.10.got_ref.part_ref), custom_call_target="tpu_custom_call" | custom-call | tf_op jit(solution)/shard_map/totals/pallas_call | solution.py:674
  125.9 2.6 %collective-permute-start.4 = (f32[4,2176]{1,0:T(4,128)}, f32[4,2176]{1,0:T(4,128)S(1)}, u32[]{:S(2)}, u32[]{:S(2)}) collective-permute-start(f32[4,2176]{1,0:T(4,128)} %get-tuple-element.34), channel_id=1, source_target_pairs={{0,1},{1,0},{2,3},{3,2},{4,5},{5,4},{6,7},{7,6},{8,9},{9,8},{10,11... | collective-permute-start | bytes 104456 | tf_op jit(solution)/shard_map/ppermute | solution.py:694
  128.5 5.8 %finish.1 = (bf16[512,1024]{1,0:T(8,128)(2,1)}, bf16[3,512,1024]{2,1,0:T(8,128)(2,1)}) custom-call(s32[4]{0:T(128)} %get-tuple-element.20.code_ref, s32[6]{0:T(128)} %get-tuple-element.21.slot_ref, f32[1,1024]{1,0:T(1,128)} %bitcast.10, bf16[6,3,128,1024]{3,2,1,0:T(8,128)(2,1)} %bitcast.9, bf16[2,128,1024]{2,1,0:T(8,128)(2,1)} %copy-done.2, ...), custom_call_target="tpu_custom_call" | custom-call | tf_op jit(solution)/shard_map/finish/pallas_call | solution.py:696
  134.3 0.0 collective-permute-done.4
  134.4 0.6 slice_add_fusion
  (14 shorter events, 0.1 us)
Async XLA Ops:
  0.6 48.7 %copy-start = (f32[4,2049]{1,0:T(4,128)S(1)}, f32[4,2049]{1,0:T(4,128)}, u32[]{:S(2)}) copy-start(f32[4,2049]{1,0:T(4,128)} %param.9) | copy-start | bytes 98356
  3.9 14.8 %collective-permute-start = (bf16[2,128,1024]{2,1,0:T(8,128)(2,1)}, bf16[2,128,1024]{2,1,0:T(8,128)(2,1)S(1)}, u32[]{:S(2)}, u32[]{:S(2)}) collective-permute-start(bf16[2,128,1024]{2,1,0:T(8,128)(2,1)} %get-tuple-element.22), channel_id=1, source_target_pairs={{0,2},{2,4},{4,6},{6,8},{8,10},{10,12},{12,14},{14,16},{16,18},{18... | collective-permute-start | bytes 1572872 | tf_op jit(solution)/shard_map/ppermute | solution.py:541
  6.6 14.4 %collective-permute-start.1 = (bf16[2,128,1024]{2,1,0:T(8,128)(2,1)}, bf16[2,128,1024]{2,1,0:T(8,128)(2,1)S(1)}, u32[]{:S(2)}, u32[]{:S(2)}) collective-permute-start(bf16[2,128,1024]{2,1,0:T(8,128)(2,1)} %get-tuple-element.23), channel_id=1, source_target_pairs={{0,126},{2,0},{4,2},{6,4},{8,6},{10,8},{12,10},{14,12},{16,14},{18... | collective-permute-start | bytes 1572872 | tf_op jit(solution)/shard_map/ppermute | solution.py:541
  18.7 2.4 %copy-start.2 = (bf16[2,128,1024]{2,1,0:T(8,128)(2,1)}, bf16[2,128,1024]{2,1,0:T(8,128)(2,1)S(1)}, u32[]{:S(2)}) copy-start(bf16[2,128,1024]{2,1,0:T(8,128)(2,1)S(1)} %collective-permute-done.low_ref) | copy-start | bytes 1572868
  21.1 0.8 copy-start.3
  24.8 38.0 %all-to-all-start = ((bf16[64,2,16,512]{3,2,1,0:T(8,128)(2,1)}), bf16[64,2,16,512]{3,2,1,0:T(8,128)(2,1)S(1)}, u32[]{:S(2)}, u32[]{:S(2)}) async-start(bf16[64,2,16,512]{3,2,1,0:T(8,128)(2,1)} %guest_products.1), calls=%async_computation | async-start | bytes 4194304 | tf_op jit(solution)/shard_map/all_to_all | solution.py:630
  33.8 3.0 %copy-start.1 = (s32[128]{0:T(128)S(1)}, s32[128]{0:T(128)}, u32[]{:S(2)}) copy-start(s32[128]{0:T(128)} %length_ref.1) | copy-start | bytes 1540
  62.8 16.9 %collective-permute-start.2 = (bf16[2,128,1024]{2,1,0:T(8,128)(2,1)}, bf16[2,128,1024]{2,1,0:T(8,128)(2,1)S(1)}, u32[]{:S(2)}, u32[]{:S(2)}) collective-permute-start(bf16[2,128,1024]{2,1,0:T(8,128)(2,1)} %get-tuple-element.26), channel_id=1, source_target_pairs={{0,2},{2,4},{4,6},{6,8},{8,10},{10,12},{12,14},{14,16},{16,18},{18... | collective-permute-start | bytes 1572872 | tf_op jit(solution)/shard_map/ppermute | solution.py:541
  63.4 16.3 %collective-permute-start.3 = (bf16[2,128,1024]{2,1,0:T(8,128)(2,1)}, bf16[2,128,1024]{2,1,0:T(8,128)(2,1)S(1)}, u32[]{:S(2)}, u32[]{:S(2)}) collective-permute-start(bf16[2,128,1024]{2,1,0:T(8,128)(2,1)} %get-tuple-element.27), channel_id=1, source_target_pairs={{0,126},{2,0},{4,2},{6,4},{8,6},{10,8},{12,10},{14,12},{16,14},{18... | collective-permute-start | bytes 1572872 | tf_op jit(solution)/shard_map/ppermute | solution.py:541
  79.7 44.5 %copy-start.4 = (bf16[2,128,1024]{2,1,0:T(8,128)(2,1)}, bf16[2,128,1024]{2,1,0:T(8,128)(2,1)S(1)}, u32[]{:S(2)}) copy-start(bf16[2,128,1024]{2,1,0:T(8,128)(2,1)S(1)} %collective-permute-done.2.low_kv_ref) | copy-start | bytes 1572868
  79.7 44.4 %copy-start.5 = (bf16[2,128,1024]{2,1,0:T(8,128)(2,1)}, bf16[2,128,1024]{2,1,0:T(8,128)(2,1)S(1)}, u32[]{:S(2)}) copy-start(bf16[2,128,1024]{2,1,0:T(8,128)(2,1)S(1)} %collective-permute-done.3.high_kv_ref) | copy-start | bytes 1572868
  125.9 8.4 %collective-permute-start.4 = (f32[4,2176]{1,0:T(4,128)}, f32[4,2176]{1,0:T(4,128)S(1)}, u32[]{:S(2)}, u32[]{:S(2)}) collective-permute-start(f32[4,2176]{1,0:T(4,128)} %get-tuple-element.34), channel_id=1, source_target_pairs={{0,1},{1,0},{2,3},{3,2},{4,5},{5,4},{6,7},{7,6},{8,9},{9,8},{10,11... | collective-permute-start | bytes 104456 | tf_op jit(solution)/shard_map/ppermute | solution.py:694
  128.5 5.8 %copy-start.6 = (f32[4,2176]{1,0:T(4,128)S(1)}, f32[4,2176]{1,0:T(4,128)}, u32[]{:S(2)}) copy-start(f32[4,2176]{1,0:T(4,128)} %get-tuple-element.34) | copy-start | bytes 104452

commit v5 on v4

--- a/solution.py
+++ b/solution.py
@@ -292,8 +292,6 @@
     make_bands(taps_ref, fwd_ref, bwd_ref)
     x_tail[0:pad, :] = jnp.zeros((pad, BLK), BF16)
     z_head[rows : rows + pad, :] = jnp.zeros((pad, BLK), BF16)
-    back_far[...] = jnp.zeros_like(back_far)
-    far_sum[...] = jnp.zeros_like(far_sum)
     pairs[...] = jnp.zeros_like(pairs)
 
     def spread(k, total):
@@ -342,7 +340,7 @@
 
     lax.fori_loop(0, docs, spread_docs, 0, unroll=4)
 
-    step = 256
+    step = 512
     first_fwd = fwd_ref.at[far : far + BLK, :]
     first_bwd = bwd_ref.at[0:BLK, :]
 
@@ -388,6 +386,15 @@
     def outer(c, carry):
         here = pl.ds(pl.multiple_of(c * wide, wide), wide)
         reach_back, reach_ahead = table_ref[7, c * GROUP], table_ref[11, c * GROUP]
+
+        @pl.when(reach_back == 0)
+        def _():
+            far_sum[here, :] = jnp.zeros((wide, BLK), F32)
+
+        @pl.when(reach_ahead == 0)
+        def _():
+            back_far[here, :] = jnp.zeros((wide, BLK), F32)
+
         for reach in range(1, HOPS + 1):
 
             @pl.when(reach_back == reach)

time: 136 us -> 134 us (0.985)
  transfers between devices with their start and end apart: 6 -> 6, of which waited for: 3 -> 3; matrix products, arithmetic and copies ran while one was open for 0% -> 0% of each run, Pallas kernels for 31% -> 30%
where the time goes in v5:
time: 134 us
  Pallas kernels  48.8 us (36%)
  blocking collectives  44.4 us (33%)
  waiting for transfers between devices  23.6 us (18%)
  starting transfers between devices  14.9 us (11%)
    all_to_all x1, blocking collectives, on_device(): back = lax.all_to_all(reply, 'ctx', 0, 0, tiled=True)  44.4 us
    pallas_call x1, Pallas kernels, on_device(): pl.pallas_call(long_kernel, out_shape=jax.ShapeDtypeStruct((peers, 2, ch,...  15.4 us
    all_to_all x1, waiting for transfers between devices, on_device(): got = lax.all_to_all(sent, 'ctx', 0, 0, tiled=True)  13.4 us
    pallas_call x1, Pallas kernels, on_device(): pl.pallas_call(functools.partial(tables_kernel, docs), out_shape=jax.Shap...  12.5 us
    ppermute x4, waiting for transfers between devices, shifted(): lax.ppermute(array, axis, [(i, (i + by) % length) for i in range(length)])  10.2 us
    all_to_all x1, starting transfers between devices, on_device(): got = lax.all_to_all(sent, 'ctx', 0, 0, tiled=True)  8.97 us
    pallas_call x1, Pallas kernels, on_device(): pl.pallas_call(finish_kernel, out_shape=(jax.ShapeDtypeStruct((tokens, ch...  5.78 us
    pallas_call x1, Pallas kernels, on_device(): pl.pallas_call(own_kernel, out_shape=sent_shape, in_specs=[smem(), smem()...  4.19 us
  transfers between devices with their start and end apart: 6, of which 3 were waited for; matrix products, arithmetic and copies ran while one was open for 0% of the time, Pallas kernels for 30%

profile of v5, /device:TPU:1, one launch (start us, length us, event | category | flops | bytes accessed | tf_op | source)
XLA Modules:
  0.0 134.1 jit_solution(18267092535751422279)
XLA Ops:
  0.6 0.0 copy-start
  0.7 3.2 %choose.1 = (bf16[2,128,1024]{2,1,0:T(8,128)(2,1)}, bf16[2,128,1024]{2,1,0:T(8,128)(2,1)}, s32[4]{0:T(128)}, s32[6]{0:T(128)}) custom-call(s32[1]{0:T(128)} %bitcast.me_ref, s32[2,384]{1,0:T(2,128)} %bitcast.11, bf16[6,3,128,1024]{3,2,1,0:T(8,128)(2,1)} %bitcast.6), custom_call_target="tpu_custom_call" | custom-call | tf_op jit(solution)/shard_map/choose/pallas_call | solution.py:562
  3.9 2.8 %collective-permute-start = (bf16[2,128,1024]{2,1,0:T(8,128)(2,1)}, bf16[2,128,1024]{2,1,0:T(8,128)(2,1)S(1)}, u32[]{:S(2)}, u32[]{:S(2)}) collective-permute-start(bf16[2,128,1024]{2,1,0:T(8,128)(2,1)} %get-tuple-element.22), channel_id=1, source_target_pairs={{0,2},{2,4},{4,6},{6,8},{8,10},{10,12},{12,14},{14,16},{16,18},{18... | collective-permute-start | bytes 1572872 | tf_op jit(solution)/shard_map/ppermute | solution.py:548
  6.6 0.0 collective-permute-start.1
  6.6 4.2 %own_products.1.part_ref = bf16[64,2,16,512]{3,2,1,0:T(8,128)(2,1)} custom-call(s32[4]{0:T(128)} %get-tuple-element.20.code_ref, s32[6]{0:T(128)} %get-tuple-element.21.slot_ref, bf16[6,3,128,1024]{3,2,1,0:T(8,128)(2,1)} %bitcast.7, bf16[512,1024]{1,0:T(8,128)(2,1)} %grad_ref.5), custom_call_target="tpu_custom_call" | custom-call | bytes 20000000 | tf_op jit(solution)/shard_map/own_products/pallas_call | solution.py:611
  10.8 7.9 %collective-permute-done.low_ref = bf16[2,128,1024]{2,1,0:T(8,128)(2,1)S(1)} collective-permute-done((bf16[2,128,1024]{2,1,0:T(8,128)(2,1)}, bf16[2,128,1024]{2,1,0:T(8,128)(2,1)S(1)}, u32[]{:S(2)}, u32[]{:S(2)}) %collective-permute-start) | collective-permute-done | bytes 524320 | tf_op jit(solution)/shard_map/ppermute | solution.py:548
  18.7 2.4 %collective-permute-done.1.high_ref = bf16[2,128,1024]{2,1,0:T(8,128)(2,1)S(1)} collective-permute-done((bf16[2,128,1024]{2,1,0:T(8,128)(2,1)}, bf16[2,128,1024]{2,1,0:T(8,128)(2,1)S(1)}, u32[]{:S(2)}, u32[]{:S(2)}) %collective-permute-start.1) | collective-permute-done | bytes 524320 | tf_op jit(solution)/shard_map/ppermute | solution.py:548
  21.1 0.8 copy-done.3
  21.9 3.0 %guest_products.1 = bf16[64,2,16,512]{3,2,1,0:T(8,128)(2,1)} custom-call(s32[4]{0:T(128)} %get-tuple-element.20.code_ref, bf16[2,128,1024]{2,1,0:T(8,128)(2,1)} %copy-done.2, bf16[2,128,1024]{2,1,0:T(8,128)(2,1)} %copy-done.3, bf16[512,1024]{1,0:T(8,128)(2,1)} %grad_ref.5, bf16[64,2,16,512]{3,2,1,0:T(8,128)(2,1)} %own_products.1.part_ref), custom_call_target="tpu_custom_call", output_to_operand_aliasing={{}: (4, {})} | custom-call | tf_op jit(solution)/shard_map/guest_products/pallas_call | solution.py:621
  24.8 9.0 %all-to-all-start = ((bf16[64,2,16,512]{3,2,1,0:T(8,128)(2,1)}), bf16[64,2,16,512]{3,2,1,0:T(8,128)(2,1)S(1)}, u32[]{:S(2)}, u32[]{:S(2)}) async-start(bf16[64,2,16,512]{3,2,1,0:T(8,128)(2,1)} %guest_products.1), calls=%async_computation | async-start | bytes 4194304 | tf_op jit(solution)/shard_map/all_to_all | solution.py:637
  33.8 0.0 copy-start.1
  33.8 3.0 %later.1 = (bf16[2,128,1024]{2,1,0:T(8,128)(2,1)}, bf16[2,128,1024]{2,1,0:T(8,128)(2,1)}) custom-call(s32[6]{0:T(128)} %get-tuple-element.21.slot_ref, bf16[6,3,128,1024]{3,2,1,0:T(8,128)(2,1)} %bitcast.8), custom_call_target="tpu_custom_call" | custom-call | bytes 6000000 | tf_op jit(solution)/shard_map/later/pallas_call | solution.py:579
  36.9 12.5 %tables.1.table_ref = s32[16,128]{1,0:T(8,128)S(1)} custom-call(s32[128]{0:T(128)S(1)} %copy-done.1), custom_call_target="tpu_custom_call" | custom-call | bytes 20000000 | tf_op jit(solution)/shard_map/tables/pallas_call | solution.py:595
  49.4 13.4 %all-to-all-done.got_ref = bf16[64,2,16,512]{3,2,1,0:T(8,128)(2,1)S(1)} async-done(((bf16[64,2,16,512]{3,2,1,0:T(8,128)(2,1)}), bf16[64,2,16,512]{3,2,1,0:T(8,128)(2,1)S(1)}, u32[]{:S(2)}, u32[]{:S(2)}) %all-to-all-start) | async-done | bytes 2097184 | tf_op jit(solution)/shard_map/all_to_all | solution.py:637
  62.8 0.6 collective-permute-start.2
  63.4 0.0 collective-permute-start.3
  63.4 15.4 %long_filter.1 = bf16[64,2,16,640]{3,2,1,0:T(8,128)(2,1)S(1)} custom-call(s32[1]{0:T(128)} %bitcast.me_ref, s32[16,128]{1,0:T(8,128)S(1)} %tables.1.table_ref, bf16[64,2,16,512]{3,2,1,0:T(8,128)(2,1)S(1)} %all-to-all-done.got_ref, f32[1,2560]{1,0:T(1,128)S(1)} %pad_convert_fusion.taps_ref), custom_call_target="tpu_custom_call" | custom-call | flops 8053063680 | bytes 7000000 | tf_op jit(solution)/shard_map/long_filter/pallas_call | solution.py:644
  78.8 0.0 collective-permute-done.3.high_kv_ref
  78.8 44.4 %all_to_all.10.got_ref.part_ref = bf16[64,2,16,640]{3,2,1,0:T(8,128)(2,1)} all-to-all(bf16[64,2,16,640]{3,2,1,0:T(8,128)(2,1)S(1)} %long_filter.1), channel_id=1, replica_groups=mesh['ctx'=64,'ch'=2] {'ctx'}, dimensions={0} | all-to-all | bytes 5242880 | tf_op jit(solution)/shard_map/all_to_all | solution.py:677
  123.3 1.7 %totals.1 = (f32[4,2176]{1,0:T(4,128)}, f32[8,128]{1,0:T(8,128)}) custom-call(bf16[64,2,16,640]{3,2,1,0:T(8,128)(2,1)} %all_to_all.10.got_ref.part_ref), custom_call_target="tpu_custom_call" | custom-call | tf_op jit(solution)/shard_map/totals/pallas_call | solution.py:681
  125.0 2.6 %collective-permute-start.4 = (f32[4,2176]{1,0:T(4,128)}, f32[4,2176]{1,0:T(4,128)S(1)}, u32[]{:S(2)}, u32[]{:S(2)}) collective-permute-start(f32[4,2176]{1,0:T(4,128)} %get-tuple-element.34), channel_id=1, source_target_pairs={{0,1},{1,0},{2,3},{3,2},{4,5},{5,4},{6,7},{7,6},{8,9},{9,8},{10,11... | collective-permute-start | bytes 104456 | tf_op jit(solution)/shard_map/ppermute | solution.py:701
  127.6 5.8 %finish.1 = (bf16[512,1024]{1,0:T(8,128)(2,1)}, bf16[3,512,1024]{2,1,0:T(8,128)(2,1)}) custom-call(s32[4]{0:T(128)} %get-tuple-element.20.code_ref, s32[6]{0:T(128)} %get-tuple-element.21.slot_ref, f32[1,1024]{1,0:T(1,128)} %bitcast.10, bf16[6,3,128,1024]{3,2,1,0:T(8,128)(2,1)} %bitcast.9, bf16[2,128,1024]{2,1,0:T(8,128)(2,1)} %copy-done.2, ...), custom_call_target="tpu_custom_call" | custom-call | tf_op jit(solution)/shard_map/finish/pallas_call | solution.py:703
  133.4 0.0 collective-permute-done.4
  133.4 0.6 slice_add_fusion
  (14 shorter events, 0.1 us)
Async XLA Ops:
  0.6 48.8 %copy-start = (f32[4,2049]{1,0:T(4,128)S(1)}, f32[4,2049]{1,0:T(4,128)}, u32[]{:S(2)}) copy-start(f32[4,2049]{1,0:T(4,128)} %param.9) | copy-start | bytes 98356
  3.9 14.8 %collective-permute-start = (bf16[2,128,1024]{2,1,0:T(8,128)(2,1)}, bf16[2,128,1024]{2,1,0:T(8,128)(2,1)S(1)}, u32[]{:S(2)}, u32[]{:S(2)}) collective-permute-start(bf16[2,128,1024]{2,1,0:T(8,128)(2,1)} %get-tuple-element.22), channel_id=1, source_target_pairs={{0,2},{2,4},{4,6},{6,8},{8,10},{10,12},{12,14},{14,16},{16,18},{18... | collective-permute-start | bytes 1572872 | tf_op jit(solution)/shard_map/ppermute | solution.py:548
  6.6 14.4 %collective-permute-start.1 = (bf16[2,128,1024]{2,1,0:T(8,128)(2,1)}, bf16[2,128,1024]{2,1,0:T(8,128)(2,1)S(1)}, u32[]{:S(2)}, u32[]{:S(2)}) collective-permute-start(bf16[2,128,1024]{2,1,0:T(8,128)(2,1)} %get-tuple-element.23), channel_id=1, source_target_pairs={{0,126},{2,0},{4,2},{6,4},{8,6},{10,8},{12,10},{14,12},{16,14},{18... | collective-permute-start | bytes 1572872 | tf_op jit(solution)/shard_map/ppermute | solution.py:548
  18.7 2.4 %copy-start.2 = (bf16[2,128,1024]{2,1,0:T(8,128)(2,1)}, bf16[2,128,1024]{2,1,0:T(8,128)(2,1)S(1)}, u32[]{:S(2)}) copy-start(bf16[2,128,1024]{2,1,0:T(8,128)(2,1)S(1)} %collective-permute-done.low_ref) | copy-start | bytes 1572868
  21.1 0.8 copy-start.3
  24.8 38.0 %all-to-all-start = ((bf16[64,2,16,512]{3,2,1,0:T(8,128)(2,1)}), bf16[64,2,16,512]{3,2,1,0:T(8,128)(2,1)S(1)}, u32[]{:S(2)}, u32[]{:S(2)}) async-start(bf16[64,2,16,512]{3,2,1,0:T(8,128)(2,1)} %guest_products.1), calls=%async_computation | async-start | bytes 4194304 | tf_op jit(solution)/shard_map/all_to_all | solution.py:637
  33.8 3.0 %copy-start.1 = (s32[128]{0:T(128)S(1)}, s32[128]{0:T(128)}, u32[]{:S(2)}) copy-start(s32[128]{0:T(128)} %length_ref.1) | copy-start | bytes 1540
  62.8 16.0 %collective-permute-start.2 = (bf16[2,128,1024]{2,1,0:T(8,128)(2,1)}, bf16[2,128,1024]{2,1,0:T(8,128)(2,1)S(1)}, u32[]{:S(2)}, u32[]{:S(2)}) collective-permute-start(bf16[2,128,1024]{2,1,0:T(8,128)(2,1)} %get-tuple-element.26), channel_id=1, source_target_pairs={{0,2},{2,4},{4,6},{6,8},{8,10},{10,12},{12,14},{14,16},{16,18},{18... | collective-permute-start | bytes 1572872 | tf_op jit(solution)/shard_map/ppermute | solution.py:548
  63.4 15.4 %collective-permute-start.3 = (bf16[2,128,1024]{2,1,0:T(8,128)(2,1)}, bf16[2,128,1024]{2,1,0:T(8,128)(2,1)S(1)}, u32[]{:S(2)}, u32[]{:S(2)}) collective-permute-start(bf16[2,128,1024]{2,1,0:T(8,128)(2,1)} %get-tuple-element.27), channel_id=1, source_target_pairs={{0,126},{2,0},{4,2},{6,4},{8,6},{10,8},{12,10},{14,12},{16,14},{18... | collective-permute-start | bytes 1572872 | tf_op jit(solution)/shard_map/ppermute | solution.py:548
  78.8 44.5 %copy-start.4 = (bf16[2,128,1024]{2,1,0:T(8,128)(2,1)}, bf16[2,128,1024]{2,1,0:T(8,128)(2,1)S(1)}, u32[]{:S(2)}) copy-start(bf16[2,128,1024]{2,1,0:T(8,128)(2,1)S(1)} %collective-permute-done.2.low_kv_ref) | copy-start | bytes 1572868
  78.8 44.4 %copy-start.5 = (bf16[2,128,1024]{2,1,0:T(8,128)(2,1)}, bf16[2,128,1024]{2,1,0:T(8,128)(2,1)S(1)}, u32[]{:S(2)}) copy-start(bf16[2,128,1024]{2,1,0:T(8,128)(2,1)S(1)} %collective-permute-done.3.high_kv_ref) | copy-start | bytes 1572868
  125.0 8.4 %collective-permute-start.4 = (f32[4,2176]{1,0:T(4,128)}, f32[4,2176]{1,0:T(4,128)S(1)}, u32[]{:S(2)}, u32[]{:S(2)}) collective-permute-start(f32[4,2176]{1,0:T(4,128)} %get-tuple-element.34), channel_id=1, source_target_pairs={{0,1},{1,0},{2,3},{3,2},{4,5},{5,4},{6,7},{7,6},{8,9},{9,8},{10,11... | collective-permute-start | bytes 104456 | tf_op jit(solution)/shard_map/ppermute | solution.py:701
  127.6 5.8 %copy-start.6 = (f32[4,2176]{1,0:T(4,128)S(1)}, f32[4,2176]{1,0:T(4,128)}, u32[]{:S(2)}) copy-start(f32[4,2176]{1,0:T(4,128)} %get-tuple-element.34) | copy-start | bytes 104452

commit v6 on v5

--- a/solution.py
+++ b/solution.py
@@ -18,7 +18,7 @@
 SLOTS = 6
 ROWS = 4
 LANES = 128
-WIDE = 256
+WIDE = 128
 GROUP = 32
 TAP_ROWS = 17
 VLIM = 56 * 1024 * 1024

time: 134 us -> 135 us (level)
  transfers between devices with their start and end apart: 6 -> 6, of which waited for: 3 -> 3; matrix products, arithmetic and copies ran while one was open for 0% -> 0% of each run, Pallas kernels for 30% -> 31%
where the time goes in v6:
time: 135 us; the launch traced here: 134 us
  Pallas kernels  48.9 us (36%)
  blocking collectives  44.4 us (33%)
  waiting for transfers between devices  23.5 us (17%)
  starting transfers between devices  14.7 us (11%)
    all_to_all x1, blocking collectives, on_device(): back = lax.all_to_all(reply, 'ctx', 0, 0, tiled=True)  44.4 us
    pallas_call x1, Pallas kernels, on_device(): pl.pallas_call(long_kernel, out_shape=jax.ShapeDtypeStruct((peers, 2, ch,...  15.4 us
    all_to_all x1, waiting for transfers between devices, on_device(): got = lax.all_to_all(sent, 'ctx', 0, 0, tiled=True)  13.4 us
    pallas_call x1, Pallas kernels, on_device(): pl.pallas_call(functools.partial(tables_kernel, docs), out_shape=jax.Shap...  12.5 us
    ppermute x4, waiting for transfers between devices, shifted(): lax.ppermute(array, axis, [(i, (i + by) % length) for i in range(length)])  10.1 us
    all_to_all x1, starting transfers between devices, on_device(): got = lax.all_to_all(sent, 'ctx', 0, 0, tiled=True)  8.74 us
    pallas_call x1, Pallas kernels, on_device(): pl.pallas_call(finish_kernel, out_shape=(jax.ShapeDtypeStruct((tokens, ch...  5.66 us
    pallas_call x1, Pallas kernels, on_device(): pl.pallas_call(own_kernel, out_shape=sent_shape, in_specs=[smem(), smem()...  4.36 us
  transfers between devices with their start and end apart: 6, of which 3 were waited for; matrix products, arithmetic and copies ran while one was open for 0% of the time, Pallas kernels for 31%

profile of v6, /device:TPU:1, one launch (start us, length us, event | category | flops | bytes accessed | tf_op | source)
XLA Modules:
  0.0 133.8 jit_solution(171534947114502927)
XLA Ops:
  0.6 0.0 copy-start
  0.7 3.2 %choose.1 = (bf16[2,128,1024]{2,1,0:T(8,128)(2,1)}, bf16[2,128,1024]{2,1,0:T(8,128)(2,1)}, s32[4]{0:T(128)}, s32[6]{0:T(128)}) custom-call(s32[1]{0:T(128)} %bitcast.me_ref, s32[2,384]{1,0:T(2,128)} %bitcast.11, bf16[6,3,128,1024]{3,2,1,0:T(8,128)(2,1)} %bitcast.6), custom_call_target="tpu_custom_call" | custom-call | tf_op jit(solution)/shard_map/choose/pallas_call | solution.py:562
  3.9 2.8 %collective-permute-start = (bf16[2,128,1024]{2,1,0:T(8,128)(2,1)}, bf16[2,128,1024]{2,1,0:T(8,128)(2,1)S(1)}, u32[]{:S(2)}, u32[]{:S(2)}) collective-permute-start(bf16[2,128,1024]{2,1,0:T(8,128)(2,1)} %get-tuple-element.22), channel_id=1, source_target_pairs={{0,2},{2,4},{4,6},{6,8},{8,10},{10,12},{12,14},{14,16},{16,18},{18... | collective-permute-start | bytes 1572872 | tf_op jit(solution)/shard_map/ppermute | solution.py:548
  6.6 0.0 collective-permute-start.1
  6.6 4.4 %own_products.1.part_ref = bf16[64,2,16,512]{3,2,1,0:T(8,128)(2,1)} custom-call(s32[4]{0:T(128)} %get-tuple-element.20.code_ref, s32[6]{0:T(128)} %get-tuple-element.21.slot_ref, bf16[6,3,128,1024]{3,2,1,0:T(8,128)(2,1)} %bitcast.7, bf16[512,1024]{1,0:T(8,128)(2,1)} %grad_ref.5), custom_call_target="tpu_custom_call" | custom-call | bytes 20000000 | tf_op jit(solution)/shard_map/own_products/pallas_call | solution.py:611
  11.0 7.7 %collective-permute-done.low_ref = bf16[2,128,1024]{2,1,0:T(8,128)(2,1)S(1)} collective-permute-done((bf16[2,128,1024]{2,1,0:T(8,128)(2,1)}, bf16[2,128,1024]{2,1,0:T(8,128)(2,1)S(1)}, u32[]{:S(2)}, u32[]{:S(2)}) %collective-permute-start) | collective-permute-done | bytes 524320 | tf_op jit(solution)/shard_map/ppermute | solution.py:548
  18.7 2.4 %collective-permute-done.1.high_ref = bf16[2,128,1024]{2,1,0:T(8,128)(2,1)S(1)} collective-permute-done((bf16[2,128,1024]{2,1,0:T(8,128)(2,1)}, bf16[2,128,1024]{2,1,0:T(8,128)(2,1)S(1)}, u32[]{:S(2)}, u32[]{:S(2)}) %collective-permute-start.1) | collective-permute-done | bytes 524320 | tf_op jit(solution)/shard_map/ppermute | solution.py:548
  21.1 0.8 copy-done.3
  21.9 3.0 %guest_products.1 = bf16[64,2,16,512]{3,2,1,0:T(8,128)(2,1)} custom-call(s32[4]{0:T(128)} %get-tuple-element.20.code_ref, bf16[2,128,1024]{2,1,0:T(8,128)(2,1)} %copy-done.2, bf16[2,128,1024]{2,1,0:T(8,128)(2,1)} %copy-done.3, bf16[512,1024]{1,0:T(8,128)(2,1)} %grad_ref.5, bf16[64,2,16,512]{3,2,1,0:T(8,128)(2,1)} %own_products.1.part_ref), custom_call_target="tpu_custom_call", output_to_operand_aliasing={{}: (4, {})} | custom-call | tf_op jit(solution)/shard_map/guest_products/pallas_call | solution.py:621
  24.9 8.7 %all-to-all-start = ((bf16[64,2,16,512]{3,2,1,0:T(8,128)(2,1)}), bf16[64,2,16,512]{3,2,1,0:T(8,128)(2,1)S(1)}, u32[]{:S(2)}, u32[]{:S(2)}) async-start(bf16[64,2,16,512]{3,2,1,0:T(8,128)(2,1)} %guest_products.1), calls=%async_computation | async-start | bytes 4194304 | tf_op jit(solution)/shard_map/all_to_all | solution.py:637
  33.7 0.0 copy-start.1
  33.7 3.0 %later.1 = (bf16[2,128,1024]{2,1,0:T(8,128)(2,1)}, bf16[2,128,1024]{2,1,0:T(8,128)(2,1)}) custom-call(s32[6]{0:T(128)} %get-tuple-element.21.slot_ref, bf16[6,3,128,1024]{3,2,1,0:T(8,128)(2,1)} %bitcast.8), custom_call_target="tpu_custom_call" | custom-call | bytes 6000000 | tf_op jit(solution)/shard_map/later/pallas_call | solution.py:579
  36.7 12.5 %tables.1.table_ref = s32[16,128]{1,0:T(8,128)S(1)} custom-call(s32[128]{0:T(128)S(1)} %copy-done.1), custom_call_target="tpu_custom_call" | custom-call | bytes 20000000 | tf_op jit(solution)/shard_map/tables/pallas_call | solution.py:595
  49.3 13.4 %all-to-all-done.got_ref = bf16[64,2,16,512]{3,2,1,0:T(8,128)(2,1)S(1)} async-done(((bf16[64,2,16,512]{3,2,1,0:T(8,128)(2,1)}), bf16[64,2,16,512]{3,2,1,0:T(8,128)(2,1)S(1)}, u32[]{:S(2)}, u32[]{:S(2)}) %all-to-all-start) | async-done | bytes 2097184 | tf_op jit(solution)/shard_map/all_to_all | solution.py:637
  62.7 0.6 collective-permute-start.2
  63.2 0.0 collective-permute-start.3
  63.2 15.4 %long_filter.1 = bf16[64,2,16,640]{3,2,1,0:T(8,128)(2,1)S(1)} custom-call(s32[1]{0:T(128)} %bitcast.me_ref, s32[16,128]{1,0:T(8,128)S(1)} %tables.1.table_ref, bf16[64,2,16,512]{3,2,1,0:T(8,128)(2,1)S(1)} %all-to-all-done.got_ref, f32[1,2560]{1,0:T(1,128)S(1)} %pad_convert_fusion.taps_ref), custom_call_target="tpu_custom_call" | custom-call | flops 8053063680 | bytes 7000000 | tf_op jit(solution)/shard_map/long_filter/pallas_call | solution.py:644
  78.6 0.0 collective-permute-done.2.low_kv_ref
  78.7 0.0 collective-permute-done.3.high_kv_ref
  78.7 44.4 %all_to_all.10.got_ref.part_ref = bf16[64,2,16,640]{3,2,1,0:T(8,128)(2,1)} all-to-all(bf16[64,2,16,640]{3,2,1,0:T(8,128)(2,1)S(1)} %long_filter.1), channel_id=1, replica_groups=mesh['ctx'=64,'ch'=2] {'ctx'}, dimensions={0} | all-to-all | bytes 5242880 | tf_op jit(solution)/shard_map/all_to_all | solution.py:677
  123.1 1.7 %totals.1 = (f32[4,2176]{1,0:T(4,128)}, f32[8,128]{1,0:T(8,128)}) custom-call(bf16[64,2,16,640]{3,2,1,0:T(8,128)(2,1)} %all_to_all.10.got_ref.part_ref), custom_call_target="tpu_custom_call" | custom-call | tf_op jit(solution)/shard_map/totals/pallas_call | solution.py:681
  124.8 2.6 %collective-permute-start.4 = (f32[4,2176]{1,0:T(4,128)}, f32[4,2176]{1,0:T(4,128)S(1)}, u32[]{:S(2)}, u32[]{:S(2)}) collective-permute-start(f32[4,2176]{1,0:T(4,128)} %get-tuple-element.34), channel_id=1, source_target_pairs={{0,1},{1,0},{2,3},{3,2},{4,5},{5,4},{6,7},{7,6},{8,9},{9,8},{10,11... | collective-permute-start | bytes 104456 | tf_op jit(solution)/shard_map/ppermute | solution.py:701
  127.5 5.7 %finish.1 = (bf16[512,1024]{1,0:T(8,128)(2,1)}, bf16[3,512,1024]{2,1,0:T(8,128)(2,1)}) custom-call(s32[4]{0:T(128)} %get-tuple-element.20.code_ref, s32[6]{0:T(128)} %get-tuple-element.21.slot_ref, f32[1,1024]{1,0:T(1,128)} %bitcast.10, bf16[6,3,128,1024]{3,2,1,0:T(8,128)(2,1)} %bitcast.9, bf16[2,128,1024]{2,1,0:T(8,128)(2,1)} %copy-done.2, ...), custom_call_target="tpu_custom_call" | custom-call | tf_op jit(solution)/shard_map/finish/pallas_call | solution.py:703
  133.2 0.6 slice_add_fusion
  (14 shorter events, 0.1 us)
Async XLA Ops:
  0.6 48.6 %copy-start = (f32[4,2049]{1,0:T(4,128)S(1)}, f32[4,2049]{1,0:T(4,128)}, u32[]{:S(2)}) copy-start(f32[4,2049]{1,0:T(4,128)} %param.9) | copy-start | bytes 98356
  3.9 14.8 %collective-permute-start = (bf16[2,128,1024]{2,1,0:T(8,128)(2,1)}, bf16[2,128,1024]{2,1,0:T(8,128)(2,1)S(1)}, u32[]{:S(2)}, u32[]{:S(2)}) collective-permute-start(bf16[2,128,1024]{2,1,0:T(8,128)(2,1)} %get-tuple-element.22), channel_id=1, source_target_pairs={{0,2},{2,4},{4,6},{6,8},{8,10},{10,12},{12,14},{14,16},{16,18},{18... | collective-permute-start | bytes 1572872 | tf_op jit(solution)/shard_map/ppermute | solution.py:548
  6.6 14.4 %collective-permute-start.1 = (bf16[2,128,1024]{2,1,0:T(8,128)(2,1)}, bf16[2,128,1024]{2,1,0:T(8,128)(2,1)S(1)}, u32[]{:S(2)}, u32[]{:S(2)}) collective-permute-start(bf16[2,128,1024]{2,1,0:T(8,128)(2,1)} %get-tuple-element.23), channel_id=1, source_target_pairs={{0,126},{2,0},{4,2},{6,4},{8,6},{10,8},{12,10},{14,12},{16,14},{18... | collective-permute-start | bytes 1572872 | tf_op jit(solution)/shard_map/ppermute | solution.py:548
  18.7 2.4 %copy-start.2 = (bf16[2,128,1024]{2,1,0:T(8,128)(2,1)}, bf16[2,128,1024]{2,1,0:T(8,128)(2,1)S(1)}, u32[]{:S(2)}) copy-start(bf16[2,128,1024]{2,1,0:T(8,128)(2,1)S(1)} %collective-permute-done.low_ref) | copy-start | bytes 1572868
  21.1 0.8 copy-start.3
  24.9 37.8 %all-to-all-start = ((bf16[64,2,16,512]{3,2,1,0:T(8,128)(2,1)}), bf16[64,2,16,512]{3,2,1,0:T(8,128)(2,1)S(1)}, u32[]{:S(2)}, u32[]{:S(2)}) async-start(bf16[64,2,16,512]{3,2,1,0:T(8,128)(2,1)} %guest_products.1), calls=%async_computation | async-start | bytes 4194304 | tf_op jit(solution)/shard_map/all_to_all | solution.py:637
  33.7 3.0 %copy-start.1 = (s32[128]{0:T(128)S(1)}, s32[128]{0:T(128)}, u32[]{:S(2)}) copy-start(s32[128]{0:T(128)} %length_ref.1) | copy-start | bytes 1540
  62.7 16.0 %collective-permute-start.2 = (bf16[2,128,1024]{2,1,0:T(8,128)(2,1)}, bf16[2,128,1024]{2,1,0:T(8,128)(2,1)S(1)}, u32[]{:S(2)}, u32[]{:S(2)}) collective-permute-start(bf16[2,128,1024]{2,1,0:T(8,128)(2,1)} %get-tuple-element.26), channel_id=1, source_target_pairs={{0,2},{2,4},{4,6},{6,8},{8,10},{10,12},{12,14},{14,16},{16,18},{18... | collective-permute-start | bytes 1572872 | tf_op jit(solution)/shard_map/ppermute | solution.py:548
  63.2 15.4 %collective-permute-start.3 = (bf16[2,128,1024]{2,1,0:T(8,128)(2,1)}, bf16[2,128,1024]{2,1,0:T(8,128)(2,1)S(1)}, u32[]{:S(2)}, u32[]{:S(2)}) collective-permute-start(bf16[2,128,1024]{2,1,0:T(8,128)(2,1)} %get-tuple-element.27), channel_id=1, source_target_pairs={{0,126},{2,0},{4,2},{6,4},{8,6},{10,8},{12,10},{14,12},{16,14},{18... | collective-permute-start | bytes 1572872 | tf_op jit(solution)/shard_map/ppermute | solution.py:548
  78.6 44.5 %copy-start.4 = (bf16[2,128,1024]{2,1,0:T(8,128)(2,1)}, bf16[2,128,1024]{2,1,0:T(8,128)(2,1)S(1)}, u32[]{:S(2)}) copy-start(bf16[2,128,1024]{2,1,0:T(8,128)(2,1)S(1)} %collective-permute-done.2.low_kv_ref) | copy-start | bytes 1572868
  78.7 44.4 %copy-start.5 = (bf16[2,128,1024]{2,1,0:T(8,128)(2,1)}, bf16[2,128,1024]{2,1,0:T(8,128)(2,1)S(1)}, u32[]{:S(2)}) copy-start(bf16[2,128,1024]{2,1,0:T(8,128)(2,1)S(1)} %collective-permute-done.3.high_kv_ref) | copy-start | bytes 1572868
  124.8 8.3 %collective-permute-start.4 = (f32[4,2176]{1,0:T(4,128)}, f32[4,2176]{1,0:T(4,128)S(1)}, u32[]{:S(2)}, u32[]{:S(2)}) collective-permute-start(f32[4,2176]{1,0:T(4,128)} %get-tuple-element.34), channel_id=1, source_target_pairs={{0,1},{1,0},{2,3},{3,2},{4,5},{5,4},{6,7},{7,6},{8,9},{9,8},{10,11... | collective-permute-start | bytes 104456 | tf_op jit(solution)/shard_map/ppermute | solution.py:701
  127.5 5.7 %copy-start.6 = (f32[4,2176]{1,0:T(4,128)S(1)}, f32[4,2176]{1,0:T(4,128)}, u32[]{:S(2)}) copy-start(f32[4,2176]{1,0:T(4,128)} %get-tuple-element.34) | copy-start | bytes 104452
